TPU v7x, 32 devices: a whole 2x2x4 slice. The times are simulated.
32 devices in a mesh: dp: 8 (over z, y), fsdp: 4 (over x, core).
Axes of the slice: x: 2, y: 2, z: 4, core: 2. Of those that a mesh axis runs over, the one named last changes fastest.
Arguments:
- inputs: bfloat16 [32768, 768], P(('dp', 'fsdp')), may hold values from -6 to 6
- lengths: int32 [64, 2], P(('dp', 'fsdp')), may hold values from 1 to 507, as said below
- query_matrix: bfloat16 [768, 768], P(('dp', 'fsdp')), may hold values from -0.21875 to 0.21875
- key_weight: bfloat16 [768, 768], P(('dp', 'fsdp')), may hold values from -0.21875 to 0.21875
- value_matrix: bfloat16 [768, 768], P(('dp', 'fsdp')), may hold values from -0.21875 to 0.21875
- output_weight: bfloat16 [768, 768], P(('dp', 'fsdp')), may hold values from -1.25 to 1.25
- inner_weight: bfloat16 [768, 3072], P(('dp', 'fsdp')), may hold values from -0.21875 to 0.21875
- outer_weight: bfloat16 [3072, 768], P(('dp', 'fsdp')), may hold values from -0.109375 to 0.109375
- attn_gain: bfloat16 [768], replicated, may hold values from 0.5 to 1.5
- attn_shift: bfloat16 [768], replicated, may hold values from -1.5 to 1.5
- ffn_gain: bfloat16 [768], replicated, may hold values from 0.5 to 1.5
- ffn_shift: bfloat16 [768], replicated, may hold values from -1.5 to 1.5
- query_down: float32 [768, 8], replicated, may hold values from -0.21875 to 0.21875
- query_raise_weight: float32 [8, 768], replicated, may hold values from -1 to 1
- value_down: float32 [768, 8], replicated, may hold values from -0.21875 to 0.21875
- value_raise_weight: float32 [8, 768], replicated, may hold values from -1 to 1
- grad_output: bfloat16 [32768, 768], P(('dp', 'fsdp')), may hold values from -6 to 6
Outputs:
- outputs: bfloat16 [32768, 768], P(('dp', 'fsdp'))
- grad_inputs: float32 [32768, 768], P(('dp', 'fsdp'))
- grad_query_down: float32 [768, 8], replicated
- grad_query_up: float32 [8, 768], replicated
- grad_value_down: float32 [768, 8], replicated
- grad_value_up: float32 [8, 768], replicated
Inputs may be any that keep to these rules, and one draw needn't show every extreme that they name: lengths[s, 0] and lengths[s, 1] are slot s's premise and hypothesis token counts, each 1 or more, with lengths[s, 0] + lengths[s, 1] + 4 <= 512; in every draw some slot has lengths[s, 0] + lengths[s, 1] + 4 == 512.
All inputs are finite; a program needn't handle non-finite values.
Results may differ from a plain program's by a relative error of at most 0.017.
The roundings to bfloat16 on the way count: a program that leaves them out, or rounds other values in their place, can miss the bound.
Values may be sent and summed in bfloat16 or wider, within the bound.
No kernel may reach another device: no remote copies, remote signals or barrier semaphores. Data moves between devices by JAX's collectives and lax.ppermute only.
A program may use at most 128 MiB of HBM per device.

v0:
```python
import jax
import jax.numpy as jnp
from jax import lax
from jax.sharding import PartitionSpec as P

HEAD_DIM = 64
SLOT_LEN = 512


adapter_scale = 2.0
score_scale = 0.125
norm_eps = 1e-05
masked_score = -1e30


def norm_apply(value, norm_gain, norm_shift):
    row_mean = jnp.mean(value, axis=-1, keepdims=True)
    centred = value - row_mean
    spread = jnp.mean(centred * centred, axis=-1, keepdims=True)
    return centred * lax.rsqrt(spread + norm_eps) * norm_gain + norm_shift


def gelu_exact(value):
    return jax.nn.gelu(value, approximate=False)


def heads_view(matrix, slot_count):
    return matrix.reshape(slot_count, SLOT_LEN, matrix.shape[1] // HEAD_DIM, HEAD_DIM)


def slot_scores(query_rows, key_rows, valid_len):
    scores = (
        jnp.einsum("qhe,khe->hqk", query_rows, key_rows, preferred_element_type=jnp.float32)
        * score_scale
    )
    places = lax.broadcasted_iota(jnp.int32, (1, 1, key_rows.shape[0]), 2) < valid_len
    return jnp.where(places, scores, masked_score)


def slot_forward(slot_item):
    query_rows, key_rows, value_rows, valid_len = slot_item
    scores = slot_scores(query_rows, key_rows, valid_len)
    row_top = jnp.max(scores, axis=-1, keepdims=True)
    shifted = jnp.exp(scores - row_top)
    row_total = jnp.sum(shifted, axis=-1, keepdims=True)
    prob_low = (shifted / row_total).astype(jnp.bfloat16)
    attn_mixed = jnp.einsum(
        "hqk,khe->qhe", prob_low, value_rows, preferred_element_type=jnp.float32
    )
    return (attn_mixed.astype(jnp.bfloat16), (row_top + jnp.log(row_total))[..., 0])


def slot_backward(slot_item):
    query_rows, key_rows, value_rows, valid_len, log_total, grad_mixed = slot_item
    scores = slot_scores(query_rows, key_rows, valid_len)
    prob_full = jnp.exp(scores - log_total[..., None])
    prob_low = prob_full.astype(jnp.bfloat16)
    value_row_gradient = jnp.einsum(
        "hqk,qhe->khe", prob_low, grad_mixed, preferred_element_type=jnp.float32
    )
    grad_probs = jnp.einsum(
        "qhe,khe->hqk", grad_mixed, value_rows, preferred_element_type=jnp.float32
    )
    grad_scores = prob_full * (grad_probs - jnp.sum(prob_full * grad_probs, axis=-1, keepdims=True))
    grad_low = grad_scores.astype(jnp.bfloat16)
    query_row_gradient = (
        jnp.einsum("hqk,khe->qhe", grad_low, key_rows, preferred_element_type=jnp.float32)
        * score_scale
    )
    grad_keys = (
        jnp.einsum("hqk,qhe->khe", grad_low, query_rows, preferred_element_type=jnp.float32)
        * score_scale
    )
    return (
        query_row_gradient.astype(jnp.bfloat16),
        grad_keys.astype(jnp.bfloat16),
        value_row_gradient.astype(jnp.bfloat16),
    )


def attention_weights(query_matrix, key_weight, value_matrix, output_weight):
    return (
        lax.all_gather(query_matrix, ("dp", "fsdp"), axis=0, tiled=True),
        lax.all_gather(key_weight, ("dp", "fsdp"), axis=0, tiled=True),
        lax.all_gather(value_matrix, ("dp", "fsdp"), axis=0, tiled=True),
        lax.all_gather(output_weight, ("dp", "fsdp"), axis=0, tiled=True),
    )


def feed_weights(inner_weight, outer_weight):
    return (
        lax.all_gather(inner_weight, ("dp", "fsdp"), axis=0, tiled=True),
        lax.all_gather(outer_weight, ("dp", "fsdp"), axis=0, tiled=True),
    )


def forward_pass(inputs, valid_len, attention, feed, norms, adapter_factors):
    whole_query, whole_key, whole_value, whole_output = attention
    whole_inner, whole_outer = feed
    down_query, raised_query, down_value, raised_value = adapter_factors
    row_count, model_width = inputs.shape
    slot_count = valid_len.shape[0]
    reduced_query = jnp.dot(inputs, down_query, preferred_element_type=jnp.float32).astype(
        jnp.bfloat16
    )
    reduced_value = jnp.dot(inputs, down_value, preferred_element_type=jnp.float32).astype(
        jnp.bfloat16
    )
    query_rows = (
        jnp.dot(inputs, whole_query, preferred_element_type=jnp.float32)
        + adapter_scale * jnp.dot(reduced_query, raised_query, preferred_element_type=jnp.float32)
    ).astype(jnp.bfloat16)
    key_rows = jnp.dot(inputs, whole_key, preferred_element_type=jnp.float32).astype(jnp.bfloat16)
    value_rows = (
        jnp.dot(inputs, whole_value, preferred_element_type=jnp.float32)
        + adapter_scale * jnp.dot(reduced_value, raised_value, preferred_element_type=jnp.float32)
    ).astype(jnp.bfloat16)
    attn_mixed, log_total = lax.map(
        slot_forward,
        (
            heads_view(query_rows, slot_count),
            heads_view(key_rows, slot_count),
            heads_view(value_rows, slot_count),
            valid_len,
        ),
    )
    attn_mixed = attn_mixed.reshape(row_count, model_width)
    first_sum = inputs.astype(jnp.float32) + jnp.dot(
        attn_mixed, whole_output, preferred_element_type=jnp.float32
    )
    first_norm = norm_apply(first_sum, norms[0], norms[1])
    inner_act = jnp.dot(
        first_norm.astype(jnp.bfloat16), whole_inner, preferred_element_type=jnp.float32
    )
    active = gelu_exact(inner_act).astype(jnp.bfloat16)
    second_sum = first_norm + jnp.dot(active, whole_outer, preferred_element_type=jnp.float32)
    return (
        query_rows,
        key_rows,
        value_rows,
        reduced_query,
        reduced_value,
        log_total,
        first_sum,
        inner_act,
        second_sum,
    )


def shards(
    inputs,
    lengths,
    query_matrix,
    key_weight,
    value_matrix,
    output_weight,
    inner_weight,
    outer_weight,
    attn_gain,
    attn_shift,
    ffn_gain,
    ffn_shift,
    query_down,
    query_raise_weight,
    value_down,
    value_raise_weight,
    grad_output,
):
    valid_len = lengths[:, 0] + lengths[:, 1] + 4
    row_count, model_width = inputs.shape
    slot_count = valid_len.shape[0]
    norms = (
        attn_gain.astype(jnp.float32),
        attn_shift.astype(jnp.float32),
        ffn_gain.astype(jnp.float32),
        ffn_shift.astype(jnp.float32),
    )
    adapter_factors = (
        query_down.astype(jnp.bfloat16),
        query_raise_weight.astype(jnp.bfloat16),
        value_down.astype(jnp.bfloat16),
        value_raise_weight.astype(jnp.bfloat16),
    )
    attention = attention_weights(query_matrix, key_weight, value_matrix, output_weight)
    feed = feed_weights(inner_weight, outer_weight)
    forward_state = forward_pass(inputs, valid_len, attention, feed, norms, adapter_factors)
    outputs = norm_apply(forward_state[8], norms[2], norms[3]).astype(jnp.bfloat16)
    tied = lax.optimization_barrier(
        (query_matrix, key_weight, value_matrix, output_weight, inner_weight, outer_weight, outputs)
    )
    back_attention = attention_weights(tied[0], tied[1], tied[2], tied[3])
    back_feed = feed_weights(tied[4], tied[5])
    back_state = forward_pass(inputs, valid_len, back_attention, back_feed, norms, adapter_factors)
    whole_query, whole_key, whole_value, whole_output = back_attention
    whole_inner, whole_outer = back_feed
    (
        query_rows,
        key_rows,
        value_rows,
        reduced_query,
        reduced_value,
        log_total,
        first_sum,
        inner_act,
        second_sum,
    ) = back_state

    def second_norm(value):
        return norm_apply(value, norms[2], norms[3])

    def first_normer(value):
        return norm_apply(value, norms[0], norms[1])

    unused_second, second_pull = jax.vjp(second_norm, second_sum)
    grad_second = second_pull(grad_output.astype(jnp.float32))[0]
    grad_active = jnp.dot(
        grad_second.astype(jnp.bfloat16), whole_outer.T, preferred_element_type=jnp.float32
    )
    unused_gelu, gelu_pull = jax.vjp(gelu_exact, inner_act)
    grad_inner = gelu_pull(grad_active)[0].astype(jnp.bfloat16)
    grad_first = grad_second + jnp.dot(
        grad_inner, whole_inner.T, preferred_element_type=jnp.float32
    )
    unused_first, first_pull = jax.vjp(first_normer, first_sum)
    grad_first_sum = first_pull(grad_first)[0]
    grad_mixed = jnp.dot(
        grad_first_sum.astype(jnp.bfloat16), whole_output.T, preferred_element_type=jnp.float32
    ).astype(jnp.bfloat16)
    query_row_gradient, grad_keys, value_row_gradient = lax.map(
        slot_backward,
        (
            heads_view(query_rows, slot_count),
            heads_view(key_rows, slot_count),
            heads_view(value_rows, slot_count),
            valid_len,
            log_total,
            heads_view(grad_mixed, slot_count),
        ),
    )
    query_row_gradient = query_row_gradient.reshape(row_count, model_width)
    grad_keys = grad_keys.reshape(row_count, model_width)
    value_row_gradient = value_row_gradient.reshape(row_count, model_width)
    grad_low_query = (
        adapter_scale
        * jnp.dot(query_row_gradient, adapter_factors[1].T, preferred_element_type=jnp.float32)
    ).astype(jnp.bfloat16)
    grad_low_value = (
        adapter_scale
        * jnp.dot(value_row_gradient, adapter_factors[3].T, preferred_element_type=jnp.float32)
    ).astype(jnp.bfloat16)
    grad_inputs = grad_first_sum + jnp.dot(
        query_row_gradient, whole_query.T, preferred_element_type=jnp.float32
    )
    grad_inputs = grad_inputs + jnp.dot(grad_keys, whole_key.T, preferred_element_type=jnp.float32)
    grad_inputs = grad_inputs + jnp.dot(
        value_row_gradient, whole_value.T, preferred_element_type=jnp.float32
    )
    grad_inputs = grad_inputs + jnp.dot(
        grad_low_query, adapter_factors[0].T, preferred_element_type=jnp.float32
    )
    grad_inputs = grad_inputs + jnp.dot(
        grad_low_value, adapter_factors[2].T, preferred_element_type=jnp.float32
    )
    term_query_down = jnp.dot(inputs.T, grad_low_query, preferred_element_type=jnp.float32)
    query_raise_term = adapter_scale * jnp.dot(
        reduced_query.T, query_row_gradient, preferred_element_type=jnp.float32
    )
    term_value_down = jnp.dot(inputs.T, grad_low_value, preferred_element_type=jnp.float32)
    value_raise_term = adapter_scale * jnp.dot(
        reduced_value.T, value_row_gradient, preferred_element_type=jnp.float32
    )
    summed = lax.psum(
        (term_query_down, query_raise_term, term_value_down, value_raise_term), ("dp", "fsdp")
    )
    slot_total = slot_count * lax.axis_size("dp") * lax.axis_size("fsdp")
    return (
        outputs,
        grad_inputs,
        summed[0] / slot_total,
        summed[1] / slot_total,
        summed[2] / slot_total,
        summed[3] / slot_total,
    )


def solution(mesh):
    return jax.shard_map(
        shards,
        mesh=mesh,
        in_specs=(
            P(("dp", "fsdp"), None),
            P(("dp", "fsdp"), None),
            P(("dp", "fsdp"), None),
            P(("dp", "fsdp"), None),
            P(("dp", "fsdp"), None),
            P(("dp", "fsdp"), None),
            P(("dp", "fsdp"), None),
            P(("dp", "fsdp"), None),
            P(),
            P(),
            P(),
            P(),
            P(),
            P(),
            P(),
            P(),
            P(("dp", "fsdp"), None),
        ),
        out_specs=(P(("dp", "fsdp"), None), P(("dp", "fsdp"), None), P(), P(), P(), P()),
        check_vma=False,
    )
```

profile of v0, /device:TPU:0, one launch (start us, length us, event | category | flops | bytes accessed | tf_op | source)
XLA Modules:
  0.0 994.1 jit_solution(2027714974978963168)
XLA Ops:
  21.0 46.7 %all-gather.13.cloned.1.call-done = bf16[768,768]{1,0:T(8,128)(2,1)} async-done(((bf16[24,768]{1,0:T(8,128)(2,1)}), bf16[768,768]{1,0:T(8,128)(2,1)}) %all-gather.13.cloned.1.call-update) | async-done | bytes 1179664 | tf_op jit(solution)/shard_map/all_gather | solution.py:85
  67.7 4.8 add_convert_fusion.4
  79.5 44.1 %all-gather.15.cloned.1.call-done = bf16[768,768]{1,0:T(8,128)(2,1)} async-done(((bf16[24,768]{1,0:T(8,128)(2,1)}), bf16[768,768]{1,0:T(8,128)(2,1)}) %all-gather.15.cloned.1.call-update) | async-done | bytes 1179664 | tf_op jit(solution)/shard_map/all_gather | solution.py:83
  135.4 44.1 %all-gather.17.cloned.1.call-done = bf16[768,768]{1,0:T(8,128)(2,1)} async-done(((bf16[24,768]{1,0:T(8,128)(2,1)}), bf16[768,768]{1,0:T(8,128)(2,1)}) %all-gather.17.cloned.1.call-update) | async-done | bytes 1179664 | tf_op jit(solution)/shard_map/all_gather | solution.py:84
  185.8 36.2 %while.36 = (s32[]{:T(128)}, bf16[2,512,12,64]{1,3,2,0:T(8,128)(2,1)S(1)}, bf16[2,512,12,64]{1,3,2,0:T(8,128)(2,1)}, s32[2]{0:T(128)S(1)}, bf16[2,512,12,64]{1,3...) while((s32[]{:T(128)}, bf16[2,512,12,64]{1,3,2,0:T(8,128)(2,1)S(1)}, ...), condition=%wide.region_3.4_spmd, body=%wide.region_0.3_spmd.sunk | while | flops 824574976 | bytes 34663544 | solution.py:118
  187.2 11.0 %fusion.295 = (f32[12,512]{1,0:T(8,128)S(1)}, f32[12,512,512]{1,2,0:T(8,128)}) fusion(pred[512]{0:T(512)(128)(4,1)S(1)} %iota_compare_fusion.6, bf16[2,512,12,64]{1,3,2,0:T(8,128)(2,1)} %get-tuple-element.456, s32[]{:T(128)} %get-tuple-element.444, bf16[2,512,12,64]{1,3,2,0:T(8,128)(2,1)} %get-tuple-element.455), kind=kOutput, calls=%fused_computation.253.clone.1 | convolution fusion | flops 415236608 | bytes 14181888 | tf_op jit(solution)/shard_map/while/body/eval_jaxpr/sub | solution.py:44
  198.2 5.8 fusion.296
  205.2 11.0 %fusion.295 = (f32[12,512]{1,0:T(8,128)S(1)}, f32[12,512,512]{1,2,0:T(8,128)}) fusion(pred[512]{0:T(512)(128)(4,1)S(1)} %iota_compare_fusion.6, bf16[2,512,12,64]{1,3,2,0:T(8,128)(2,1)} %get-tuple-element.456, s32[]{:T(128)} %get-tuple-element.444, bf16[2,512,12,64]{1,3,2,0:T(8,128)(2,1)} %get-tuple-element.455), kind=kOutput, calls=%fused_computation.253.clone.1 | convolution fusion | flops 415236608 | bytes 14181888 | tf_op jit(solution)/shard_map/while/body/eval_jaxpr/sub | solution.py:44
  216.2 5.8 fusion.296
  225.2 10.1 %all-gather.19.cloned.1.call-done = bf16[768,768]{1,0:T(8,128)(2,1)} async-done(((bf16[24,768]{1,0:T(8,128)(2,1)}), bf16[768,768]{1,0:T(8,128)(2,1)}) %all-gather.19.cloned.1.call-update) | async-done | bytes 1179664 | tf_op jit(solution)/shard_map/all_gather | solution.py:86
  239.4 61.2 %all-gather.21.cloned.1.call-done = bf16[768,3072]{1,0:T(8,128)(2,1)} async-done(((bf16[24,3072]{1,0:T(8,128)(2,1)}), bf16[768,3072]{1,0:T(8,128)(2,1)}) %all-gather.21.cloned.1.call-update) | async-done | bytes 4718608 | tf_op jit(solution)/shard_map/all_gather | solution.py:92
  300.6 35.7 %fusion.124.clone.4 = bf16[1024,3072]{1,0:T(8,128)(2,1)} fusion(bf16[768,3072]{1,0:T(8,128)(2,1)} %all-gather.21.cloned.1.call-done, f32[1024,768]{0,1:T(8,128)S(1)} %get-tuple-element.269, f32[768]{0:T(1024)S(1)} %convert_element_type.146, f32[768]{0:T(1024)S(1)} %convert_element_type.145, ...), kind=kOutput, calls=%fused_computation.96.clone.clone.clone.clone.clone.clone.1 | convolution fusion | flops 5040242688 | bytes 14170112 | tf_op jit(solution)/shard_map/dot_general | solution.py:132
  336.3 29.5 %all-gather.23.cloned.1.call-done = bf16[3072,768]{1,0:T(8,128)(2,1)} async-done(((bf16[96,768]{1,0:T(8,128)(2,1)}), bf16[3072,768]{1,0:T(8,128)(2,1)}) %all-gather.23.cloned.1.call-update) | async-done | bytes 4718608 | tf_op jit(solution)/shard_map/all_gather | solution.py:93
  365.8 8.9 fusion.202
  383.2 45.8 %all-gather.25.cloned.1.call-done = bf16[768,768]{1,0:T(8,128)(2,1)} async-done(((bf16[24,768]{1,0:T(8,128)(2,1)}), bf16[768,768]{1,0:T(8,128)(2,1)}) %all-gather.25.cloned.1.call-update) | async-done | bytes 1179664 | tf_op jit(solution)/shard_map/all_gather | solution.py:85
  428.9 4.8 fusion.118
  440.8 44.1 %all-gather.27.cloned.1.call-done = bf16[768,768]{1,0:T(8,128)(2,1)} async-done(((bf16[24,768]{1,0:T(8,128)(2,1)}), bf16[768,768]{1,0:T(8,128)(2,1)}) %all-gather.27.cloned.1.call-update) | async-done | bytes 1179664 | tf_op jit(solution)/shard_map/all_gather | solution.py:83
  484.8 4.8 fusion.117
  495.4 45.3 %all-gather.29.cloned.1.call-done = bf16[768,768]{1,0:T(8,128)(2,1)} async-done(((bf16[24,768]{1,0:T(8,128)(2,1)}), bf16[768,768]{1,0:T(8,128)(2,1)}) %all-gather.29.cloned.1.call-update) | async-done | bytes 1179664 | tf_op jit(solution)/shard_map/all_gather | solution.py:84
  551.5 22.9 %while.37 = (s32[]{:T(128)}, bf16[2,512,12,64]{1,3,2,0:T(8,128)(2,1)}, f32[2,12,512]{2,1,0:T(8,128)S(1)}, bf16[2,512,12,64]{1,3,2,0:T(8,128)(2,1)}, s32[2]{0:T(1...) while((s32[]{:T(128)}, ...), condition=%wide.region_11.12_spmd, body=%wide.region_8.11_spmd.sunk | while | flops 843442688 | bytes 47427716 | solution.py:118
  579.0 17.5 %all-gather.31.cloned.1.call-done = bf16[768,768]{1,0:T(8,128)(2,1)} async-done(((bf16[24,768]{1,0:T(8,128)(2,1)}), bf16[768,768]{1,0:T(8,128)(2,1)}) %all-gather.31.cloned.1.call-update) | async-done | bytes 1179664 | tf_op jit(solution)/shard_map/all_gather | solution.py:86
  602.3 59.7 %all-gather.33.cloned.1.call-done = bf16[768,3072]{1,0:T(8,128)(2,1)} async-done(((bf16[24,3072]{1,0:T(8,128)(2,1)}), bf16[768,3072]{1,0:T(8,128)(2,1)}) %all-gather.33.cloned.1.call-update) | async-done | bytes 4718608 | tf_op jit(solution)/shard_map/all_gather | solution.py:92
  662.0 35.8 %fusion.99 = (f32[1024,3072]{1,0:T(8,128)}, f32[1024,3072]{1,0:T(8,128)}) fusion(bf16[768,3072]{1,0:T(8,128)(2,1)} %all-gather.33.cloned.1.call-done, f32[1024,768]{0,1:T(8,128)} %copy-done.10, f32[1024]{0:T(1024)S(1)} %fusion.155, f32[1024]{0:T(1024)S(1)} %broadcast_multiply_fusion.5, f32[768]{0:T(1024)S(1)} %convert_element_type.146, ...), kind=kOutput, calls=%fused_computation.97 | convolution fusion | flops 5030805504 | bytes 33044480 | tf_op jit(solution)/shard_map/dot_general | solution.py:132
  697.8 29.5 %all-gather.35.cloned.1.call-done = bf16[3072,768]{1,0:T(8,128)(2,1)} async-done(((bf16[96,768]{1,0:T(8,128)(2,1)}), bf16[3072,768]{1,0:T(8,128)(2,1)}) %all-gather.35.cloned.1.call-update) | async-done | bytes 4718608 | tf_op jit(solution)/shard_map/all_gather | solution.py:93
  727.3 17.4 %fusion.204 = (f32[1024]{0:T(1024)S(1)}, f32[1024,768]{0,1:T(8,128)}) fusion(bf16[3072,768]{1,0:T(8,128)(2,1)} %all-gather.35.cloned.1.call-done, f32[1024,3072]{1,0:T(8,128)} %get-tuple-element.274, f32[1024,3072]{1,0:T(8,128)} %get-tuple-element.275, f32[768]{0:T(1024)S(1)} %convert_element_type.146, f32[768]{0:T(1024)S(1)} %convert_element_type.145, ...), kind=kOutput, calls=%fused_computation.257 | convolution fusion | flops 4845992960 | bytes 36194304 | tf_op jit(solution)/shard_map/dot_general | solution.py:136
  749.3 22.8 %multiply_reduce_fusion.1 = (f32[1024]{0:T(1024)S(1)}, f32[1024,768]{0,1:T(8,128)}) fusion(f32[1024,768]{0,1:T(8,128)} %copy-done.10, f32[1024]{0:T(1024)S(1)} %broadcast_multiply_fusion.5, f32[768]{0:T(1024)S(1)} %convert_element_type.145, bf16[768,3072]{1,0:T(8,128)(2,1)} %all-gather.33.cloned.1.call-done, f32[1024,3072]{1,0:T(8,128)} %get-tuple-element.274, ...), kind=kOutput, calls=%fused_computation.141 | convolution fusion | flops 9725017088 | bytes 45643776 | tf_op jit(solution)/shard_map/dot_general | solution.py:221
  793.8 52.1 %while.38 = (s32[]{:T(128)}, bf16[2,512,12,64]{1,3,2,0:T(8,128)(2,1)}, bf16[2,512,12,64]{1,3,2,0:T(8,128)(2,1)}, bf16[2,512,12,64]{1,3,2,0:T(8,128)(2,1)}, bf16[...) while((s32[]{:T(128)}, ...), condition=%wide.region_22.23_spmd, body=%wide.region_20.22_spmd.sunk | while | flops 2062412288 | bytes 140180784 | solution.py:229
  797.1 7.3 multiply_reduce_fusion.8
  804.5 7.2 multiply_convert_fusion.8
  823.0 7.3 multiply_reduce_fusion.8
  830.3 7.2 multiply_convert_fusion.8
  873.9 110.5 %all-reduce.3.cloned.1.call-done = (f32[768,8]{0,1:T(8,128)}, f32[8,768]{1,0:T(8,128)}, f32[768,8]{0,1:T(8,128)}, f32[8,768]{1,0:T(8,128)}) async-done(((f32[768,8]{0,1:T(8,128)}, f32[8,768]{1,0:T(8,128)}, f32[768,8]{0,1:T(8,128)}, f32[8,768]{1,0:T(8,128)}), (f32[768,8]{0,1:T(8,128)}, f32[8,768]{1,0:T(8,128)}, f32[768,8]{0,1:T(8,128)}, f32[8,768]{1,0:T(8,128)})) %all-reduce.3.cloned.1.call-update) | async-done | bytes 98320 | tf_op jit(solution)/shard_map/psum | solution.py:272
  (250 shorter events, 191.9 us)
Async XLA Ops:
  7.2 6.7 copy-start
  7.2 6.7 copy-start.29
  7.2 7.2 copy-start.27
  7.2 60.5 %all-gather.13.cloned.1.call-start = ((), (), s32[]{:S(2)}) async-start(), calls=%async_computation | async-start | bytes 1216512 | tf_op jit(solution)/shard_map/all_gather | solution.py:85
  7.9 115.7 %all-gather.15.cloned.1.call-start = ((), (), s32[]{:S(2)}) async-start(), calls=%async_computation.1 | async-start | bytes 1216512 | tf_op jit(solution)/shard_map/all_gather | solution.py:83
  8.7 170.8 %all-gather.17.cloned.1.call-start = ((), (), s32[]{:S(2)}) async-start(), calls=%async_computation.2 | async-start | bytes 1216512 | tf_op jit(solution)/shard_map/all_gather | solution.py:84
  9.4 225.9 %all-gather.19.cloned.1.call-start = ((), (), s32[]{:S(2)}) async-start(), calls=%async_computation.3 | async-start | bytes 1216512 | tf_op jit(solution)/shard_map/all_gather | solution.py:86
  10.0 290.6 %all-gather.21.cloned.1.call-start = ((), (), s32[]{:S(2)}) async-start(), calls=%async_computation.4 | async-start | bytes 4866048 | tf_op jit(solution)/shard_map/all_gather | solution.py:92
  10.6 355.3 %all-gather.23.cloned.1.call-start = ((), (), s32[]{:S(2)}) async-start(), calls=%async_computation.5 | async-start | bytes 4866048 | tf_op jit(solution)/shard_map/all_gather | solution.py:93
  11.2 3.9 copy-start.38
  11.2 3.9 copy-start.39
  11.2 4.5 copy-start.40
  11.2 5.1 copy-start.23
  11.2 417.7 %all-gather.25.cloned.1.call-start = ((), (), s32[]{:S(2)}) async-start(), calls=%async_computation.6 | async-start | bytes 1216512 | tf_op jit(solution)/shard_map/all_gather | solution.py:85
  13.9 4.8 copy-start.25
  14.4 6.6 copy-start.21
  14.9 6.1 copy-start.19
  187.2 11.0 %copy-start.17 = (bf16[2,512,12,64]{1,3,2,0:T(8,128)(2,1)S(1)}, bf16[2,512,12,64]{1,3,2,0:T(8,128)(2,1)}, u32[]{:S(2)}) copy-start(bf16[2,512,12,64]{1,3,2,0:T(8,128)(2,1)} %get-tuple-element.453) | copy-start | bytes 4718596 | tf_op jit(solution)/shard_map/while
  205.2 11.0 %copy-start.17 = (bf16[2,512,12,64]{1,3,2,0:T(8,128)(2,1)S(1)}, bf16[2,512,12,64]{1,3,2,0:T(8,128)(2,1)}, u32[]{:S(2)}) copy-start(bf16[2,512,12,64]{1,3,2,0:T(8,128)(2,1)} %get-tuple-element.453) | copy-start | bytes 4718596 | tf_op jit(solution)/shard_map/while
  375.9 108.9 %all-gather.27.cloned.1.call-start = ((), (), s32[]{:S(2)}) async-start(), calls=%async_computation.7 | async-start | bytes 1216512 | tf_op jit(solution)/shard_map/all_gather | solution.py:83
  376.7 164.1 %all-gather.29.cloned.1.call-start = ((), (), s32[]{:S(2)}) async-start(), calls=%async_computation.8 | async-start | bytes 1216512 | tf_op jit(solution)/shard_map/all_gather | solution.py:84
  377.4 219.1 %all-gather.31.cloned.1.call-start = ((), (), s32[]{:S(2)}) async-start(), calls=%async_computation.9 | async-start | bytes 1216512 | tf_op jit(solution)/shard_map/all_gather | solution.py:86
  378.0 284.0 %all-gather.33.cloned.1.call-start = ((), (), s32[]{:S(2)}) async-start(), calls=%async_computation.10 | async-start | bytes 4866048 | tf_op jit(solution)/shard_map/all_gather | solution.py:92
  378.8 348.5 %all-gather.35.cloned.1.call-start = ((), (), s32[]{:S(2)}) async-start(), calls=%async_computation.11 | async-start | bytes 4866048 | tf_op jit(solution)/shard_map/all_gather | solution.py:93
  378.8 50.1 %copy-start.1 = (bf16[1024,768]{1,0:T(8,128)(2,1)S(1)}, bf16[1024,768]{1,0:T(8,128)(2,1)}, u32[]{:S(2)}) copy-start(bf16[1024,768]{1,0:T(8,128)(2,1)} %param.23) | copy-start | bytes 4718596
  383.1 601.3 %all-reduce.3.cloned.1.call-start = ((), (), s32[]{:S(2)}) async-start(), calls=%async_computation.12 | async-start | bytes 196608 | tf_op jit(solution)/shard_map/psum | solution.py:272
  574.4 4.6 copy-start.41
  727.3 17.4 %copy-start.32 = (f32[768]{0:T(1024)S(1)}, f32[768]{0:T(1024)}, u32[]{:S(2)}) copy-start(f32[768]{0:T(1024)} %convert_element_type.149) | copy-start | bytes 9220
  772.2 5.7 copy-start.45
  789.8 4.0 copy-start.42
  804.5 7.2 copy-start.15
  830.3 7.2 copy-start.15
  (35 other events, 77.2 us)
Sparse Core Ops, SparseCore 0:
  10.9 56.7 all-gather.12
  70.6 52.9 all-gather.14
  126.5 52.9 all-gather.16
  182.3 52.9 all-gather.18
  238.0 62.5 all-gather.20
  303.4 62.4 all-gather.22
  376.1 52.8 all-gather.24
  431.8 52.9 all-gather.26
  487.7 52.9 all-gather.28
  543.5 52.9 all-gather.30
  599.4 62.5 all-gather.32
  664.8 62.4 all-gather.34
  863.3 121.0 all-reduce.2
where the time goes:
time: 1000 us; the launch traced here: 994 us
  waiting for transfers between devices  594 us (59%)
  matrix products  256 us (26%)
  local copies, waits for them, and re-layouts  89.4 us (9%)
  other arithmetic  37.5 us (4%)
  between operations  15 us (2%)
    all_gather x2, waiting for transfers between devices, feed_weights(): lax.all_gather(inner_weight, ('dp', 'fsdp'), axis=0, tiled=True)  121 us
    psum x1, waiting for transfers between devices, shards(): lax.psum((term_query_down, query_raise_term, term_value_down, value_raise...  110 us
    all_gather x2, waiting for transfers between devices, attention_weights(): lax.all_gather(value_matrix, ('dp', 'fsdp'), axis=0, tiled=True)  92.5 us
    all_gather x2, waiting for transfers between devices, attention_weights(): lax.all_gather(key_weight, ('dp', 'fsdp'), axis=0, tiled=True)  89.4 us
    all_gather x2, waiting for transfers between devices, attention_weights(): lax.all_gather(query_matrix, ('dp', 'fsdp'), axis=0, tiled=True)  88.2 us
    dot_general x2, matrix products, forward_pass(): jnp.dot(first_norm.astype(jnp.bfloat16), whole_inner, preferred_element_t...  71.5 us
    all_gather x2, waiting for transfers between devices, feed_weights(): lax.all_gather(outer_weight, ('dp', 'fsdp'), axis=0, tiled=True)  59 us
    all_gather x2, waiting for transfers between devices, attention_weights(): lax.all_gather(output_weight, ('dp', 'fsdp'), axis=0, tiled=True)  27.6 us
  transfers between devices with their start and end apart: 13, of which 13 were waited for; matrix products, arithmetic and copies ran while one was open for 23% of the time, Pallas kernels for 0%

commit v1 on v0

v1 whole, which is shorter than its diff:
```python
import functools
import jax
import jax.numpy as jnp
from jax import lax
from jax.experimental import pallas as pl
from jax.experimental.pallas import tpu as pltpu
from jax.sharding import PartitionSpec as P

HEAD_DIM=64; SLOT=512
F32=jnp.float32; BF=jnp.bfloat16
VM=58*1024*1024

def dg(a,b,ca,cb):
    return lax.dot_general(a,b,(((ca,),(cb,)),((),())),preferred_element_type=F32)

def attend_kernel(valid_ref, x_ref, wq_ref, wk_ref, wv_ref, dn_ref, upq_ref, upv_ref,
                  q_ref, k_ref, v_ref, e_ref, ot_ref, o_ref, rt_ref, low_ref, lowv):
    s=pl.program_id(0); j=pl.program_id(1)
    x=x_ref[...]
    @pl.when(j==0)
    def _():
        low=dg(x,dn_ref[...],1,0).astype(BF)
        lowv[...]=low
        low_ref[0]=low.T[:32]
    low=lowv[...]
    q=(dg(x,wq_ref[...],1,0)+2.0*dg(low,upq_ref[...],1,0)).astype(BF)
    k=dg(x,wk_ref[...],1,0).astype(BF)
    v=(dg(x,wv_ref[...],1,0)+2.0*dg(low,upv_ref[...],1,0)).astype(BF)
    q_ref[...]=q; k_ref[...]=k; v_ref[...]=v
    valid=valid_ref[s]
    lane=lax.broadcasted_iota(jnp.int32,(SLOT,128),1)
    row=lax.broadcasted_iota(jnp.int32,(SLOT,128),0)
    bias=jnp.where(row<valid,0.0,-1e30).astype(F32)
    totals=[]
    for p in range(2):
        qp=q[:,128*p:128*p+128].astype(F32)*0.125
        kp=k[:,128*p:128*p+128].astype(F32)
        vp=v[:,128*p:128*p+128].astype(F32)
        for h in range(2):
            own=(lane<64) if h==0 else (lane>=64)
            aux=64 if h==0 else 0
            one=jnp.where(lane==aux,1.0,0.0)
            qm=jnp.where(own,qp,one).astype(BF)
            km=jnp.where(own,kp,jnp.where(lane==aux,bias,0.0)).astype(BF)
            vm=jnp.where(own,vp,one).astype(BF)
            st=dg(km,qm,1,1)
            top=jnp.max(st,axis=0,keepdims=True)
            e=jnp.exp(st-top).astype(BF)
            e_ref[0,2*p+h]=e
            ot=dg(vm,e,0,0)
            total=ot[aux:aux+1]
            r=1.0/total
            totals.append(r)
            lo=64*h
            ob=(ot[lo:lo+64]*r).astype(BF)
            ot_ref[0,128*p+lo:128*p+lo+64]=ob
    o_ref[...]=ot_ref[0].T
    rt_ref[0,0]=jnp.concatenate(totals+totals,axis=0)

def attend(valid,x,wq,wk,wv,dn,upq,upv):
    rows,D=x.shape; S=rows//SLOT; J=D//256; H=D//HEAD_DIM
    gs=pltpu.PrefetchScalarGridSpec(num_scalar_prefetch=1,grid=(S,J),
        in_specs=[pl.BlockSpec((SLOT,D),lambda s,j,_:(s,0)),
                  *[pl.BlockSpec((D,256),lambda s,j,_:(0,j))]*3,
                  pl.BlockSpec((D,128),lambda s,j,_:(0,0)),
                  *[pl.BlockSpec((128,256),lambda s,j,_:(0,j))]*2],
        out_specs=[*[pl.BlockSpec((SLOT,256),lambda s,j,_:(s,j))]*3,
                   pl.BlockSpec((1,4,SLOT,SLOT),lambda s,j,_:(s,j,0,0)),
                   pl.BlockSpec((1,256,SLOT),lambda s,j,_:(s,j,0)),
                   pl.BlockSpec((SLOT,256),lambda s,j,_:(s,j)),
                   pl.BlockSpec((1,1,8,SLOT),lambda s,j,_:(s,j,0,0)),
                   pl.BlockSpec((1,32,SLOT),lambda s,j,_:(s,0,0))],
        scratch_shapes=[pltpu.VMEM((SLOT,128),BF)])
    sd=jax.ShapeDtypeStruct
    return pl.pallas_call(attend_kernel,grid_spec=gs,
        out_shape=[*[sd((rows,D),BF)]*3, sd((S,H,SLOT,SLOT),BF), sd((S,D,SLOT),BF), sd((rows,D),BF),
                   sd((S,J,8,SLOT),F32), sd((S,32,SLOT),BF)],
        compiler_params=pltpu.CompilerParams(vmem_limit_bytes=VM),name="attend")(valid,x,wq,wk,wv,dn,upq,upv)

def norm_stats(value):
    mean=jnp.mean(value,axis=-1,keepdims=True)
    c=value-mean
    r=lax.rsqrt(jnp.mean(c*c,axis=-1,keepdims=True)+1e-5)
    return c*r,r

def norm_back(g,n,r):
    return r*(g-jnp.mean(g,axis=-1,keepdims=True)-n*jnp.mean(g*n,axis=-1,keepdims=True))

def gelu_pair(v):
    a=jnp.abs(v)
    t=1.0/(1.0+(0.3275911*0.7071067811865476)*a)
    ex=jnp.exp(-0.5*v*v)
    poly=t*(0.127414796+t*(-0.142248368+t*(0.7107068705+t*(-0.7265760135+t*0.5307027145))))
    half=poly*ex
    cdf=jnp.where(v>=0,1.0-half,half)
    return v*cdf, cdf+v*(ex*0.3989422804014327)

CH=512
def feed_kernel(x_ref,o_ref,go_ref,wo_ref,wi_ref,wt_ref,nm_ref,out_ref,gfs_ref,gmt_ref,gp_ref):
    ag,ash,fg,fsh=(nm_ref[i:i+1,:] for i in range(4))
    first=x_ref[...].astype(F32)+dg(o_ref[...],wo_ref[...],1,0)
    n1,r1=norm_stats(first)
    h=n1*ag+ash
    hb=h.astype(BF)
    acc=h
    nc=wi_ref.shape[1]//CH
    for c in range(nc):
        z=dg(hb,wi_ref[:,c*CH:(c+1)*CH],1,0)
        act,gp=gelu_pair(z)
        gp_ref[:,c*CH:(c+1)*CH]=gp
        acc=acc+dg(act.astype(BF),wt_ref[c*CH:(c+1)*CH,:],1,0)
    n2,r2=norm_stats(acc)
    out_ref[...]=(n2*fg+fsh).astype(BF)
    g2=norm_back(go_ref[...].astype(F32)*fg,n2,r2)
    g2b=g2.astype(BF)
    acc=g2
    for c in range(nc):
        ga=dg(g2b,wt_ref[c*CH:(c+1)*CH,:],1,1)
        gi=(ga*gp_ref[:,c*CH:(c+1)*CH]).astype(BF)
        acc=acc+dg(gi,wi_ref[:,c*CH:(c+1)*CH],1,1)
    g1=norm_back(acc*ag,n1,r1)
    gfs_ref[...]=g1
    gmt_ref[...]=dg(wo_ref[...],g1.astype(BF),1,1).astype(BF)

def feed(x,o,go,wo,wi,wt,nm,T=256):
    rows,D=x.shape; FF=wi.shape[1]
    sd=jax.ShapeDtypeStruct
    row=pl.BlockSpec((T,D),lambda i:(i,0))
    one=lambda shape: pl.BlockSpec(shape,lambda i:(0,0),pipeline_mode=pl.Buffered(1))
    return pl.pallas_call(feed_kernel,grid=(rows//T,),
        in_specs=[row,row,row,one((D,D)),one((D,FF)),one((FF,D)),one((8,D))],
        out_specs=[row,row,pl.BlockSpec((D,T),lambda i:(0,i))],
        out_shape=[sd((rows,D),BF),sd((rows,D),F32),sd((D,rows),BF)],
        scratch_shapes=[pltpu.VMEM((T,FF),F32)],
        compiler_params=pltpu.CompilerParams(vmem_limit_bytes=VM),name="feed")(x,o,go,wo,wi,wt,nm)

def attend_back_kernel(q_ref,k_ref,v_ref,e_ref,ot_ref,rt_ref,gmt_ref,x_ref,low_ref,upq_ref,upv_ref,
                       dq_ref,dk_ref,dv_ref,gl_ref,ad_ref,glacc):
    s=pl.program_id(0); j=pl.program_id(1); J=pl.num_programs(1)
    lane=lax.broadcasted_iota(jnp.int32,(SLOT,128),1)
    rowi=lax.broadcasted_iota(jnp.int32,(128,SLOT),0)
    dqts=[]
    for p in range(2):
        cols=slice(128*p,128*p+128)
        qp=q_ref[:,cols].astype(F32)*0.125; kp=k_ref[:,cols].astype(F32)*0.125; vp=v_ref[:,cols].astype(F32)
        gm=gmt_ref[cols,:].astype(F32); om=ot_ref[0,cols,:].astype(F32)
        pr=gm*om
        dkp=None; dvp=None; dqt=None
        for h in range(2):
            own=(lane<64) if h==0 else (lane>=64)
            ownr=(rowi<64) if h==0 else (rowi>=64)
            aux=64 if h==0 else 0
            r=rt_ref[0,0,2*p+h:2*p+h+1,:]
            d=-jnp.sum(pr[64*h:64*h+64],axis=0,keepdims=True)*r
            dhi=d.astype(BF).astype(F32)
            dlo=d-dhi
            gs=gm*r
            gaug=jnp.where(ownr,gs,jnp.where(rowi==aux,dhi,jnp.where(rowi==aux+1,dlo,0.0))).astype(BF)
            gown=jnp.where(ownr,gs,0.0).astype(BF)
            vm=jnp.where(own,vp,jnp.where((lane==aux)|(lane==aux+1),1.0,0.0)).astype(BF)
            e=e_ref[0,2*p+h]
            ds=(dg(vm,gaug,1,0)*e.astype(F32)).astype(BF)
            qm=jnp.where(own,qp,0.0).astype(BF)
            km=jnp.where(own,kp,0.0).astype(BF)
            dv=dg(e,gown,1,1)
            dk=dg(ds,qm,1,0)
            dq=dg(km,ds,0,0)
            dvp=dv if dvp is None else dvp+dv
            dkp=dk if dkp is None else dkp+dk
            dqt=dq if dqt is None else dqt+dq
        dk_ref[:,cols]=dkp.astype(BF)
        dv_ref[:,cols]=dvp.astype(BF)
        dqts.append(dqt.astype(BF))
    dqt=jnp.concatenate(dqts,axis=0)
    dqb=dqt.T
    dq_ref[...]=dqb
    dvb=dv_ref[...]
    glq=dg(upq_ref[...],dqt,1,0)
    glv=dg(upv_ref[...],dvb,1,1)
    part=2.0*(glq+glv)
    @pl.when(j==0)
    def _(): glacc[...]=part
    @pl.when(j>0)
    def _(): glacc[...]+=part
    low=low_ref[0]
    c0=pl.multiple_of(j*256,256)
    upq=2.0*dg(low[:16],dqb,1,0)
    upv=2.0*dg(low[:16],dvb,1,0)
    upg=jnp.concatenate([upq[0:8],upv[8:16]],axis=0)
    @pl.when(s==0)
    def _(): ad_ref[16:32,pl.ds(c0,256)]=upg
    @pl.when(s>0)
    def _(): ad_ref[16:32,pl.ds(c0,256)]+=upg
    @pl.when(j==J-1)
    def _():
        gl=glacc[...].astype(BF)
        gl_ref[0]=gl
        dn=dg(gl,x_ref[...],1,0)
        @pl.when(s==0)
        def _(): ad_ref[0:16,:]=dn
        @pl.when(s>0)
        def _(): ad_ref[0:16,:]+=dn

def attend_back(q,k,v,e,ot,rt,gmt,x,low,upq,upv):
    rows,D=x.shape; S=rows//SLOT; J=D//256
    sd=jax.ShapeDtypeStruct
    blk=pl.BlockSpec((SLOT,256),lambda s,j:(s,j))
    return pl.pallas_call(attend_back_kernel,grid=(S,J),
        in_specs=[blk,blk,blk,pl.BlockSpec((1,4,SLOT,SLOT),lambda s,j:(s,j,0,0)),
                  pl.BlockSpec((1,256,SLOT),lambda s,j:(s,j,0)),
                  pl.BlockSpec((1,1,8,SLOT),lambda s,j:(s,j,0,0)),
                  pl.BlockSpec((256,SLOT),lambda s,j:(j,s)),
                  pl.BlockSpec((SLOT,D),lambda s,j:(s,0)),
                  pl.BlockSpec((1,32,SLOT),lambda s,j:(s,0,0)),
                  pl.BlockSpec((16,256),lambda s,j:(0,j)),pl.BlockSpec((16,256),lambda s,j:(0,j))],
        out_specs=[blk,blk,blk,pl.BlockSpec((1,16,SLOT),lambda s,j:(s,0,0)),pl.BlockSpec((32,D),lambda s,j:(0,0))],
        out_shape=[sd((rows,D),BF)]*3+[sd((S,16,SLOT),BF),sd((32,D),F32)],
        scratch_shapes=[pltpu.VMEM((16,SLOT),F32)],
        compiler_params=pltpu.CompilerParams(vmem_limit_bytes=VM),name="attend_back")(q,k,v,e,ot,rt,gmt,x,low,upq,upv)

def inputs_kernel(gfs_ref,dq_ref,dk_ref,dv_ref,gl_ref,wq_ref,wk_ref,wv_ref,dnt_ref,out_ref):
    out_ref[...]=(gfs_ref[...]+dg(dq_ref[...],wq_ref[...],1,1)+dg(dk_ref[...],wk_ref[...],1,1)
        +dg(dv_ref[...],wv_ref[...],1,1)+dg(gl_ref[0],dnt_ref[...],0,0))

def inputs_grad(gfs,dq,dk,dv,gl,wq,wk,wv,dnt):
    rows,D=gfs.shape
    T=SLOT
    row=pl.BlockSpec((T,D),lambda i:(i,0))
    one=lambda shape: pl.BlockSpec(shape,lambda i:(0,0),pipeline_mode=pl.Buffered(1))
    return pl.pallas_call(inputs_kernel,grid=(rows//T,),
        in_specs=[row,row,row,row,pl.BlockSpec((1,16,T),lambda i:(i,0,0)),one((D,D)),one((D,D)),one((D,D)),one((16,D))],
        out_specs=row,out_shape=jax.ShapeDtypeStruct((rows,D),F32),
        compiler_params=pltpu.CompilerParams(vmem_limit_bytes=VM),name="inputs_grad")(gfs,dq,dk,dv,gl,wq,wk,wv,dnt)

def layer(x,valid,wq,wk,wv,wo,wi,wt,ag,ash,fg,fsh,qd,qu,vd,vu,go):
    D=x.shape[1]
    dn16=jnp.concatenate([qd,vd],1).astype(BF)
    dn=jnp.pad(dn16,((0,0),(0,112)))
    qub=qu.astype(BF); vub=vu.astype(BF)
    z8=jnp.zeros_like(qub)
    upq16=jnp.concatenate([qub,z8],0); upv16=jnp.concatenate([z8,vub],0)
    upq=jnp.pad(upq16,((0,112),(0,0))); upv=jnp.pad(upv16,((0,112),(0,0)))
    nm=jnp.pad(jnp.stack([ag,ash,fg,fsh]).astype(F32),((0,4),(0,0)))
    q,k,v,e,ot,o,rt,low=attend(valid,x,wq,wk,wv,dn,upq,upv)
    out,gfs,gmt=feed(x,o,go,wo,wi,wt,nm)
    dq,dk,dv,gl,ad=attend_back(q,k,v,e,ot,rt,gmt,x,low,upq16,upv16)
    gx=inputs_grad(gfs,dq,dk,dv,gl,wq,wk,wv,dn16.T)
    return out,gx,ad


AXES=("dp","fsdp")

def gather_all(pieces):
    width=pieces[0].shape[1]
    packed=jnp.concatenate([p.reshape(-1,width) for p in pieces],0)
    n=lax.axis_size("dp")*lax.axis_size("fsdp")
    got=lax.all_gather(packed,AXES,axis=0,tiled=True).reshape(n,packed.shape[0],width)
    out=[];at=0
    for p in pieces:
        r=p.size//width
        out.append(got[:,at:at+r].reshape(n*p.shape[0],p.shape[1])); at+=r
    return out

def shards(x,lengths,wq,wk,wv,wo,wi,wt,ag,ash,fg,fsh,qd,qu,vd,vu,go):
    valid=lengths[:,0]+lengths[:,1]+4
    wq,wk,wv,wo,wi,wt=gather_all((wq,wk,wv,wo,wi,wt))
    out,gx,ad=layer(x,valid,wq,wk,wv,wo,wi,wt,ag,ash,fg,fsh,qd,qu,vd,vu,go)
    slots=lengths.shape[0]*lax.axis_size("dp")*lax.axis_size("fsdp")
    ad=lax.psum(ad,AXES)/slots
    return out,gx,ad[0:8].T,ad[16:24],ad[8:16].T,ad[24:32]

def solution(mesh):
    sp=P(AXES,None)
    return jax.shard_map(shards,mesh=mesh,in_specs=(sp,)*8+(P(),)*8+(sp,),
        out_specs=(sp,sp,P(),P(),P(),P()),check_vma=False)
```

time: 1000 us -> 354 us (0.35)
  waiting for transfers between devices: 594 us -> 211 us
  matrix products: 256 us -> 0 us
  Pallas kernels: 0 us -> 94.7 us
  local copies, waits for them, and re-layouts: 89.4 us -> 29.9 us
  other arithmetic: 37.5 us -> 2.93 us
    all_gather x12 -> x1, waiting for transfers between devices: 478 us -> 102 us  [gather_all(): lax.all_gather(packed, AXES, axis=0, tiled=True)]
    dot_general x45 -> x0, matrix products: 234 us -> none  [the longest x2 71.5 us: forward_pass(): jnp.dot(first_norm.astype(jnp.bfloat16), whole_inner, preferred_element_t...]
    pallas_call x0 -> x4, Pallas kernels: none -> 94.7 us  [the longest x1 44.8 us: feed(): pl.pallas_call(feed_kernel, grid=(rows // T,), in_specs=[row, row, row, o...]
    while x44 -> x0, local copies, waits for them, and re-layouts: 31.2 us -> none  [the longest x8 18.3 us: forward_pass(): lax.map(slot_forward, (heads_view(query_rows, slot_count), heads_view(key...]
    sub x2 -> x0, matrix products: 22 us -> none  [slot_forward(): shifted = jnp.exp(scores - row_top)]
    unnamed x85 -> x30, local copies, waits for them, and re-layouts: 20.7 us -> 4.07 us
    convert_element_type x7 -> x2, other arithmetic: 16.2 us -> 0.01 us  [the longest x1 0.01 us: layer(): qub = qu.astype(BF)]
    reduce_sum x8 -> x0, other arithmetic: 14.6 us -> none  [the longest x2 5.21 us: slot_forward(): row_total = jnp.sum(shifted, axis=-1, keepdims=True)]
  transfers between devices with their start and end apart: 13 -> 2, of which waited for: 13 -> 2; matrix products, arithmetic and copies ran while one was open for 23% -> 1% of each run, Pallas kernels for 0% -> 3%
where the time goes in v1:
time: 354 us; the launch traced here: 353 us
  waiting for transfers between devices  211 us (60%)
  Pallas kernels  94.7 us (27%)
  local copies, waits for them, and re-layouts  29.9 us (8%)
  between operations  14.3 us (4%)
    psum x1, waiting for transfers between devices, shards(): ad = lax.psum(ad, AXES) / slots  110 us
    all_gather x1, waiting for transfers between devices, gather_all(): lax.all_gather(packed, AXES, axis=0, tiled=True)  102 us
    pallas_call x1, Pallas kernels, feed(): pl.pallas_call(feed_kernel, grid=(rows // T,), in_specs=[row, row, row, o...  44.8 us
    pallas_call x1, Pallas kernels, attend(): pl.pallas_call(attend_kernel, grid_spec=gs, out_shape=[*[sd((rows, D), BF...  22.1 us
    pallas_call x1, Pallas kernels, attend_back(): pl.pallas_call(attend_back_kernel, grid=(S, J), in_specs=[blk, blk, blk,...  18.4 us
    slice x2, local copies, waits for them, and re-layouts, gather_all(): out.append(got[:, at:at + r].reshape(n * p.shape[0], p.shape[1]))  12.7 us
    pallas_call x1, Pallas kernels, inputs_grad(): pl.pallas_call(inputs_kernel, grid=(rows // T,), in_specs=[row, row, row,...  9.32 us
    reshape x1, local copies, waits for them, and re-layouts, gather_all(): out.append(got[:, at:at + r].reshape(n * p.shape[0], p.shape[1]))  8.46 us
  transfers between devices with their start and end apart: 2, of which 2 were waited for; matrix products, arithmetic and copies ran while one was open for 1% of the time, Pallas kernels for 3%

profile of v1, /device:TPU:0, one launch (start us, length us, event | category | flops | bytes accessed | tf_op | source)
XLA Modules:
  0.0 353.0 jit_solution(10979975775183433521)
XLA Ops:
  7.3 0.0 all-gather.2.cloned.1.call-start
  7.3 1.0 reshape.39
  8.3 0.8 constant_dynamic-update-slice_fusion.5
  9.1 0.8 constant_dynamic-update-slice_fusion.4
  9.9 0.8 constant_dynamic-update-slice_fusion.3
  10.6 0.8 constant_dynamic-update-slice_fusion.2
  11.4 0.9 constant_dynamic-update-slice_fusion
  12.4 0.0 copy-start
  12.4 0.8 copy-done
  13.1 0.0 all-gather.2.cloned.1.call-update
  13.1 0.0 all-reduce.8.cloned.1.call-start
  13.4 0.0 copy-start.1
  13.4 0.0 copy-start.2
  13.4 0.6 fusion.8
  14.0 0.2 copy.24
  14.2 0.7 pad.19.clone.dn_ref
  14.9 0.7 pad.21.upv_ref
  15.6 0.7 pad.20.upq_ref
  16.3 0.8 add_reduce_fusion.valid_ref
  17.1 0.6 fusion.7.nm_ref
  17.7 101.5 %all-gather.2.cloned.1.call-done = bf16[9216,768]{1,0:T(8,128)(2,1)} async-done(((bf16[288,768]{1,0:T(8,128)(2,1)}), bf16[9216,768]{1,0:T(8,128)(2,1)}) %all-gather.2.cloned.1.call-update) | async-done | bytes 14155792 | tf_op jit(solution)/shard_map/all_gather | solution.py:257
  119.2 4.7 %fusion.10 = (bf16[32,24,768]{2,1,0:T(8,128)(2,1)}, bf16[32,24,768]{2,1,0:T(8,128)(2,1)}, bf16[32,24,768]{2,1,0:T(8,128)(2,1)}, bf16[32,24,768]{2,1,0:T(8,128)(2,1)}) fusion(bf16[32,288,768]{2,1,0:T(8,128)(2,1)} %bitcast.13), kind=kLoop, calls=%fused_computation.22 | loop fusion | bytes 9437184 | tf_op jit(solution)/shard_map/slice | solution.py:261
  123.9 8.0 %fusion.9 = (bf16[32,96,768]{2,1,0:T(8,128)(2,1)}, bf16[32,96,768]{2,1,0:T(8,128)(2,1)}) fusion(bf16[32,288,768]{2,1,0:T(8,128)(2,1)} %bitcast.14), kind=kLoop, calls=%fused_computation.21 | loop fusion | bytes 18874368 | tf_op jit(solution)/shard_map/slice | solution.py:261
  131.9 8.5 %reshape.45.wi_ref = bf16[768,3072]{1,0:T(8,128)(2,1)} reshape(bf16[32,96,768]{2,1,0:T(8,128)(2,1)} %get-tuple-element.39) | data formatting | bytes 9437184 | tf_op jit(solution)/shard_map/reshape | solution.py:261
  140.4 22.1 %attend.1 = (bf16[1024,768]{1,0:T(8,128)(2,1)}, bf16[1024,768]{1,0:T(8,128)(2,1)}, bf16[1024,768]{1,0:T(8,128)(2,1)}, bf16[2,12,512,512]{3,2,1,0:T(8,128)(2,1)},...) custom-call(s32[2]{0:T(128)} %add_reduce_fusion.valid_ref, ...), custom_call_target="tpu_custom_call" | custom-call | tf_op jit(solution)/shard_map/attend/pallas_call | solution.py:75
  162.5 44.8 %feed.1 = (bf16[1024,768]{1,0:T(8,128)(2,1)}, f32[1024,768]{1,0:T(8,128)}, bf16[768,1024]{1,0:T(8,128)(2,1)}) custom-call(bf16[1024,768]{1,0:T(8,128)(2,1)} %x_ref.5, bf16[1024,768]{1,0:T(8,128)(2,1)} %get-tuple-element.22.o_ref, bf16[1024,768]{1,0:T(8,128)(2,1)} %go_ref.1, bf16[768,768]{1,0:T(8,128)(2,1)} %bitcast.21, bf16[768,3072]{1,0:T(8,128)(2,1)} %reshape.45.wi_ref, ...), custom_call_target="tpu_custom_call" | custom-call | tf_op jit(solution)/shard_map/feed/pallas_call | solution.py:130
  207.3 18.4 %attend_back.1 = (bf16[1024,768]{1,0:T(8,128)(2,1)}, bf16[1024,768]{1,0:T(8,128)(2,1)}, bf16[1024,768]{1,0:T(8,128)(2,1)}, bf16[2,16,512]{2,1,0:T(8,128)(2,1)}, f32[32,768]{1,0:T(8,128)}) custom-call(bf16[1024,768]{1,0:T(8,128)(2,1)} %get-tuple-element.25.q_ref, bf16[1024,768]{1,0:T(8,128)(2,1)} %get-tuple-element.26.k_ref, ...), custom_call_target="tpu_custom_call" | custom-call | tf_op jit(solution)/shard_map/attend_back/pallas_call | solution.py:208
  225.8 0.0 all-reduce.8.cloned.1.call-update
  225.8 9.3 %inputs_grad.1 = f32[1024,768]{1,0:T(8,128)} custom-call(f32[1024,768]{1,0:T(8,128)} %get-tuple-element.24.gfs_ref, bf16[1024,768]{1,0:T(8,128)(2,1)} %get-tuple-element.33.dq_ref, bf16[1024,768]{1,0:T(8,128)(2,1)} %get-tuple-element.34.dk_ref, bf16[1024,768]{1,0:T(8,128)(2,1)} %get-tuple-element.35.dv_ref, bf16[2,16,512]{2,1,0:T(8,128)(2,1)} %get-tuple-element.36.gl_ref, ...), custom_call_target="tpu_custom_call" | custom-call | tf_op jit(solution)/shard_map/inputs_grad/pallas_call | solution.py:230
  235.1 109.5 %all-reduce.8.cloned.1.call-done = f32[32,768]{1,0:T(8,128)} async-done(((f32[32,768]{1,0:T(8,128)}), f32[32,768]{1,0:T(8,128)}) %all-reduce.8.cloned.1.call-update) | async-done | bytes 98320 | tf_op jit(solution)/shard_map/psum | solution.py:269
  344.6 0.9 broadcast_multiply_fusion
  345.5 0.6 fusion.11
  (31 shorter events, 0.1 us)
Async XLA Ops:
  7.2 6.0 %copy-start.8 = (bf16[768]{0:T(1024)(128)(2,1)S(1)}, bf16[768]{0:T(1024)(128)(2,1)}, u32[]{:S(2)}) copy-start(bf16[768]{0:T(1024)(128)(2,1)} %param.25) | copy-start | bytes 4612
  7.2 6.0 %copy-start.9 = (bf16[768]{0:T(1024)(128)(2,1)S(1)}, bf16[768]{0:T(1024)(128)(2,1)}, u32[]{:S(2)}) copy-start(bf16[768]{0:T(1024)(128)(2,1)} %param.26) | copy-start | bytes 4612
  7.2 6.0 %copy-start.10 = (bf16[768]{0:T(1024)(128)(2,1)S(1)}, bf16[768]{0:T(1024)(128)(2,1)}, u32[]{:S(2)}) copy-start(bf16[768]{0:T(1024)(128)(2,1)} %param.27) | copy-start | bytes 4612
  7.2 6.1 %copy-start.11 = (bf16[768]{0:T(1024)(128)(2,1)S(1)}, bf16[768]{0:T(1024)(128)(2,1)}, u32[]{:S(2)}) copy-start(bf16[768]{0:T(1024)(128)(2,1)} %param.28) | copy-start | bytes 4612
  7.2 6.1 %copy-start.3 = (f32[768,8]{0,1:T(8,128)S(1)}, f32[768,8]{0,1:T(8,128)}, u32[]{:S(2)}) copy-start(f32[768,8]{0,1:T(8,128)} %param.29) | copy-start | bytes 73732
  7.2 6.1 %copy-start.4 = (f32[8,768]{1,0:T(8,128)S(1)}, f32[8,768]{1,0:T(8,128)}, u32[]{:S(2)}) copy-start(f32[8,768]{1,0:T(8,128)} %param.30) | copy-start | bytes 73732
  7.2 6.1 %copy-start.5 = (f32[768,8]{0,1:T(8,128)S(1)}, f32[768,8]{0,1:T(8,128)}, u32[]{:S(2)}) copy-start(f32[768,8]{0,1:T(8,128)} %param.31) | copy-start | bytes 73732
  7.2 6.1 %copy-start.6 = (f32[8,768]{1,0:T(8,128)S(1)}, f32[8,768]{1,0:T(8,128)}, u32[]{:S(2)}) copy-start(f32[8,768]{1,0:T(8,128)} %param.32) | copy-start | bytes 73732
  7.2 9.1 %copy-start.7 = (s32[2,2]{1,0:T(2,128)S(1)}, s32[2,2]{1,0:T(2,128)}, u32[]{:S(2)}) copy-start(s32[2,2]{1,0:T(2,128)} %param.18) | copy-start | bytes 52
  7.3 112.0 %all-gather.2.cloned.1.call-start = ((), (), s32[]{:S(2)}) async-start(), calls=%async_computation | async-start | bytes 14598144 | tf_op jit(solution)/shard_map/all_gather | solution.py:257
  12.4 0.8 copy-start
  13.1 331.5 %all-reduce.8.cloned.1.call-start = ((), (), s32[]{:S(2)}) async-start(), calls=%async_computation.1 | async-start | bytes 196608 | tf_op jit(solution)/shard_map/psum | solution.py:269
  13.4 110.5 %copy-start.1 = (bf16[16,768]{1,0:T(8,128)(2,1)}, bf16[16,768]{1,0:T(8,128)(2,1)S(1)}, u32[]{:S(2)}) copy-start(bf16[16,768]{1,0:T(8,128)(2,1)S(1)} %concatenate.15.upq_ref) | copy-start | bytes 73732
  13.4 110.5 %copy-start.2 = (bf16[16,768]{1,0:T(8,128)(2,1)}, bf16[16,768]{1,0:T(8,128)(2,1)S(1)}, u32[]{:S(2)}) copy-start(bf16[16,768]{1,0:T(8,128)(2,1)S(1)} %concatenate.16.upv_ref) | copy-start | bytes 73732
Sparse Core Ops, SparseCore 0:
  13.3 105.9 all-gather.1
  225.9 118.6 all-reduce.7

commit v2 on v1

v2 whole, which is shorter than its diff:
```python
import functools
import jax
import jax.numpy as jnp
from jax import lax
from jax.experimental import pallas as pl
from jax.experimental.pallas import tpu as pltpu
from jax.sharding import PartitionSpec as P

HEAD_DIM=64; SLOT=512
F32=jnp.float32; BF=jnp.bfloat16
MIB=1024*1024
AXES=("dp","fsdp")
sd=jax.ShapeDtypeStruct
ANY=pl.BlockSpec(memory_space=pl.ANY)
HELD=pl.BlockSpec(memory_space=pltpu.VMEM)
SCALARS=pl.BlockSpec(memory_space=pltpu.SMEM)


def params(mib=56):
    return pltpu.CompilerParams(vmem_limit_bytes=mib*MIB)

def takes(us):
    return pl.CostEstimate(flops=int(us*1.1e9),bytes_accessed=0,transcendentals=0)


def dg(a,b,ca,cb):
    return lax.dot_general(a,b,(((ca,),(cb,)),((),())),preferred_element_type=F32)

def far(v):
    return pltpu.with_memory_space_constraint(v,pltpu.HBM)


def block_copies(layout,me,bufs,outs,sems):
    if layout is None:
        return [[pltpu.make_async_copy(b,o,sems.at[t])] for t,(b,o) in enumerate(zip(bufs,outs))]
    first,second,other_first,other_second=bufs
    chip=lax.div(me,2); core=lax.rem(me,2)
    lists=[[] for _ in layout]
    count=[0]
    def add(lay,buf,at_block,origin,rel):
        dst=lax.bitwise_xor(chip,rel)
        half=buf.shape[-1]
        at=0
        for t,(bands,rows,start,size) in enumerate(lay):
            for b in range(bands):
                to=outs[t].at[pl.ds(pl.multiple_of(dst*rows+start,16),size),pl.ds(pl.multiple_of(2*half*b+origin*half,128),half)]
                lists[t].append(pltpu.make_async_copy(buf.at[at_block,pl.ds(at,size),:],to,sems.at[count[0]]))
                count[0]+=1
                at+=size
    for which,(near,far) in enumerate(((first,second),(other_first,other_second))):
        origin=core if which==0 else 1-core
        near_axis=1+origin
        far_axis=2-origin
        for hop,buf in enumerate((near,far)):
            for i in range(8):
                add(layout,buf,i,origin,hop*far_axis+(i//4)*near_axis+4*(i%4))
    return lists

def start_all(copies):
    for c in copies: c.start()

def wait_all(copies):
    for c in copies: c.wait()

def copy_count(layout):
    return 2 if layout is None else 32*sum(l[0] for l in layout)

def prep_kernel(qdt_ref,vdt_ref,qu_ref,vu_ref,ag_ref,ash_ref,fg_ref,fsh_ref,dn_ref,upq_ref,upv_ref,dnt_ref,nm_ref):
    D=qu_ref.shape[1]
    both=jnp.concatenate([qdt_ref[...],vdt_ref[...]],axis=0)
    dnt_ref[...]=both.astype(BF)
    dn_ref[...]=jnp.concatenate([both,jnp.zeros((112,D),F32)],axis=0).T.astype(BF)
    z8=jnp.zeros((8,D),F32); z=jnp.zeros((112,D),F32)
    upq_ref[...]=jnp.concatenate([qu_ref[...],z8,z],axis=0).astype(BF)
    upv_ref[...]=jnp.concatenate([z8,vu_ref[...],z],axis=0).astype(BF)
    for i,r in enumerate((ag_ref,ash_ref,fg_ref,fsh_ref)):
        nm_ref[i:i+1,:]=r[...].astype(F32)
    nm_ref[4:8,:]=jnp.zeros((4,D),F32)

def prep(qd,qu,vd,vu,ag,ash,fg,fsh):
    D=qu.shape[1]
    return pl.pallas_call(prep_kernel,out_shape=[sd((D,128),BF),sd((128,D),BF),sd((128,D),BF),sd((16,D),BF),sd((8,D),F32)],
        compiler_params=params(8),cost_estimate=takes(1),name="prep")(qd.T,vd.T,qu,vu,*(v.reshape(1,D) for v in (ag,ash,fg,fsh)))


def project_kernel(layout,sc_ref,x_ref,dn_ref,upq_ref,upv_ref,*rest):
    *blocks,qkv_ref,low_ref,wo,w,sems,osem=rest
    i=pl.program_id(0)
    D=x_ref.shape[1]
    whole=[pltpu.make_async_copy(w,wo,osem.at[0])]
    @pl.when(i==0)
    def _():
        copies,=block_copies(layout,sc_ref[0],blocks,(w,),sems)
        start_all(copies); wait_all(copies); start_all(whole)
    x=x_ref[...]
    rows=pl.ds(pl.multiple_of(i*SLOT,SLOT),SLOT)
    low=dg(x,dn_ref[...],1,0).astype(BF)
    low_ref[...]=low.T[:32]
    qkv_ref[rows,0:D]=(dg(x,w[:,0:D],1,0)+2.0*dg(low,upq_ref[...],1,0)).astype(BF)
    qkv_ref[rows,D:2*D]=dg(x,w[:,D:2*D],1,0).astype(BF)
    qkv_ref[rows,2*D:]=(dg(x,w[:,2*D:],1,0)+2.0*dg(low,upv_ref[...],1,0)).astype(BF)
    @pl.when(i==pl.num_programs(0)-1)
    def _(): wait_all(whole)

def project(scalars,x,dn,upq,upv,blocks,layout):
    rows,D=x.shape
    return pl.pallas_call(functools.partial(project_kernel,layout),grid=(rows//SLOT,),
        in_specs=[SCALARS,pl.BlockSpec((SLOT,D),lambda i:(i,0)),HELD,HELD,HELD]+[ANY]*len(blocks),
        out_specs=[HELD,pl.BlockSpec((32,SLOT),lambda i:(0,i)),ANY],
        out_shape=[sd((rows,3*D),BF),sd((32,rows),BF),pltpu.HBM((D,3*D),BF)],
        scratch_shapes=[pltpu.VMEM((D,3*D),BF),pltpu.SemaphoreType.DMA((copy_count(layout),)),pltpu.SemaphoreType.DMA((1,))],
        compiler_params=params(LIM["project"]),cost_estimate=takes(8),name="project")(scalars,x,dn,upq,upv,*map(far,blocks))

def attend_kernel(sc_ref,qkv_ref,e_ref,ot_ref,o_ref,rt_ref):
    s=pl.program_id(0); j=pl.program_id(1); J=pl.num_programs(1); D=256*J
    lane=lax.broadcasted_iota(jnp.int32,(SLOT,128),1)
    row=lax.broadcasted_iota(jnp.int32,(SLOT,128),0)
    bias=jnp.where(row<sc_ref[1+s],0.0,-1e30).astype(F32)
    rows=pl.ds(pl.multiple_of(s*SLOT,SLOT),SLOT)
    def part(which,p):
        return qkv_ref[rows,pl.ds(pl.multiple_of(which*D+256*j+128*p,128),128)].astype(F32)
    totals=[]; os=[]
    for p in range(2):
        qp=part(0,p)*0.125
        kp=part(1,p)
        vp=part(2,p)
        for h in range(2):
            own=(lane<64) if h==0 else (lane>=64)
            aux=64 if h==0 else 0
            one=jnp.where(lane==aux,1.0,0.0)
            qm=jnp.where(own,qp,one).astype(BF)
            km=jnp.where(own,kp,jnp.where(lane==aux,bias,0.0)).astype(BF)
            vm=jnp.where(own,vp,one).astype(BF)
            st=dg(km,qm,1,1)
            top=jnp.max(st,axis=0,keepdims=True)
            e=jnp.exp(st-top).astype(BF)
            e_ref[2*p+h]=e
            ot=dg(vm,e,0,0)
            r=1.0/ot[aux:aux+1]
            totals.append(r)
            lo=64*h
            os.append((ot[lo:lo+64]*r).astype(BF))
    ot=jnp.concatenate(os,axis=0)
    ot_ref[...]=ot
    o_ref[rows,pl.ds(pl.multiple_of(256*j,256),256)]=ot.T
    rt_ref[0]=jnp.concatenate(totals+totals,axis=0)

def attend(scalars,qkv,slots):
    rows=qkv.shape[0]; D=qkv.shape[1]//3; J=D//256; H=D//HEAD_DIM
    return pl.pallas_call(attend_kernel,grid=(slots,J),
        in_specs=[SCALARS,HELD],
        out_specs=[pl.BlockSpec((4,SLOT,SLOT),lambda s,j:(s*J+j,0,0)),pl.BlockSpec((256,SLOT),lambda s,j:(s*J+j,0)),HELD,pl.BlockSpec((1,8,SLOT),lambda s,j:(s*J+j,0,0))],
        out_shape=[pltpu.HBM((slots*H,SLOT,SLOT),BF),pltpu.HBM((slots*D,SLOT),BF),pltpu.VMEM((rows,D),BF),pltpu.HBM((slots*J,8,SLOT),F32)],
        compiler_params=params(LIM["attend"]),cost_estimate=takes(16),name="attend")(scalars,qkv)


def norm_stats(value):
    mean=jnp.mean(value,axis=-1,keepdims=True)
    c=value-mean
    r=lax.rsqrt(jnp.mean(c*c,axis=-1,keepdims=True)+1e-5)
    return c*r,r

def norm_back(g,n,r):
    return r*(g-jnp.mean(g,axis=-1,keepdims=True)-n*jnp.mean(g*n,axis=-1,keepdims=True))

def gelu_pair(v):
    cdf=0.5+0.5*lax.erf(v*0.7071067811865476)
    return v*cdf, cdf+(0.3989422804014327*v)*jnp.exp(-0.5*v*v)

CH=512
TILE=256
LIM={"project":20,"attend":24,"feed_in":16,"feed_out":24,"attend_back":24,"inputs_grad":24}

def feed_in_kernel(layout,sc_ref,x_ref,o_ref,nm_ref,*rest):
    *blocks,n1_ref,r1_ref,act_ref,gp_ref,wo,wi,sems=rest
    i=pl.program_id(0)
    @pl.when(i==0)
    def _():
        lists=block_copies(layout,sc_ref[0],blocks,(wo,wi),sems)
        for l in lists: start_all(l)
        for l in lists: wait_all(l)
    T=x_ref.shape[0]
    rows=pl.ds(pl.multiple_of(i*T,T),T)
    first=x_ref[...].astype(F32)+dg(o_ref[rows,:],wo[...],1,0)
    n1,r1=norm_stats(first)
    n1_ref[rows,:]=n1; r1_ref[rows,:]=jnp.broadcast_to(r1,(T,128))
    hb=(n1*nm_ref[0:1,:]+nm_ref[1:2,:]).astype(BF)
    for c in range(wi.shape[1]//CH):
        z=dg(hb,wi[:,c*CH:(c+1)*CH],1,0)
        act,gp=gelu_pair(z)
        act_ref[rows,c*CH:(c+1)*CH]=act.astype(BF)
        gp_ref[rows,c*CH:(c+1)*CH]=gp.astype(BF)

def feed_in(scalars,x,o,nm,blocks,layout,FF):
    rows,D=x.shape
    return pl.pallas_call(functools.partial(feed_in_kernel,layout),grid=(rows//TILE,),
        in_specs=[SCALARS,pl.BlockSpec((TILE,D),lambda i:(i,0)),HELD,HELD]+[ANY]*len(blocks),
        out_specs=[HELD]*6,
        out_shape=[pltpu.VMEM((rows,D),F32),pltpu.VMEM((rows,128),F32),pltpu.VMEM((rows,FF),BF),pltpu.VMEM((rows,FF),BF),pltpu.VMEM((D,D),BF),pltpu.VMEM((D,FF),BF)],
        scratch_shapes=[pltpu.SemaphoreType.DMA((copy_count(layout),))],
        compiler_params=params(LIM["feed_in"]),cost_estimate=takes(17),name="feed_in")(scalars,x,o,nm,*map(far,blocks))

def feed_out_kernel(layout,sc_ref,n1_ref,r1_ref,act_ref,gp_ref,go_ref,nm_ref,wo,wi,*rest):
    *blocks,out_ref,gfs_ref,gmt_ref,wt,gi_ref,sems=rest
    i=pl.program_id(0)
    @pl.when(i==0)
    def _():
        copies,=block_copies(layout,sc_ref[0],blocks,(wt,),sems)
        start_all(copies); wait_all(copies)
    T=go_ref.shape[0]
    rows=pl.ds(pl.multiple_of(i*T,T),T)
    ag,ash,fg,fsh=(nm_ref[i:i+1,:] for i in range(4))
    n1=n1_ref[rows,:]; r1=r1_ref[rows,0:1]
    acc=n1*ag+ash+dg(act_ref[rows,:],wt[...],1,0)
    n2,r2=norm_stats(acc)
    out_ref[...]=(n2*fg+fsh).astype(BF)
    g2=norm_back(go_ref[...].astype(F32)*fg,n2,r2)
    g2b=g2.astype(BF)
    for c in range(wi.shape[1]//CH):
        ga=dg(g2b,wt[c*CH:(c+1)*CH,:],1,1)
        gi_ref[:,c*CH:(c+1)*CH]=(ga*gp_ref[rows,c*CH:(c+1)*CH].astype(F32)).astype(BF)
    g1=norm_back((g2+dg(gi_ref[...],wi[...],1,1))*ag,n1,r1)
    gfs_ref[...]=g1
    gmt_ref[:,rows]=dg(wo[...],g1.astype(BF),1,1).astype(BF)

def feed_out(scalars,n1,r1,act,gp,go,wo,wi,nm,blocks,layout):
    rows,D=n1.shape; FF=wi.shape[1]
    row=pl.BlockSpec((TILE,D),lambda i:(i,0))
    return pl.pallas_call(functools.partial(feed_out_kernel,layout),grid=(rows//TILE,),
        in_specs=[SCALARS,HELD,HELD,HELD,HELD,row,HELD,HELD,HELD]+[ANY]*len(blocks),
        out_specs=[row,row,HELD],
        out_shape=[sd((rows,D),BF),pltpu.HBM((rows,D),F32),pltpu.VMEM((D,rows),BF)],
        scratch_shapes=[pltpu.VMEM((FF,D),BF),pltpu.VMEM((TILE,FF),BF),pltpu.SemaphoreType.DMA((copy_count(layout),))],
        compiler_params=params(LIM["feed_out"]),cost_estimate=takes(28),name="feed_out")(scalars,n1,r1,act,gp,go,nm,wo,wi,*map(far,blocks))


def attend_back_kernel(sc_ref,q_ref,k_ref,v_ref,e_ref,ot_ref,rt_ref,gmt_ref,x_ref,low_ref,upq_ref,upv_ref,
                       d_ref,gl_ref,mine_ref,other_ref,glacc,ad_ref):
    s=pl.program_id(0); j=pl.program_id(1); J=pl.num_programs(1)
    lane=lax.broadcasted_iota(jnp.int32,(SLOT,128),1)
    rowi=lax.broadcasted_iota(jnp.int32,(128,SLOT),0)
    D=256*J
    rows=pl.ds(pl.multiple_of(s*SLOT,SLOT),SLOT)
    def place_of(which,p):
        return rows,pl.ds(pl.multiple_of(which*D+256*j+128*p,128),128)
    gmq=gmt_ref[pl.ds(pl.multiple_of(256*j,256),256),rows]
    otq=ot_ref[...]
    dqts=[]; dvs=[]
    for p in range(2):
        cols=slice(128*p,128*p+128)
        qp,kp,vp=(w[:,cols].astype(F32) for w in (q_ref,k_ref,v_ref))
        qp=qp*0.125; kp=kp*0.125
        gm=gmq[cols,:].astype(F32); om=otq[cols,:].astype(F32)
        pr=gm*om
        dkp=None; dvp=None; dqt=None
        for h in range(2):
            own=(lane<64) if h==0 else (lane>=64)
            ownr=(rowi<64) if h==0 else (rowi>=64)
            aux=64 if h==0 else 0
            r=rt_ref[0,2*p+h:2*p+h+1,:]
            d=-jnp.sum(pr[64*h:64*h+64],axis=0,keepdims=True)*r
            dhi=d.astype(BF).astype(F32)
            dlo=d-dhi
            gs=gm*r
            gaug=jnp.where(ownr,gs,jnp.where(rowi==aux,dhi,jnp.where(rowi==aux+1,dlo,0.0))).astype(BF)
            gown=jnp.where(ownr,gs,0.0).astype(BF)
            vm=jnp.where(own,vp,jnp.where((lane==aux)|(lane==aux+1),1.0,0.0)).astype(BF)
            e=e_ref[2*p+h]
            ds=(dg(vm,gaug,1,0)*e.astype(F32)).astype(BF)
            qm=jnp.where(own,qp,0.0).astype(BF)
            km=jnp.where(own,kp,0.0).astype(BF)
            dv=dg(e,gown,1,1)
            dk=dg(ds,qm,1,0)
            dq=dg(km,ds,0,0)
            dvp=dv if dvp is None else dvp+dv
            dkp=dk if dkp is None else dkp+dk
            dqt=dq if dqt is None else dqt+dq
        d_ref[place_of(1,p)]=dkp.astype(BF)
        dvs.append(dvp.astype(BF))
        d_ref[place_of(2,p)]=dvs[p]
        dqts.append(dqt.astype(BF))
    dqt=jnp.concatenate(dqts,axis=0)
    dqb=dqt.T
    d_ref[rows,pl.ds(pl.multiple_of(256*j,256),256)]=dqb
    dvb=jnp.concatenate(dvs,axis=1)
    glq=dg(upq_ref[...],dqt,1,0)
    glv=dg(upv_ref[...],dvb,1,1)
    part=2.0*(glq+glv)
    @pl.when(j==0)
    def _(): glacc[...]=part
    @pl.when(j>0)
    def _(): glacc[...]+=part
    low=low_ref[...]
    c0=pl.multiple_of(j*256,256)
    upq=2.0*dg(low[:16],dqb,1,0)
    upv=2.0*dg(low[:16],dvb,1,0)
    upg=jnp.concatenate([upq[0:8],upv[8:16]],axis=0)
    def add(rows,cols,v):
        @pl.when(s==0)
        def _(): ad_ref[rows,cols]=v
        @pl.when(s>0)
        def _(): ad_ref[rows,cols]+=v
    add(slice(16,32),pl.ds(c0,256),upg)
    @pl.when(j==J-1)
    def _():
        gl=glacc[...].astype(BF)
        gl_ref[...]=gl
        add(slice(0,16),slice(None),dg(gl,x_ref[...],1,0))
        core=lax.rem(sc_ref[0],2)
        for c,(a,b) in enumerate(((mine_ref,other_ref),(other_ref,mine_ref))):
            @pl.when((s==pl.num_programs(0)-1)&(core==c))
            def _():
                a[...]=ad_ref[0:16,:]
                b[...]=ad_ref[16:32,:]

def attend_back(scalars,qkv,e,ot,rt,gmt,x,low,upq,upv):
    rows,D=x.shape; J=D//256; S=rows//SLOT
    up=pl.BlockSpec((16,256),lambda s,j:(0,j))
    return pl.pallas_call(attend_back_kernel,grid=(S,J),
        in_specs=[SCALARS,*[pl.BlockSpec((SLOT,256),lambda s,j,w=w:(s,w*J+j)) for w in range(3)],
                  pl.BlockSpec((4,SLOT,SLOT),lambda s,j:(s*J+j,0,0)),pl.BlockSpec((256,SLOT),lambda s,j:(s*J+j,0)),
                  pl.BlockSpec((1,8,SLOT),lambda s,j:(s*J+j,0,0)),HELD,
                  pl.BlockSpec((SLOT,D),lambda s,j:(s,0)),pl.BlockSpec((32,SLOT),lambda s,j:(0,s)),up,up],
        out_specs=[HELD,pl.BlockSpec((16,SLOT),lambda s,j:(0,s)),HELD,HELD],
        out_shape=[pltpu.VMEM((rows,3*D),BF),sd((16,rows),BF),pltpu.VMEM((16,D),F32),pltpu.VMEM((16,D),F32)],
        scratch_shapes=[pltpu.VMEM((16,SLOT),F32),pltpu.VMEM((32,D),F32)],
        compiler_params=params(LIM["attend_back"]),cost_estimate=takes(18),name="attend_back")(scalars,far(qkv),far(qkv),far(qkv),far(e),far(ot),rt,gmt,x,low,upq,upv)

def inputs_kernel(gfs_ref,d_ref,gl,w_ref,dnt_ref,out_ref):
    T=gfs_ref.shape[0]
    rows=pl.ds(pl.multiple_of(pl.program_id(0)*T,T),T)
    out_ref[...]=gfs_ref[...]+dg(d_ref[rows,:],w_ref[...],1,1)+dg(gl[...],dnt_ref[...],0,0)

def inputs_grad(gfs,d,gl,w,dnt):
    rows,D=gfs.shape
    row=pl.BlockSpec((SLOT,D),lambda i:(i,0))
    return pl.pallas_call(inputs_kernel,grid=(rows//SLOT,),
        in_specs=[row,HELD,pl.BlockSpec((16,SLOT),lambda i:(0,i)),HELD,HELD],
        out_specs=row,out_shape=sd((rows,D),F32),
        compiler_params=params(LIM["inputs_grad"]),cost_estimate=takes(7),name="inputs_grad")(gfs,d,gl,w,dnt)


def device_count():
    return lax.axis_size("dp")*lax.axis_size("fsdp")

def permute(v,target):
    return lax.ppermute(v,AXES,[(i,target(i)) for i in range(device_count())])

def exchange(v,mask):
    return permute(v,lambda i:i^mask)

def along_z(block):
    top=device_count()//4
    return [block]+[exchange(block,top*m) for m in (1,2,3)]

def near_hop(v):
    return permute(v,lambda i:i^(4 if i%2 else 2))

def far_hop(v):
    return permute(v,lambda i:i^(2 if i%2 else 4))

def core_pair(v):
    groups=[[2*i,2*i+1] for i in range(lax.axis_size("fsdp")//2)]
    return lax.all_gather(v,"fsdp",axis=0,tiled=False,axis_index_groups=groups)

def column_half(both):
    c=lax.axis_index("fsdp")%2
    half=both.shape[2]//2
    return lax.dynamic_slice_in_dim(both,c*half,half,axis=2).reshape(-1,half)

def total_over_devices(mine,other,meanwhile):
    n=device_count()
    mine=mine+exchange(other,1)
    got=[exchange(mine,m) for m in range(2,n//4,2)]
    for g in got: mine=mine+g
    got=[exchange(mine,m) for m in (n//4,n//2,3*n//4)]
    got,done=tie(got,meanwhile())
    for g in got: mine=mine+g
    return mine,exchange(mine,1),done

def finish_kernel(scale,sc_ref,mine_ref,other_ref,*outs):
    core=lax.rem(sc_ref[0],2)
    for c,halves in enumerate(((mine_ref,other_ref),(other_ref,mine_ref))):
        @pl.when(core==c)
        def _():
            for i,o in enumerate(outs): o[...]=halves[i//2][8*(i%2):8*(i%2)+8,:]*scale

def finish(scalars,mine,other,scale):
    D=mine.shape[1]
    return pl.pallas_call(functools.partial(finish_kernel,scale),in_specs=[SCALARS,HELD,HELD],out_specs=[HELD]*4,
        out_shape=[sd((8,D),F32)]*4,compiler_params=params(8),cost_estimate=takes(1),name="finish")(scalars,mine,other)

def tie(*v):
    return lax.optimization_barrier(v)

def by_hops(scalars,x,wq,wk,wv,wo,wi,wt,ag,ash,fg,fsh,qd,qu,vd,vu,go):
    D=wq.shape[1]; FF=wi.shape[1]; bands=FF//D; r=wq.shape[0]; rt_=wt.shape[0]
    top=device_count()//4
    both=core_pair(jnp.concatenate([wq,wk,wv],0))
    s1=jnp.concatenate([column_half(both[:,r*t:r*t+r]) for t in range(3)],0)
    z1=along_z(s1)
    wo,wi,wt,qd,s1=tie(wo,wi,wt,qd,s1)
    bo,bi,bt=core_pair(wo),core_pair(wi),core_pair(wt)
    s2=jnp.concatenate([column_half(bo)]+[column_half(bi[:,:,D*t:D*t+D]) for t in range(bands)],0)
    s3=column_half(bt)
    dn,upq,upv,dnt,nm=prep(qd,qu,vd,vu,ag,ash,fg,fsh)
    z1,s2,s3,dn,scalars=tie(z1,s2,s3,dn,scalars)
    a1=jnp.stack(z1,0)
    n1=near_hop(a1)
    z22=exchange(s2,2*top)
    n1,z22,s2=tie(n1,z22,s2)
    f1=jnp.concatenate([a1,n1],0)
    h1=far_hop(f1); of1=exchange(f1,1)
    z23=exchange(s2,3*top); z21=exchange(s2,top)
    h1,of1,z23,z21,s3=tie(h1,of1,z23,z21,s3)
    oh1=exchange(h1,1)
    a2=jnp.stack([s2,z21,z22,z23],0)
    n2=near_hop(a2)
    z31,z32,z33=(exchange(s3,m*top) for m in (1,2,3))
    oh1,=tie(oh1)
    qkv,low,wqkv=project(scalars,x,dn,upq,upv,(f1,h1,of1,oh1),((3,2*r,0,2*r),))
    n2,qkv,z31,z32,z33,s3=tie(n2,qkv,z31,z32,z33,s3)
    f2=jnp.concatenate([a2,n2],0)
    h2=far_hop(f2); of2=exchange(f2,1)
    a3=jnp.stack([s3,z31,z32,z33],0)
    n3=near_hop(a3)
    e,ot,o,rt=attend(scalars,qkv,x.shape[0]//SLOT)
    h2,o,of2=tie(h2,o,of2)
    oh2=exchange(h2,1)
    n3,oh2=tie(n3,oh2)
    f3=jnp.concatenate([a3,n3],0)
    h3=far_hop(f3); of3=exchange(f3,1)
    nn,r1,act,gp,wo,wi=feed_in(scalars,x,o,nm,(f2,h2,of2,oh2),((1,2*r,0,2*r),(bands,2*r,0,2*r)),FF)
    h3,nn,of3=tie(h3,nn,of3)
    oh3=exchange(h3,1)
    out,gfs,gmt=feed_out(scalars,nn,r1,act,gp,go,wo,wi,nm,(f3,h3,of3,oh3),((1,2*rt_,0,2*rt_),))
    return qkv,low,wqkv,e,ot,rt,out,gfs,gmt,upq,upv,dnt

def by_all_gather(scalars,x,wq,wk,wv,wo,wi,wt,ag,ash,fg,fsh,qd,qu,vd,vu,go):
    wq,wk,wv,wo,wi,wt=(lax.all_gather(w,AXES,axis=0,tiled=True) for w in (wq,wk,wv,wo,wi,wt))
    dn,upq,upv,dnt,nm=prep(qd,qu,vd,vu,ag,ash,fg,fsh)
    qkv,low,wqkv=project(scalars,x,dn,upq,upv,(jnp.concatenate([wq,wk,wv],1),),None)
    e,ot,o,rt=attend(scalars,qkv,x.shape[0]//SLOT)
    nn,r1,act,gp,wo,wi=feed_in(scalars,x,o,nm,(wo,wi),None,wi.shape[1])
    out,gfs,gmt=feed_out(scalars,nn,r1,act,gp,go,wo,wi,nm,(wt,),None)
    return qkv,low,wqkv,e,ot,rt,out,gfs,gmt,upq,upv,dnt

def shards(x,lengths,wq,wk,wv,wo,wi,wt,ag,ash,fg,fsh,qd,qu,vd,vu,go):
    n=device_count()
    valid=lengths[:,0]+lengths[:,1]+4
    me=(lax.axis_index("dp")*lax.axis_size("fsdp")+lax.axis_index("fsdp")).reshape(1)
    scalars=jnp.concatenate([me,valid]).astype(jnp.int32)
    forward=by_hops if n==32 and wq.shape[0]%8==0 else by_all_gather
    qkv,low,wqkv,e,ot,rt,out,gfs,gmt,upq,upv,dnt=forward(scalars,x,wq,wk,wv,wo,wi,wt,ag,ash,fg,fsh,qd,qu,vd,vu,go)
    d,gl,mine,other=attend_back(scalars,qkv,e,ot,rt,gmt,x,low,upq,upv)
    mine,other,gx=total_over_devices(mine,other,lambda: inputs_grad(gfs,d,gl,wqkv,dnt))
    qd,vd,qu,vu=finish(scalars,mine,other,1.0/(lengths.shape[0]*n))
    return out,gx,qd.T,qu,vd.T,vu

def solution(mesh):
    sp=P(AXES,None)
    return jax.shard_map(shards,mesh=mesh,in_specs=(sp,)*8+(P(),)*8+(sp,),
        out_specs=(sp,sp,P(),P(),P(),P()),check_vma=False)
```

time: 354 us -> 177 us (0.50)
  waiting for transfers between devices: 211 us -> 39.4 us
  starting transfers between devices: 0.08 us -> 30.4 us
  local copies, waits for them, and re-layouts: 29.9 us -> 2.89 us
  between operations: 14.3 us -> 1.37 us
  blocking collectives: 0 us -> 8.08 us
    psum x1 -> x0, waiting for transfers between devices: 110 us -> none  [shards(): ad = lax.psum(ad, AXES) / slots]
    all_gather x1 -> x0, waiting for transfers between devices: 102 us -> none  [gather_all(): lax.all_gather(packed, AXES, axis=0, tiled=True)]
    ppermute x0 -> x29, waiting for transfers between devices: none -> 39.4 us  [permute(): lax.ppermute(v, AXES, [(i, target(i)) for i in range(device_count())])]
    ppermute x0 -> x29, starting transfers between devices: none -> 30.4 us  [permute(): lax.ppermute(v, AXES, [(i, target(i)) for i in range(device_count())])]
    slice x3 -> x2, local copies, waits for them, and re-layouts: 13.3 us -> 0.04 us  [the longest x1 0.02 us: by_hops(): bi[:, :, D * t:D * t + D]]
    reshape x2 -> x4, local copies, waits for them, and re-layouts: 9.48 us -> 0.02 us  [prep(): v.reshape(1, D)]
    all_gather x0 -> x4, blocking collectives: none -> 8.08 us  [core_pair(): lax.all_gather(v, 'fsdp', axis=0, tiled=False, axis_index_groups=groups)]
    pallas_call x4 -> x8, Pallas kernels: 94.7 us -> 92.6 us  [the longest x1 26.5 us: feed_out(): pl.pallas_call(functools.partial(feed_out_kernel, layout), grid=(rows //...]
  transfers between devices with their start and end apart: 2 -> 29, of which waited for: 2 -> 13; matrix products, arithmetic and copies ran while one was open for 1% -> 1% of each run, Pallas kernels for 3% -> 27%
where the time goes in v2:
time: 177 us; the launch traced here: 176 us
  Pallas kernels  92.6 us (52%)
  waiting for transfers between devices  39.4 us (22%)
  starting transfers between devices  30.4 us (17%)
  blocking collectives  8.08 us (5%)
  local copies, waits for them, and re-layouts  2.89 us (2%)
    ppermute x29, waiting for transfers between devices, permute(): lax.ppermute(v, AXES, [(i, target(i)) for i in range(device_count())])  39.4 us
    ppermute x29, starting transfers between devices, permute(): lax.ppermute(v, AXES, [(i, target(i)) for i in range(device_count())])  30.4 us
    pallas_call x1, Pallas kernels, feed_out(): pl.pallas_call(functools.partial(feed_out_kernel, layout), grid=(rows //...  26.5 us
    pallas_call x1, Pallas kernels, attend_back(): pl.pallas_call(attend_back_kernel, grid=(S, J), in_specs=[SCALARS, *[pl.B...  17.3 us
    pallas_call x1, Pallas kernels, feed_in(): pl.pallas_call(functools.partial(feed_in_kernel, layout), grid=(rows // T...  17.1 us
    pallas_call x1, Pallas kernels, attend(): pl.pallas_call(attend_kernel, grid=(slots, J), in_specs=[SCALARS, HELD],...  15.7 us
    pallas_call x1, Pallas kernels, project(): pl.pallas_call(functools.partial(project_kernel, layout), grid=(rows // S...  8.97 us
    all_gather x4, blocking collectives, core_pair(): lax.all_gather(v, 'fsdp', axis=0, tiled=False, axis_index_groups=groups)  8.08 us
  transfers between devices with their start and end apart: 29, of which 13 were waited for; matrix products, arithmetic and copies ran while one was open for 1% of the time, Pallas kernels for 27%

profile of v2, /device:TPU:0, one launch (start us, length us, event | category | flops | bytes accessed | tf_op | source)
XLA Modules:
  0.0 176.2 jit_solution(11075416501497881918)
XLA Ops:
  1.6 2.2 %all-gather = bf16[144,768]{1,0:T(8,128)(2,1)S(1)} all-gather(bf16[72,768]{1,0:T(8,128)(2,1)S(1)} %pad_maximum_fusion.3), channel_id=2, replica_groups={{0,1},{2,3},{4,5},{6,7},{8,9},{10,11},{12,13},{14,15},{16,17},{18,19},{..., dimensions={0}, use_global_device_ids=true | all-gather | bytes 331776 | tf_op jit(solution)/shard_map/all_gather | solution.py:364
  4.0 5.0 %collective-permute-start.2 = (bf16[144,384]{1,0:T(8,128)(2,1)S(1)}, bf16[144,384]{1,0:T(8,128)(2,1)S(1)}, u32[]{:S(2)}, u32[]{:S(2)}) collective-permute-start(bf16[144,384]{1,0:T(8,128)(2,1)S(1)} %pad_maximum_fusion.4), channel_id=1, source_target_pairs={{0,24},{1,25},{2,26},{3,27},{4,28},{5,29},{6,30},{7,31},{8,16},{9,... | collective-permute-start | bytes 331784 | tf_op jit(solution)/shard_map/ppermute | solution.py:347
  9.9 1.9 %all-gather.1 = bf16[48,768]{1,0:T(8,128)(2,1)S(1)} all-gather(bf16[24,768]{1,0:T(8,128)(2,1)S(1)} %copy-done.12), channel_id=3, replica_groups={{0,1},{2,3},{4,5},{6,7},{8,9},{10,11},{12,13},{14,15},{16,17},{18,19},{..., dimensions={0}, use_global_device_ids=true | all-gather | bytes 110592 | tf_op jit(solution)/shard_map/all_gather | solution.py:364
  11.8 2.0 %all-gather.2 = bf16[48,3072]{1,0:T(8,128)(2,1)S(1)} all-gather(bf16[24,3072]{1,0:T(8,128)(2,1)S(1)} %copy-done.10), channel_id=4, replica_groups={{0,1},{2,3},{4,5},{6,7},{8,9},{10,11},{12,13},{14,15},{16,17},{18,19},{..., dimensions={0}, use_global_device_ids=true | all-gather | bytes 442368 | tf_op jit(solution)/shard_map/all_gather | solution.py:364
  13.9 2.0 %all-gather.3 = bf16[192,768]{1,0:T(8,128)(2,1)S(1)} all-gather(bf16[96,768]{1,0:T(8,128)(2,1)S(1)} %copy-done.11), channel_id=5, replica_groups={{0,1},{2,3},{4,5},{6,7},{8,9},{10,11},{12,13},{14,15},{16,17},{18,19},{..., dimensions={0}, use_global_device_ids=true | all-gather | bytes 442368 | tf_op jit(solution)/shard_map/all_gather | solution.py:364
  16.3 2.3 %collective-permute-done.1 = bf16[144,384]{1,0:T(8,128)(2,1)S(1)} collective-permute-done((bf16[144,384]{1,0:T(8,128)(2,1)S(1)}, bf16[144,384]{1,0:T(8,128)(2,1)S(1)}, u32[]{:S(2)}, u32[]{:S(2)}) %collective-permute-start.1) | collective-permute-done | bytes 110624 | tf_op jit(solution)/shard_map/ppermute | solution.py:347
  18.8 1.6 collective-permute-start.3
  20.4 8.8 %collective-permute-done.4 = bf16[240,384]{1,0:T(8,128)(2,1)S(1)} collective-permute-done((bf16[240,384]{1,0:T(8,128)(2,1)S(1)}, bf16[240,384]{1,0:T(8,128)(2,1)S(1)}, u32[]{:S(2)}, u32[]{:S(2)}) %collective-permute-start.4) | collective-permute-done | bytes 184352 | tf_op jit(solution)/shard_map/ppermute | solution.py:347
  29.3 1.6 collective-permute-start.5
  31.9 1.3 collective-permute-start.7
  33.2 4.9 %collective-permute-done.8 = bf16[240,384]{1,0:T(8,128)(2,1)S(1)} collective-permute-done((bf16[240,384]{1,0:T(8,128)(2,1)S(1)}, bf16[240,384]{1,0:T(8,128)(2,1)S(1)}, u32[]{:S(2)}, u32[]{:S(2)}) %collective-permute-start.8) | collective-permute-done | bytes 184352 | tf_op jit(solution)/shard_map/ppermute | solution.py:347
  38.1 3.8 %collective-permute-done.7 = bf16[240,384]{1,0:T(8,128)(2,1)S(1)} collective-permute-done((bf16[240,384]{1,0:T(8,128)(2,1)S(1)}, bf16[240,384]{1,0:T(8,128)(2,1)S(1)}, u32[]{:S(2)}, u32[]{:S(2)}) %collective-permute-start.7) | collective-permute-done | bytes 184352 | tf_op jit(solution)/shard_map/ppermute | solution.py:347
  42.5 2.1 %collective-permute-start.13 = (bf16[192,384]{1,0:T(8,128)(2,1)S(1)}, bf16[192,384]{1,0:T(8,128)(2,1)S(1)}, u32[]{:S(2)}, u32[]{:S(2)}) collective-permute-start(bf16[192,384]{1,0:T(8,128)(2,1)S(1)} %bitcast.44), channel_id=1, source_target_pairs={{0,24},{1,25},{2,26},{3,27},{4,28},{5,29},{6,30},{7,31},{8,16},{9,... | collective-permute-start | bytes 442376 | tf_op jit(solution)/shard_map/ppermute | solution.py:347
  45.0 2.0 %collective-permute-start.11 = (bf16[192,384]{1,0:T(8,128)(2,1)S(1)}, bf16[192,384]{1,0:T(8,128)(2,1)S(1)}, u32[]{:S(2)}, u32[]{:S(2)}) collective-permute-start(bf16[192,384]{1,0:T(8,128)(2,1)S(1)} %bitcast.46), channel_id=1, source_target_pairs={{0,8},{1,9},{2,10},{3,11},{4,12},{5,13},{6,14},{7,15},{8,0},{9,1},... | collective-permute-start | bytes 442376 | tf_op jit(solution)/shard_map/ppermute | solution.py:347
  47.1 1.6 collective-permute-start.9
  49.7 9.0 %project.1 = (bf16[1024,2304]{1,0:T(8,128)(2,1)S(1)}, bf16[32,1024]{1,0:T(8,128)(2,1)S(1)}, bf16[768,2304]{1,0:T(8,128)(2,1)}) custom-call(s32[3]{0:T(128)S(1)} %pad_add_fusion.sc_ref, bf16[1024,768]{1,0:T(8,128)(2,1)S(1)} %copy-done.1, bf16[768,128]{1,0:T(8,128)(2,1)S(1)} %get-tuple-element.90.dn_ref, bf16[128,768]{1,0:T(8,128)(2,1)S(1)} %get-tuple-element.91.upq_ref, ...), custom_call_target="tpu_custom_call" | custom-call | flops 8800000000 | tf_op jit(solution)/shard_map/project/pallas_call | solution.py:107
  59.0 1.6 collective-permute-start.15
  60.6 15.7 %attend.1 = (bf16[24,512,512]{2,1,0:T(8,128)(2,1)}, bf16[1536,512]{1,0:T(8,128)(2,1)}, bf16[1024,768]{1,0:T(8,128)(2,1)S(1)}, f32[6,8,512]{2,1,0:T(8,128)}) custom-call(s32[3]{0:T(128)S(1)} %pad_add_fusion.sc_ref, bf16[1024,2304]{1,0:T(8,128)(2,1)S(1)} %get-tuple-element.102.qkv_ref.q_ref.k_ref.v_ref), custom_call_target="tpu_custom_call" | custom-call | flops 17600000000 | tf_op jit(solution)/shard_map/attend/pallas_call | solution.py:150
  76.3 2.1 %collective-permute-done.15.rest_1_ = bf16[8,240,384]{2,1,0:T(8,128)(2,1)S(1)} collective-permute-done((bf16[8,240,384]{2,1,0:T(8,128)(2,1)S(1)}, bf16[8,240,384]{2,1,0:T(8,128)(2,1)S(1)}, u32[]{:S(2)}, u32[]{:S(2)}) %collective-permute-start.15) | collective-permute-done | bytes 1474592 | tf_op jit(solution)/shard_map/ppermute | solution.py:347
  78.5 1.5 collective-permute-start.14
  80.1 8.3 %collective-permute-done.14 = bf16[4,192,384]{2,1,0:T(8,128)(2,1)S(1)} collective-permute-done((bf16[4,192,384]{2,1,0:T(8,128)(2,1)S(1)}, bf16[4,192,384]{2,1,0:T(8,128)(2,1)S(1)}, u32[]{:S(2)}, u32[]{:S(2)}) %collective-permute-start.14) | collective-permute-done | bytes 589856 | tf_op jit(solution)/shard_map/ppermute | solution.py:347
  88.7 1.6 collective-permute-start.18
  90.3 17.1 %feed_in.1 = (f32[1024,768]{1,0:T(8,128)S(1)}, f32[1024,128]{1,0:T(8,128)S(1)}, bf16[1024,3072]{1,0:T(8,128)(2,1)S(1)}, bf16[1024,3072]{1,0:T(8,128)(2,1)S(1)}, ...) custom-call(s32[3]{0:T(128)S(1)} %pad_add_fusion.sc_ref, bf16[1024,768]{1,0:T(8,128)(2,1)S(1)} %copy-done.1, ...), custom_call_target="tpu_custom_call" | custom-call | flops 18699999232 | tf_op jit(solution)/shard_map/feed_in/pallas_call | solution.py:196
  107.6 2.8 %collective-permute-done.20.rest_3_ = bf16[8,192,384]{2,1,0:T(8,128)(2,1)S(1)} collective-permute-done((bf16[8,192,384]{2,1,0:T(8,128)(2,1)S(1)}, bf16[8,192,384]{2,1,0:T(8,128)(2,1)S(1)}, u32[]{:S(2)}, u32[]{:S(2)}) %collective-permute-start.20) | collective-permute-done | bytes 1179680 | tf_op jit(solution)/shard_map/ppermute | solution.py:347
  111.4 26.5 %feed_out.1 = (bf16[1024,768]{1,0:T(8,128)(2,1)}, f32[1024,768]{1,0:T(8,128)}, bf16[768,1024]{1,0:T(8,128)(2,1)S(1)}) custom-call(s32[3]{0:T(128)S(1)} %pad_add_fusion.sc_ref, f32[1024,768]{1,0:T(8,128)S(1)} %get-tuple-element.111.n1_ref, f32[1024,128]{1,0:T(8,128)S(1)} %get-tuple-element.112.r1_ref, bf16[1024,3072]{1,0:T(8,128)(2,1)S(1)} %get-tuple-element.113.act_ref, ...), custom_call_target="tpu_custom_call" | custom-call | flops 30799998976 | tf_op jit(solution)/shard_map/feed_out/pallas_call | solution.py:229
  137.9 17.3 %attend_back.1 = (bf16[1024,2304]{1,0:T(8,128)(2,1)S(1)}, bf16[16,1024]{1,0:T(8,128)(2,1)S(1)}, f32[16,768]{1,0:T(8,128)S(1)}, f32[16,768]{1,0:T(8,128)S(1)}) custom-call(s32[3]{0:T(128)S(1)} %pad_add_fusion.sc_ref, bf16[1024,2304]{1,0:T(8,128)(2,1)} %copy-done.8, bf16[1024,2304]{1,0:T(8,128)(2,1)} %copy-done.8, bf16[1024,2304]{1,0:T(8,128)(2,1)} %copy-done.8, ...), custom_call_target="tpu_custom_call" | custom-call | flops 19800000512 | tf_op jit(solution)/shard_map/attend_back/pallas_call | solution.py:319
  156.6 1.8 collective-permute-start.24
  160.1 1.6 collective-permute-done.24
  163.6 1.9 %collective-permute-start.27 = (f32[16,768]{1,0:T(8,128)S(1)}, f32[16,768]{1,0:T(8,128)S(1)}, u32[]{:S(2)}, u32[]{:S(2)}) collective-permute-start(f32[16,768]{1,0:T(8,128)S(1)} %add_add_fusion.1), channel_id=1, source_target_pairs={{0,24},{1,25},{2,26},{3,27},{4,28},{5,29},{6,30},{7,31},{8,16},{9,... | collective-permute-start | bytes 147464 | tf_op jit(solution)/shard_map/ppermute | solution.py:347
  165.5 2.5 %collective-permute-start.25 = (f32[16,768]{1,0:T(8,128)S(1)}, f32[16,768]{1,0:T(8,128)S(1)}, u32[]{:S(2)}, u32[]{:S(2)}) collective-permute-start(f32[16,768]{1,0:T(8,128)S(1)} %add_add_fusion.1), channel_id=1, source_target_pairs={{0,8},{1,9},{2,10},{3,11},{4,12},{5,13},{6,14},{7,15},{8,0},{9,1},... | collective-permute-start | bytes 147464 | tf_op jit(solution)/shard_map/ppermute | solution.py:347
  168.1 5.6 %inputs_grad.1 = f32[1024,768]{1,0:T(8,128)} custom-call(f32[1024,768]{1,0:T(8,128)S(1)} %copy-done.7, bf16[1024,2304]{1,0:T(8,128)(2,1)S(1)} %get-tuple-element.128.d_ref, bf16[16,1024]{1,0:T(8,128)(2,1)S(1)} %get-tuple-element.129.gl, bf16[768,2304]{1,0:T(8,128)(2,1)S(1)} %copy-done.6, bf16[16,768]{1,0:T(8,128)(2,1)S(1)} %get-tuple-element.131.dnt_ref), custom_call_target="tpu_custom_call" | custom-call | flops 7699999744 | tf_op jit(solution)/shard_map/inputs_grad/pallas_call | solution.py:337
  173.8 1.2 collective-permute-done.28.other_ref
  (142 shorter events, 13.6 us)
Async XLA Ops:
  4.0 12.3 %collective-permute-start.2 = (bf16[144,384]{1,0:T(8,128)(2,1)S(1)}, bf16[144,384]{1,0:T(8,128)(2,1)S(1)}, u32[]{:S(2)}, u32[]{:S(2)}) collective-permute-start(bf16[144,384]{1,0:T(8,128)(2,1)S(1)} %pad_maximum_fusion.4), channel_id=1, source_target_pairs={{0,24},{1,25},{2,26},{3,27},{4,28},{5,29},{6,30},{7,31},{8,16},{9,... | collective-permute-start | bytes 331784 | tf_op jit(solution)/shard_map/ppermute | solution.py:347
  9.0 9.6 %collective-permute-start.1 = (bf16[144,384]{1,0:T(8,128)(2,1)S(1)}, bf16[144,384]{1,0:T(8,128)(2,1)S(1)}, u32[]{:S(2)}, u32[]{:S(2)}) collective-permute-start(bf16[144,384]{1,0:T(8,128)(2,1)S(1)} %pad_maximum_fusion.4), channel_id=1, source_target_pairs={{0,16},{1,17},{2,18},{3,19},{4,20},{5,21},{6,22},{7,23},{8,24},{9,... | collective-permute-start | bytes 331784 | tf_op jit(solution)/shard_map/ppermute | solution.py:347
  9.0 9.6 %collective-permute-start = (bf16[144,384]{1,0:T(8,128)(2,1)S(1)}, bf16[144,384]{1,0:T(8,128)(2,1)S(1)}, u32[]{:S(2)}, u32[]{:S(2)}) collective-permute-start(bf16[144,384]{1,0:T(8,128)(2,1)S(1)} %pad_maximum_fusion.4), channel_id=1, source_target_pairs={{0,8},{1,9},{2,10},{3,11},{4,12},{5,13},{6,14},{7,15},{8,0},{9,1},... | collective-permute-start | bytes 331784 | tf_op jit(solution)/shard_map/ppermute | solution.py:347
  18.6 10.5 %collective-permute-start.4 = (bf16[240,384]{1,0:T(8,128)(2,1)S(1)}, bf16[240,384]{1,0:T(8,128)(2,1)S(1)}, u32[]{:S(2)}, u32[]{:S(2)}) collective-permute-start(bf16[240,384]{1,0:T(8,128)(2,1)S(1)} %constant_dynamic-update-slice_fusion), channel_id=1, source_target_pairs={{0,16},{1,17},{2,18},{3,19},{4,20},{5,21},{6,22},{7,23},{8,24},{9,... | collective-permute-start | bytes 552968 | tf_op jit(solution)/shard_map/ppermute | solution.py:347
  18.8 10.4 %collective-permute-start.3 = (bf16[4,144,384]{2,1,0:T(8,128)(2,1)S(1)}, bf16[4,144,384]{2,1,0:T(8,128)(2,1)S(1)}, u32[]{:S(2)}, u32[]{:S(2)}) collective-permute-start(bf16[4,144,384]{2,1,0:T(8,128)(2,1)S(1)} %pad_maximum_fusion.2), channel_id=1, source_target_pairs={{0,2},{1,5},{2,0},{3,7},{4,6},{5,1},{6,4},{7,3},{8,10},{9,13},{10,... | collective-permute-start | bytes 1327112 | tf_op jit(solution)/shard_map/ppermute | solution.py:347
  29.3 12.7 %collective-permute-start.6 = (bf16[8,144,384]{2,1,0:T(8,128)(2,1)S(1)}, bf16[8,144,384]{2,1,0:T(8,128)(2,1)S(1)}, u32[]{:S(2)}, u32[]{:S(2)}) collective-permute-start(bf16[8,144,384]{2,1,0:T(8,128)(2,1)S(1)} %constant_dynamic-update-slice_fusion.5.rest_0_), channel_id=1, source_target_pairs={{0,1},{1,0},{2,3},{3,2},{4,5},{5,4},{6,7},{7,6},{8,9},{9,8},{10,11... | collective-permute-start | bytes 2654216 | tf_op jit(solution)/shard_map/ppermute | solution.py:347
  29.3 13.1 %collective-permute-start.5 = (bf16[8,144,384]{2,1,0:T(8,128)(2,1)S(1)}, bf16[8,144,384]{2,1,0:T(8,128)(2,1)S(1)}, u32[]{:S(2)}, u32[]{:S(2)}) collective-permute-start(bf16[8,144,384]{2,1,0:T(8,128)(2,1)S(1)} %constant_dynamic-update-slice_fusion.5.rest_0_), channel_id=1, source_target_pairs={{0,4},{1,3},{2,6},{3,1},{4,0},{5,7},{6,2},{7,5},{8,12},{9,11},{10,... | collective-permute-start | bytes 2654216 | tf_op jit(solution)/shard_map/ppermute | solution.py:347
  30.9 7.2 %collective-permute-start.8 = (bf16[240,384]{1,0:T(8,128)(2,1)S(1)}, bf16[240,384]{1,0:T(8,128)(2,1)S(1)}, u32[]{:S(2)}, u32[]{:S(2)}) collective-permute-start(bf16[240,384]{1,0:T(8,128)(2,1)S(1)} %constant_dynamic-update-slice_fusion), channel_id=1, source_target_pairs={{0,8},{1,9},{2,10},{3,11},{4,12},{5,13},{6,14},{7,15},{8,0},{9,1},... | collective-permute-start | bytes 552968 | tf_op jit(solution)/shard_map/ppermute | solution.py:347
  31.9 10.0 %collective-permute-start.7 = (bf16[240,384]{1,0:T(8,128)(2,1)S(1)}, bf16[240,384]{1,0:T(8,128)(2,1)S(1)}, u32[]{:S(2)}, u32[]{:S(2)}) collective-permute-start(bf16[240,384]{1,0:T(8,128)(2,1)S(1)} %constant_dynamic-update-slice_fusion), channel_id=1, source_target_pairs={{0,24},{1,25},{2,26},{3,27},{4,28},{5,29},{6,30},{7,31},{8,16},{9,... | collective-permute-start | bytes 552968 | tf_op jit(solution)/shard_map/ppermute | solution.py:347
  42.5 6.3 %collective-permute-start.10 = (bf16[8,144,384]{2,1,0:T(8,128)(2,1)S(1)}, bf16[8,144,384]{2,1,0:T(8,128)(2,1)S(1)}, u32[]{:S(2)}, u32[]{:S(2)}) collective-permute-start(bf16[8,144,384]{2,1,0:T(8,128)(2,1)S(1)} %collective-permute-done.5.rest_1_), channel_id=1, source_target_pairs={{0,1},{1,0},{2,3},{3,2},{4,5},{5,4},{6,7},{7,6},{8,9},{9,8},{10,11... | collective-permute-start | bytes 2654216 | tf_op jit(solution)/shard_map/ppermute | solution.py:347
  42.5 16.2 %collective-permute-start.13 = (bf16[192,384]{1,0:T(8,128)(2,1)S(1)}, bf16[192,384]{1,0:T(8,128)(2,1)S(1)}, u32[]{:S(2)}, u32[]{:S(2)}) collective-permute-start(bf16[192,384]{1,0:T(8,128)(2,1)S(1)} %bitcast.44), channel_id=1, source_target_pairs={{0,24},{1,25},{2,26},{3,27},{4,28},{5,29},{6,30},{7,31},{8,16},{9,... | collective-permute-start | bytes 442376 | tf_op jit(solution)/shard_map/ppermute | solution.py:347
  44.6 14.1 %collective-permute-start.12 = (bf16[192,384]{1,0:T(8,128)(2,1)S(1)}, bf16[192,384]{1,0:T(8,128)(2,1)S(1)}, u32[]{:S(2)}, u32[]{:S(2)}) collective-permute-start(bf16[192,384]{1,0:T(8,128)(2,1)S(1)} %bitcast.45), channel_id=1, source_target_pairs={{0,16},{1,17},{2,18},{3,19},{4,20},{5,21},{6,22},{7,23},{8,24},{9,... | collective-permute-start | bytes 442376 | tf_op jit(solution)/shard_map/ppermute | solution.py:347
  45.0 13.8 %collective-permute-start.11 = (bf16[192,384]{1,0:T(8,128)(2,1)S(1)}, bf16[192,384]{1,0:T(8,128)(2,1)S(1)}, u32[]{:S(2)}, u32[]{:S(2)}) collective-permute-start(bf16[192,384]{1,0:T(8,128)(2,1)S(1)} %bitcast.46), channel_id=1, source_target_pairs={{0,8},{1,9},{2,10},{3,11},{4,12},{5,13},{6,14},{7,15},{8,0},{9,1},... | collective-permute-start | bytes 442376 | tf_op jit(solution)/shard_map/ppermute | solution.py:347
  47.1 11.7 %collective-permute-start.9 = (bf16[4,240,384]{2,1,0:T(8,128)(2,1)S(1)}, bf16[4,240,384]{2,1,0:T(8,128)(2,1)S(1)}, u32[]{:S(2)}, u32[]{:S(2)}) collective-permute-start(bf16[4,240,384]{2,1,0:T(8,128)(2,1)S(1)} %pad_maximum_fusion), channel_id=1, source_target_pairs={{0,2},{1,5},{2,0},{3,7},{4,6},{5,1},{6,4},{7,3},{8,10},{9,13},{10,... | collective-permute-start | bytes 2211848 | tf_op jit(solution)/shard_map/ppermute | solution.py:347
  58.9 17.4 %collective-permute-start.16 = (bf16[8,240,384]{2,1,0:T(8,128)(2,1)S(1)}, bf16[8,240,384]{2,1,0:T(8,128)(2,1)S(1)}, u32[]{:S(2)}, u32[]{:S(2)}) collective-permute-start(bf16[8,240,384]{2,1,0:T(8,128)(2,1)S(1)} %constant_dynamic-update-slice_fusion.10.rest_0_), channel_id=1, source_target_pairs={{0,1},{1,0},{2,3},{3,2},{4,5},{5,4},{6,7},{7,6},{8,9},{9,8},{10,11... | collective-permute-start | bytes 4423688 | tf_op jit(solution)/shard_map/ppermute | solution.py:347
  59.0 19.4 %collective-permute-start.15 = (bf16[8,240,384]{2,1,0:T(8,128)(2,1)S(1)}, bf16[8,240,384]{2,1,0:T(8,128)(2,1)S(1)}, u32[]{:S(2)}, u32[]{:S(2)}) collective-permute-start(bf16[8,240,384]{2,1,0:T(8,128)(2,1)S(1)} %constant_dynamic-update-slice_fusion.10.rest_0_), channel_id=1, source_target_pairs={{0,4},{1,3},{2,6},{3,1},{4,0},{5,7},{6,2},{7,5},{8,12},{9,11},{10,... | collective-permute-start | bytes 4423688 | tf_op jit(solution)/shard_map/ppermute | solution.py:347
  78.4 10.1 %collective-permute-start.17 = (bf16[8,240,384]{2,1,0:T(8,128)(2,1)S(1)}, bf16[8,240,384]{2,1,0:T(8,128)(2,1)S(1)}, u32[]{:S(2)}, u32[]{:S(2)}) collective-permute-start(bf16[8,240,384]{2,1,0:T(8,128)(2,1)S(1)} %collective-permute-done.15.rest_1_), channel_id=1, source_target_pairs={{0,1},{1,0},{2,3},{3,2},{4,5},{5,4},{6,7},{7,6},{8,9},{9,8},{10,11... | collective-permute-start | bytes 4423688 | tf_op jit(solution)/shard_map/ppermute | solution.py:347
  78.5 9.9 %collective-permute-start.14 = (bf16[4,192,384]{2,1,0:T(8,128)(2,1)S(1)}, bf16[4,192,384]{2,1,0:T(8,128)(2,1)S(1)}, u32[]{:S(2)}, u32[]{:S(2)}) collective-permute-start(bf16[4,192,384]{2,1,0:T(8,128)(2,1)S(1)} %pad_maximum_fusion.1), channel_id=1, source_target_pairs={{0,2},{1,5},{2,0},{3,7},{4,6},{5,1},{6,4},{7,3},{8,10},{9,13},{10,... | collective-permute-start | bytes 1769480 | tf_op jit(solution)/shard_map/ppermute | solution.py:347
  88.6 18.8 %collective-permute-start.19 = (bf16[8,192,384]{2,1,0:T(8,128)(2,1)S(1)}, bf16[8,192,384]{2,1,0:T(8,128)(2,1)S(1)}, u32[]{:S(2)}, u32[]{:S(2)}) collective-permute-start(bf16[8,192,384]{2,1,0:T(8,128)(2,1)S(1)} %constant_dynamic-update-slice_fusion.15.rest_0_), channel_id=1, source_target_pairs={{0,1},{1,0},{2,3},{3,2},{4,5},{5,4},{6,7},{7,6},{8,9},{9,8},{10,11... | collective-permute-start | bytes 3538952 | tf_op jit(solution)/shard_map/ppermute | solution.py:347
  88.7 18.8 %collective-permute-start.18 = (bf16[8,192,384]{2,1,0:T(8,128)(2,1)S(1)}, bf16[8,192,384]{2,1,0:T(8,128)(2,1)S(1)}, u32[]{:S(2)}, u32[]{:S(2)}) collective-permute-start(bf16[8,192,384]{2,1,0:T(8,128)(2,1)S(1)} %constant_dynamic-update-slice_fusion.15.rest_0_), channel_id=1, source_target_pairs={{0,4},{1,3},{2,6},{3,1},{4,0},{5,7},{6,2},{7,5},{8,12},{9,11},{10,... | collective-permute-start | bytes 3538952 | tf_op jit(solution)/shard_map/ppermute | solution.py:347
  107.5 2.9 %collective-permute-start.20 = (bf16[8,192,384]{2,1,0:T(8,128)(2,1)S(1)}, bf16[8,192,384]{2,1,0:T(8,128)(2,1)S(1)}, u32[]{:S(2)}, u32[]{:S(2)}) collective-permute-start(bf16[8,192,384]{2,1,0:T(8,128)(2,1)S(1)} %collective-permute-done.18.rest_1_), channel_id=1, source_target_pairs={{0,1},{1,0},{2,3},{3,2},{4,5},{5,4},{6,7},{7,6},{8,9},{9,8},{10,11... | collective-permute-start | bytes 3538952 | tf_op jit(solution)/shard_map/ppermute | solution.py:347
  111.4 26.5 %copy-start.9 = (f32[6,8,512]{2,1,0:T(8,128)S(1)}, f32[6,8,512]{2,1,0:T(8,128)}, u32[]{:S(2)}) copy-start(f32[6,8,512]{2,1,0:T(8,128)} %get-tuple-element.122.rt_ref) | copy-start | bytes 294916
  137.9 30.1 %copy-start.6 = (bf16[768,2304]{1,0:T(8,128)(2,1)S(1)}, bf16[768,2304]{1,0:T(8,128)(2,1)}, u32[]{:S(2)}) copy-start(bf16[768,2304]{1,0:T(8,128)(2,1)} %get-tuple-element.130.w_ref) | copy-start | bytes 10616836
  137.9 30.1 %copy-start.7 = (f32[1024,768]{1,0:T(8,128)S(1)}, f32[1024,768]{1,0:T(8,128)}, u32[]{:S(2)}) copy-start(f32[1024,768]{1,0:T(8,128)} %get-tuple-element.127.gfs_ref) | copy-start | bytes 9437188
  155.2 1.3 collective-permute-start.21
  156.6 5.2 %collective-permute-start.24 = (f32[16,768]{1,0:T(8,128)S(1)}, f32[16,768]{1,0:T(8,128)S(1)}, u32[]{:S(2)}, u32[]{:S(2)}) collective-permute-start(f32[16,768]{1,0:T(8,128)S(1)} %add.63), channel_id=1, source_target_pairs={{0,6},{1,7},{2,4},{3,5},{4,2},{5,3},{6,0},{7,1},{8,14},{9,15},{10,... | collective-permute-start | bytes 147464 | tf_op jit(solution)/shard_map/ppermute | solution.py:347
  158.3 4.1 %collective-permute-start.23 = (f32[16,768]{1,0:T(8,128)S(1)}, f32[16,768]{1,0:T(8,128)S(1)}, u32[]{:S(2)}, u32[]{:S(2)}) collective-permute-start(f32[16,768]{1,0:T(8,128)S(1)} %add.63), channel_id=1, source_target_pairs={{0,4},{1,5},{2,6},{3,7},{4,0},{5,1},{6,2},{7,3},{8,12},{9,13},{10,... | collective-permute-start | bytes 147464 | tf_op jit(solution)/shard_map/ppermute | solution.py:347
  159.5 4.1 %collective-permute-start.22 = (f32[16,768]{1,0:T(8,128)S(1)}, f32[16,768]{1,0:T(8,128)S(1)}, u32[]{:S(2)}, u32[]{:S(2)}) collective-permute-start(f32[16,768]{1,0:T(8,128)S(1)} %add.63), channel_id=1, source_target_pairs={{0,2},{1,3},{2,0},{3,1},{4,6},{5,7},{6,4},{7,5},{8,10},{9,11},{10,... | collective-permute-start | bytes 147464 | tf_op jit(solution)/shard_map/ppermute | solution.py:347
  163.6 10.1 %collective-permute-start.27 = (f32[16,768]{1,0:T(8,128)S(1)}, f32[16,768]{1,0:T(8,128)S(1)}, u32[]{:S(2)}, u32[]{:S(2)}) collective-permute-start(f32[16,768]{1,0:T(8,128)S(1)} %add_add_fusion.1), channel_id=1, source_target_pairs={{0,24},{1,25},{2,26},{3,27},{4,28},{5,29},{6,30},{7,31},{8,16},{9,... | collective-permute-start | bytes 147464 | tf_op jit(solution)/shard_map/ppermute | solution.py:347
  165.5 8.2 %collective-permute-start.26 = (f32[16,768]{1,0:T(8,128)S(1)}, f32[16,768]{1,0:T(8,128)S(1)}, u32[]{:S(2)}, u32[]{:S(2)}) collective-permute-start(f32[16,768]{1,0:T(8,128)S(1)} %add_add_fusion.1), channel_id=1, source_target_pairs={{0,16},{1,17},{2,18},{3,19},{4,20},{5,21},{6,22},{7,23},{8,24},{9,... | collective-permute-start | bytes 147464 | tf_op jit(solution)/shard_map/ppermute | solution.py:347
  165.5 8.2 %collective-permute-start.25 = (f32[16,768]{1,0:T(8,128)S(1)}, f32[16,768]{1,0:T(8,128)S(1)}, u32[]{:S(2)}, u32[]{:S(2)}) collective-permute-start(f32[16,768]{1,0:T(8,128)S(1)} %add_add_fusion.1), channel_id=1, source_target_pairs={{0,8},{1,9},{2,10},{3,11},{4,12},{5,13},{6,14},{7,15},{8,0},{9,1},... | collective-permute-start | bytes 147464 | tf_op jit(solution)/shard_map/ppermute | solution.py:347
  173.7 1.3 collective-permute-start.28
  (27 other events, 286.9 us)

commit v3 on v2

--- a/solution.py
+++ b/solution.py
@@ -30,7 +30,7 @@
     return pltpu.with_memory_space_constraint(v,pltpu.HBM)
 
 
-def block_copies(layout,me,bufs,outs,sems):
+def block_copies(layout,me,bufs,outs,sems,near_inside=False):
     if layout is None:
         return [[pltpu.make_async_copy(b,o,sems.at[t])] for t,(b,o) in enumerate(zip(bufs,outs))]
     first,second,other_first,other_second=bufs
@@ -53,7 +53,8 @@
         far_axis=2-origin
         for hop,buf in enumerate((near,far)):
             for i in range(8):
-                add(layout,buf,i,origin,hop*far_axis+(i//4)*near_axis+4*(i%4))
+                n,z=(i%2,i//2) if near_inside else (i//4,i%4)
+                add(layout,buf,i,origin,hop*far_axis+n*near_axis+4*z)
     return lists
 
 def start_all(copies):
@@ -109,7 +110,7 @@
         out_specs=[HELD,pl.BlockSpec((32,SLOT),lambda i:(0,i)),ANY],
         out_shape=[sd((rows,3*D),BF),sd((32,rows),BF),pltpu.HBM((D,3*D),BF)],
         scratch_shapes=[pltpu.VMEM((D,3*D),BF),pltpu.SemaphoreType.DMA((copy_count(layout),)),pltpu.SemaphoreType.DMA((1,))],
-        compiler_params=params(LIM["project"]),cost_estimate=takes(8),name="project")(scalars,x,dn,upq,upv,*map(far,blocks))
+        compiler_params=params(LIM["project"]),cost_estimate=takes(8),name="project")(scalars,x,dn,upq,upv,*blocks)
 
 def attend_kernel(sc_ref,qkv_ref,e_ref,ot_ref,o_ref,rt_ref):
     s=pl.program_id(0); j=pl.program_id(1); J=pl.num_programs(1); D=256*J
@@ -169,7 +170,7 @@
 
 CH=512
 TILE=256
-LIM={"project":20,"attend":24,"feed_in":16,"feed_out":24,"attend_back":24,"inputs_grad":24}
+LIM={"project":8,"attend":10,"feed_in":6,"feed_out":14,"attend_back":10,"inputs_grad":6}
 
 def feed_in_kernel(layout,sc_ref,x_ref,o_ref,nm_ref,*rest):
     *blocks,n1_ref,r1_ref,act_ref,gp_ref,wo,wi,sems=rest
@@ -198,14 +199,14 @@
         out_specs=[HELD]*6,
         out_shape=[pltpu.VMEM((rows,D),F32),pltpu.VMEM((rows,128),F32),pltpu.VMEM((rows,FF),BF),pltpu.VMEM((rows,FF),BF),pltpu.VMEM((D,D),BF),pltpu.VMEM((D,FF),BF)],
         scratch_shapes=[pltpu.SemaphoreType.DMA((copy_count(layout),))],
-        compiler_params=params(LIM["feed_in"]),cost_estimate=takes(17),name="feed_in")(scalars,x,o,nm,*map(far,blocks))
+        compiler_params=params(LIM["feed_in"]),cost_estimate=takes(17),name="feed_in")(scalars,x,o,nm,*blocks)
 
 def feed_out_kernel(layout,sc_ref,n1_ref,r1_ref,act_ref,gp_ref,go_ref,nm_ref,wo,wi,*rest):
     *blocks,out_ref,gfs_ref,gmt_ref,wt,gi_ref,sems=rest
     i=pl.program_id(0)
     @pl.when(i==0)
     def _():
-        copies,=block_copies(layout,sc_ref[0],blocks,(wt,),sems)
+        copies,=block_copies(layout,sc_ref[0],blocks,(wt,),sems,True)
         start_all(copies); wait_all(copies)
     T=go_ref.shape[0]
     rows=pl.ds(pl.multiple_of(i*T,T),T)
@@ -231,7 +232,7 @@
         out_specs=[row,row,HELD],
         out_shape=[sd((rows,D),BF),pltpu.HBM((rows,D),F32),pltpu.VMEM((D,rows),BF)],
         scratch_shapes=[pltpu.VMEM((FF,D),BF),pltpu.VMEM((TILE,FF),BF),pltpu.SemaphoreType.DMA((copy_count(layout),))],
-        compiler_params=params(LIM["feed_out"]),cost_estimate=takes(28),name="feed_out")(scalars,n1,r1,act,gp,go,nm,wo,wi,*map(far,blocks))
+        compiler_params=params(LIM["feed_out"]),cost_estimate=takes(28),name="feed_out")(scalars,n1,r1,act,gp,go,nm,wo,wi,*blocks)
 
 
 def attend_back_kernel(sc_ref,q_ref,k_ref,v_ref,e_ref,ot_ref,rt_ref,gmt_ref,x_ref,low_ref,upq_ref,upv_ref,
@@ -404,32 +405,31 @@
     s2=jnp.concatenate([column_half(bo)]+[column_half(bi[:,:,D*t:D*t+D]) for t in range(bands)],0)
     s3=column_half(bt)
     dn,upq,upv,dnt,nm=prep(qd,qu,vd,vu,ag,ash,fg,fsh)
-    z1,s2,s3,dn,scalars=tie(z1,s2,s3,dn,scalars)
+    n3=near_hop(s3)
+    z1,s2,dn,scalars=tie(z1,s2,dn,scalars)
     a1=jnp.stack(z1,0)
     n1=near_hop(a1)
     z22=exchange(s2,2*top)
-    n1,z22,s2=tie(n1,z22,s2)
+    n1,z22,s2,n3=tie(n1,z22,s2,n3)
     f1=jnp.concatenate([a1,n1],0)
     h1=far_hop(f1); of1=exchange(f1,1)
     z23=exchange(s2,3*top); z21=exchange(s2,top)
-    h1,of1,z23,z21,s3=tie(h1,of1,z23,z21,s3)
+    h1,of1,z23,z21,n3=tie(h1,of1,z23,z21,n3)
     oh1=exchange(h1,1)
     a2=jnp.stack([s2,z21,z22,z23],0)
     n2=near_hop(a2)
-    z31,z32,z33=(exchange(s3,m*top) for m in (1,2,3))
+    z3=along_z(jnp.stack([s3,n3],0))
     oh1,=tie(oh1)
     qkv,low,wqkv=project(scalars,x,dn,upq,upv,(f1,h1,of1,oh1),((3,2*r,0,2*r),))
-    n2,qkv,z31,z32,z33,s3=tie(n2,qkv,z31,z32,z33,s3)
+    n2,qkv=tie(n2,qkv)
     f2=jnp.concatenate([a2,n2],0)
     h2=far_hop(f2); of2=exchange(f2,1)
-    a3=jnp.stack([s3,z31,z32,z33],0)
-    n3=near_hop(a3)
     e,ot,o,rt=attend(scalars,qkv,x.shape[0]//SLOT)
-    h2,o,of2=tie(h2,o,of2)
+    h2,o,of2,z3=tie(h2,o,of2,z3)
     oh2=exchange(h2,1)
-    n3,oh2=tie(n3,oh2)
-    f3=jnp.concatenate([a3,n3],0)
+    f3=jnp.concatenate(z3,0)
     h3=far_hop(f3); of3=exchange(f3,1)
+    oh2,=tie(oh2)
     nn,r1,act,gp,wo,wi=feed_in(scalars,x,o,nm,(f2,h2,of2,oh2),((1,2*r,0,2*r),(bands,2*r,0,2*r)),FF)
     h3,nn,of3=tie(h3,nn,of3)
     oh3=exchange(h3,1)

time: 177 us -> 165 us (0.932)
  waiting for transfers between devices: 39.4 us -> 31 us
  Pallas kernels: 92.6 us -> 90 us
  local copies, waits for them, and re-layouts: 2.89 us -> 0.87 us
    ppermute x29, waiting for transfers between devices: 39.4 us -> 31 us  [permute(): lax.ppermute(v, AXES, [(i, target(i)) for i in range(device_count())])]
    unnamed x76 -> x51, local copies, waits for them, and re-layouts: 2.41 us -> 0.44 us
  transfers between devices with their start and end apart: 29 -> 29, of which waited for: 13 -> 13; matrix products, arithmetic and copies ran while one was open for 1% -> 1% of each run, Pallas kernels for 27% -> 28%
where the time goes in v3:
time: 165 us; the launch traced here: 164 us
  Pallas kernels  90 us (55%)
  starting transfers between devices  31.9 us (19%)
  waiting for transfers between devices  31 us (19%)
  blocking collectives  7.94 us (5%)
    ppermute x29, starting transfers between devices, permute(): lax.ppermute(v, AXES, [(i, target(i)) for i in range(device_count())])  31.9 us
    ppermute x29, waiting for transfers between devices, permute(): lax.ppermute(v, AXES, [(i, target(i)) for i in range(device_count())])  31 us
    pallas_call x1, Pallas kernels, feed_out(): pl.pallas_call(functools.partial(feed_out_kernel, layout), grid=(rows //...  25 us
    pallas_call x1, Pallas kernels, attend_back(): pl.pallas_call(attend_back_kernel, grid=(S, J), in_specs=[SCALARS, *[pl.B...  17.3 us
    pallas_call x1, Pallas kernels, feed_in(): pl.pallas_call(functools.partial(feed_in_kernel, layout), grid=(rows // T...  16.6 us
    pallas_call x1, Pallas kernels, attend(): pl.pallas_call(attend_kernel, grid=(slots, J), in_specs=[SCALARS, HELD],...  15.8 us
    pallas_call x1, Pallas kernels, project(): pl.pallas_call(functools.partial(project_kernel, layout), grid=(rows // S...  8.37 us
    all_gather x4, blocking collectives, core_pair(): lax.all_gather(v, 'fsdp', axis=0, tiled=False, axis_index_groups=groups)  7.94 us
  transfers between devices with their start and end apart: 29, of which 13 were waited for; matrix products, arithmetic and copies ran while one was open for 1% of the time, Pallas kernels for 28%

profile of v3, /device:TPU:0, one launch (start us, length us, event | category | flops | bytes accessed | tf_op | source)
XLA Modules:
  0.0 164.5 jit_solution(5332102860197369847)
XLA Ops:
  1.7 2.1 %all-gather = bf16[144,768]{1,0:T(8,128)(2,1)S(1)} all-gather(bf16[72,768]{1,0:T(8,128)(2,1)S(1)} %pad_maximum_fusion.3), channel_id=2, replica_groups={{0,1},{2,3},{4,5},{6,7},{8,9},{10,11},{12,13},{14,15},{16,17},{18,19},{..., dimensions={0}, use_global_device_ids=true | all-gather | bytes 331776 | tf_op jit(solution)/shard_map/all_gather | solution.py:365
  3.9 5.0 %collective-permute-start.2 = (bf16[144,384]{1,0:T(8,128)(2,1)S(1)}, bf16[144,384]{1,0:T(8,128)(2,1)S(1)}, u32[]{:S(2)}, u32[]{:S(2)}) collective-permute-start(bf16[144,384]{1,0:T(8,128)(2,1)S(1)} %pad_maximum_fusion.4), channel_id=1, source_target_pairs={{0,24},{1,25},{2,26},{3,27},{4,28},{5,29},{6,30},{7,31},{8,16},{9,... | collective-permute-start | bytes 331784 | tf_op jit(solution)/shard_map/ppermute | solution.py:348
  9.5 2.0 %all-gather.3 = bf16[192,768]{1,0:T(8,128)(2,1)S(1)} all-gather(bf16[96,768]{1,0:T(8,128)(2,1)S(1)} %copy-done.10), channel_id=5, replica_groups={{0,1},{2,3},{4,5},{6,7},{8,9},{10,11},{12,13},{14,15},{16,17},{18,19},{..., dimensions={0}, use_global_device_ids=true | all-gather | bytes 442368 | tf_op jit(solution)/shard_map/all_gather | solution.py:365
  11.6 1.7 %collective-permute-start.5 = (bf16[192,384]{1,0:T(8,128)(2,1)S(1)}, bf16[192,384]{1,0:T(8,128)(2,1)S(1)}, u32[]{:S(2)}, u32[]{:S(2)}) collective-permute-start(bf16[192,384]{1,0:T(8,128)(2,1)S(1)} %bitcast.46), channel_id=1, source_target_pairs={{0,2},{1,5},{2,0},{3,7},{4,6},{5,1},{6,4},{7,3},{8,10},{9,13},{10,... | collective-permute-start | bytes 442376 | tf_op jit(solution)/shard_map/ppermute | solution.py:348
  13.6 1.9 %all-gather.1 = bf16[48,768]{1,0:T(8,128)(2,1)S(1)} all-gather(bf16[24,768]{1,0:T(8,128)(2,1)S(1)} %copy-done.12), channel_id=3, replica_groups={{0,1},{2,3},{4,5},{6,7},{8,9},{10,11},{12,13},{14,15},{16,17},{18,19},{..., dimensions={0}, use_global_device_ids=true | all-gather | bytes 110592 | tf_op jit(solution)/shard_map/all_gather | solution.py:365
  15.4 2.0 %all-gather.2 = bf16[48,3072]{1,0:T(8,128)(2,1)S(1)} all-gather(bf16[24,3072]{1,0:T(8,128)(2,1)S(1)} %copy-done.11), channel_id=4, replica_groups={{0,1},{2,3},{4,5},{6,7},{8,9},{10,11},{12,13},{14,15},{16,17},{18,19},{..., dimensions={0}, use_global_device_ids=true | all-gather | bytes 442368 | tf_op jit(solution)/shard_map/all_gather | solution.py:365
  18.5 1.6 collective-permute-start.4
  21.4 8.1 %collective-permute-done.4 = bf16[240,384]{1,0:T(8,128)(2,1)S(1)} collective-permute-done((bf16[240,384]{1,0:T(8,128)(2,1)S(1)}, bf16[240,384]{1,0:T(8,128)(2,1)S(1)}, u32[]{:S(2)}, u32[]{:S(2)}) %collective-permute-start.4) | collective-permute-done | bytes 184352 | tf_op jit(solution)/shard_map/ppermute | solution.py:348
  29.7 1.6 collective-permute-start.6
  32.3 2.0 %collective-permute-start.8 = (bf16[240,384]{1,0:T(8,128)(2,1)S(1)}, bf16[240,384]{1,0:T(8,128)(2,1)S(1)}, u32[]{:S(2)}, u32[]{:S(2)}) collective-permute-start(bf16[240,384]{1,0:T(8,128)(2,1)S(1)} %constant_dynamic-update-slice_fusion), channel_id=1, source_target_pairs={{0,24},{1,25},{2,26},{3,27},{4,28},{5,29},{6,30},{7,31},{8,16},{9,... | collective-permute-start | bytes 552968 | tf_op jit(solution)/shard_map/ppermute | solution.py:348
  34.3 3.3 %collective-permute-done.9 = bf16[240,384]{1,0:T(8,128)(2,1)S(1)} collective-permute-done((bf16[240,384]{1,0:T(8,128)(2,1)S(1)}, bf16[240,384]{1,0:T(8,128)(2,1)S(1)}, u32[]{:S(2)}, u32[]{:S(2)}) %collective-permute-start.9) | collective-permute-done | bytes 184352 | tf_op jit(solution)/shard_map/ppermute | solution.py:348
  37.7 5.4 %collective-permute-done.8 = bf16[240,384]{1,0:T(8,128)(2,1)S(1)} collective-permute-done((bf16[240,384]{1,0:T(8,128)(2,1)S(1)}, bf16[240,384]{1,0:T(8,128)(2,1)S(1)}, u32[]{:S(2)}, u32[]{:S(2)}) %collective-permute-start.8) | collective-permute-done | bytes 184352 | tf_op jit(solution)/shard_map/ppermute | solution.py:348
  43.1 2.8 %collective-permute-start.16 = (bf16[2,192,384]{2,1,0:T(8,128)(2,1)S(1)}, bf16[2,192,384]{2,1,0:T(8,128)(2,1)S(1)}, u32[]{:S(2)}, u32[]{:S(2)}) collective-permute-start(bf16[2,192,384]{2,1,0:T(8,128)(2,1)S(1)} %pad_maximum_fusion.2), channel_id=1, source_target_pairs={{0,24},{1,25},{2,26},{3,27},{4,28},{5,29},{6,30},{7,31},{8,16},{9,... | collective-permute-start | bytes 884744 | tf_op jit(solution)/shard_map/ppermute | solution.py:348
  45.9 1.6 collective-permute-start.14
  48.8 8.4 %project.1 = (bf16[1024,2304]{1,0:T(8,128)(2,1)S(1)}, bf16[32,1024]{1,0:T(8,128)(2,1)S(1)}, bf16[768,2304]{1,0:T(8,128)(2,1)}) custom-call(s32[3]{0:T(128)S(1)} %pad_add_fusion.sc_ref, bf16[1024,768]{1,0:T(8,128)(2,1)S(1)} %copy-done.1, bf16[768,128]{1,0:T(8,128)(2,1)S(1)} %get-tuple-element.88.dn_ref, bf16[128,768]{1,0:T(8,128)(2,1)S(1)} %get-tuple-element.89.upq_ref, ...), custom_call_target="tpu_custom_call" | custom-call | flops 8800000000 | tf_op jit(solution)/shard_map/project/pallas_call | solution.py:108
  57.2 2.0 %collective-permute-done.10 = bf16[4,240,384]{2,1,0:T(8,128)(2,1)S(1)} collective-permute-done((bf16[4,240,384]{2,1,0:T(8,128)(2,1)S(1)}, bf16[4,240,384]{2,1,0:T(8,128)(2,1)S(1)}, u32[]{:S(2)}, u32[]{:S(2)}) %collective-permute-start.10) | collective-permute-done | bytes 737312 | tf_op jit(solution)/shard_map/ppermute | solution.py:348
  59.4 1.3 collective-permute-start.12
  60.7 15.8 %attend.1 = (bf16[24,512,512]{2,1,0:T(8,128)(2,1)}, bf16[1536,512]{1,0:T(8,128)(2,1)}, bf16[1024,768]{1,0:T(8,128)(2,1)S(1)}, f32[6,8,512]{2,1,0:T(8,128)}) custom-call(s32[3]{0:T(128)S(1)} %pad_add_fusion.sc_ref, bf16[1024,2304]{1,0:T(8,128)(2,1)S(1)} %get-tuple-element.95.qkv_ref.q_ref.k_ref.v_ref), custom_call_target="tpu_custom_call" | custom-call | flops 17600000000 | tf_op jit(solution)/shard_map/attend/pallas_call | solution.py:151
  76.6 2.3 %collective-permute-done.12.rest_1_ = bf16[8,240,384]{2,1,0:T(8,128)(2,1)S(1)} collective-permute-done((bf16[8,240,384]{2,1,0:T(8,128)(2,1)S(1)}, bf16[8,240,384]{2,1,0:T(8,128)(2,1)S(1)}, u32[]{:S(2)}, u32[]{:S(2)}) %collective-permute-start.12) | collective-permute-done | bytes 1474592 | tf_op jit(solution)/shard_map/ppermute | solution.py:348
  79.6 1.3 collective-permute-start.17
  80.9 1.2 collective-permute-done.18.rest_3_
  82.1 16.6 %feed_in.1 = (f32[1024,768]{1,0:T(8,128)S(1)}, f32[1024,128]{1,0:T(8,128)S(1)}, bf16[1024,3072]{1,0:T(8,128)(2,1)S(1)}, bf16[1024,3072]{1,0:T(8,128)(2,1)S(1)}, ...) custom-call(s32[3]{0:T(128)S(1)} %pad_add_fusion.sc_ref, bf16[1024,768]{1,0:T(8,128)(2,1)S(1)} %copy-done.1, ...), custom_call_target="tpu_custom_call" | custom-call | flops 18699999232 | tf_op jit(solution)/shard_map/feed_in/pallas_call | solution.py:197
  98.9 2.7 %collective-permute-done.20.rest_3_ = bf16[8,192,384]{2,1,0:T(8,128)(2,1)S(1)} collective-permute-done((bf16[8,192,384]{2,1,0:T(8,128)(2,1)S(1)}, bf16[8,192,384]{2,1,0:T(8,128)(2,1)S(1)}, u32[]{:S(2)}, u32[]{:S(2)}) %collective-permute-start.20) | collective-permute-done | bytes 1179680 | tf_op jit(solution)/shard_map/ppermute | solution.py:348
  101.7 25.0 %feed_out.1 = (bf16[1024,768]{1,0:T(8,128)(2,1)}, f32[1024,768]{1,0:T(8,128)}, bf16[768,1024]{1,0:T(8,128)(2,1)S(1)}) custom-call(s32[3]{0:T(128)S(1)} %pad_add_fusion.sc_ref, f32[1024,768]{1,0:T(8,128)S(1)} %get-tuple-element.107.n1_ref, f32[1024,128]{1,0:T(8,128)S(1)} %get-tuple-element.108.r1_ref, bf16[1024,3072]{1,0:T(8,128)(2,1)S(1)} %get-tuple-element.109.act_ref, ...), custom_call_target="tpu_custom_call" | custom-call | flops 30799998976 | tf_op jit(solution)/shard_map/feed_out/pallas_call | solution.py:230
  126.6 17.3 %attend_back.1 = (bf16[1024,2304]{1,0:T(8,128)(2,1)S(1)}, bf16[16,1024]{1,0:T(8,128)(2,1)S(1)}, f32[16,768]{1,0:T(8,128)S(1)}, f32[16,768]{1,0:T(8,128)S(1)}) custom-call(s32[3]{0:T(128)S(1)} %pad_add_fusion.sc_ref, bf16[1024,2304]{1,0:T(8,128)(2,1)} %copy-done.8, bf16[1024,2304]{1,0:T(8,128)(2,1)} %copy-done.8, bf16[1024,2304]{1,0:T(8,128)(2,1)} %copy-done.8, ...), custom_call_target="tpu_custom_call" | custom-call | flops 19800000512 | tf_op jit(solution)/shard_map/attend_back/pallas_call | solution.py:320
  145.3 2.0 %collective-permute-start.24 = (f32[16,768]{1,0:T(8,128)S(1)}, f32[16,768]{1,0:T(8,128)S(1)}, u32[]{:S(2)}, u32[]{:S(2)}) collective-permute-start(f32[16,768]{1,0:T(8,128)S(1)} %add.63), channel_id=1, source_target_pairs={{0,6},{1,7},{2,4},{3,5},{4,2},{5,3},{6,0},{7,1},{8,14},{9,15},{10,... | collective-permute-start | bytes 147464 | tf_op jit(solution)/shard_map/ppermute | solution.py:348
  148.8 1.6 collective-permute-done.24
  151.8 3.1 %collective-permute-start.27 = (f32[16,768]{1,0:T(8,128)S(1)}, f32[16,768]{1,0:T(8,128)S(1)}, u32[]{:S(2)}, u32[]{:S(2)}) collective-permute-start(f32[16,768]{1,0:T(8,128)S(1)} %add_add_fusion.1), channel_id=1, source_target_pairs={{0,24},{1,25},{2,26},{3,27},{4,28},{5,29},{6,30},{7,31},{8,16},{9,... | collective-permute-start | bytes 147464 | tf_op jit(solution)/shard_map/ppermute | solution.py:348
  154.9 1.3 collective-permute-start.25
  156.3 5.6 %inputs_grad.1 = f32[1024,768]{1,0:T(8,128)} custom-call(f32[1024,768]{1,0:T(8,128)S(1)} %copy-done.7, bf16[1024,2304]{1,0:T(8,128)(2,1)S(1)} %get-tuple-element.124.d_ref, bf16[16,1024]{1,0:T(8,128)(2,1)S(1)} %get-tuple-element.125.gl, bf16[768,2304]{1,0:T(8,128)(2,1)S(1)} %copy-done.6, bf16[16,768]{1,0:T(8,128)(2,1)S(1)} %get-tuple-element.127.dnt_ref), custom_call_target="tpu_custom_call" | custom-call | flops 7699999744 | tf_op jit(solution)/shard_map/inputs_grad/pallas_call | solution.py:338
  162.0 1.2 collective-permute-done.28.other_ref
  163.3 1.2 finish.1
  (117 shorter events, 12.3 us)
Async XLA Ops:
  3.9 14.0 %collective-permute-start.2 = (bf16[144,384]{1,0:T(8,128)(2,1)S(1)}, bf16[144,384]{1,0:T(8,128)(2,1)S(1)}, u32[]{:S(2)}, u32[]{:S(2)}) collective-permute-start(bf16[144,384]{1,0:T(8,128)(2,1)S(1)} %pad_maximum_fusion.4), channel_id=1, source_target_pairs={{0,24},{1,25},{2,26},{3,27},{4,28},{5,29},{6,30},{7,31},{8,16},{9,... | collective-permute-start | bytes 331784 | tf_op jit(solution)/shard_map/ppermute | solution.py:348
  8.9 9.6 %collective-permute-start.1 = (bf16[144,384]{1,0:T(8,128)(2,1)S(1)}, bf16[144,384]{1,0:T(8,128)(2,1)S(1)}, u32[]{:S(2)}, u32[]{:S(2)}) collective-permute-start(bf16[144,384]{1,0:T(8,128)(2,1)S(1)} %pad_maximum_fusion.4), channel_id=1, source_target_pairs={{0,16},{1,17},{2,18},{3,19},{4,20},{5,21},{6,22},{7,23},{8,24},{9,... | collective-permute-start | bytes 331784 | tf_op jit(solution)/shard_map/ppermute | solution.py:348
  8.9 9.6 %collective-permute-start = (bf16[144,384]{1,0:T(8,128)(2,1)S(1)}, bf16[144,384]{1,0:T(8,128)(2,1)S(1)}, u32[]{:S(2)}, u32[]{:S(2)}) collective-permute-start(bf16[144,384]{1,0:T(8,128)(2,1)S(1)} %pad_maximum_fusion.4), channel_id=1, source_target_pairs={{0,8},{1,9},{2,10},{3,11},{4,12},{5,13},{6,14},{7,15},{8,0},{9,1},... | collective-permute-start | bytes 331784 | tf_op jit(solution)/shard_map/ppermute | solution.py:348
  11.6 9.8 %collective-permute-start.5 = (bf16[192,384]{1,0:T(8,128)(2,1)S(1)}, bf16[192,384]{1,0:T(8,128)(2,1)S(1)}, u32[]{:S(2)}, u32[]{:S(2)}) collective-permute-start(bf16[192,384]{1,0:T(8,128)(2,1)S(1)} %bitcast.46), channel_id=1, source_target_pairs={{0,2},{1,5},{2,0},{3,7},{4,6},{5,1},{6,4},{7,3},{8,10},{9,13},{10,... | collective-permute-start | bytes 442376 | tf_op jit(solution)/shard_map/ppermute | solution.py:348
  18.5 11.0 %collective-permute-start.4 = (bf16[240,384]{1,0:T(8,128)(2,1)S(1)}, bf16[240,384]{1,0:T(8,128)(2,1)S(1)}, u32[]{:S(2)}, u32[]{:S(2)}) collective-permute-start(bf16[240,384]{1,0:T(8,128)(2,1)S(1)} %constant_dynamic-update-slice_fusion), channel_id=1, source_target_pairs={{0,16},{1,17},{2,18},{3,19},{4,20},{5,21},{6,22},{7,23},{8,24},{9,... | collective-permute-start | bytes 552968 | tf_op jit(solution)/shard_map/ppermute | solution.py:348
  20.2 9.3 %collective-permute-start.3 = (bf16[4,144,384]{2,1,0:T(8,128)(2,1)S(1)}, bf16[4,144,384]{2,1,0:T(8,128)(2,1)S(1)}, u32[]{:S(2)}, u32[]{:S(2)}) collective-permute-start(bf16[4,144,384]{2,1,0:T(8,128)(2,1)S(1)} %pad_maximum_fusion.1), channel_id=1, source_target_pairs={{0,2},{1,5},{2,0},{3,7},{4,6},{5,1},{6,4},{7,3},{8,10},{9,13},{10,... | collective-permute-start | bytes 1327112 | tf_op jit(solution)/shard_map/ppermute | solution.py:348
  29.6 13.4 %collective-permute-start.7 = (bf16[8,144,384]{2,1,0:T(8,128)(2,1)S(1)}, bf16[8,144,384]{2,1,0:T(8,128)(2,1)S(1)}, u32[]{:S(2)}, u32[]{:S(2)}) collective-permute-start(bf16[8,144,384]{2,1,0:T(8,128)(2,1)S(1)} %constant_dynamic-update-slice_fusion.5.rest_0_), channel_id=1, source_target_pairs={{0,1},{1,0},{2,3},{3,2},{4,5},{5,4},{6,7},{7,6},{8,9},{9,8},{10,11... | collective-permute-start | bytes 2654216 | tf_op jit(solution)/shard_map/ppermute | solution.py:348
  29.7 13.3 %collective-permute-start.6 = (bf16[8,144,384]{2,1,0:T(8,128)(2,1)S(1)}, bf16[8,144,384]{2,1,0:T(8,128)(2,1)S(1)}, u32[]{:S(2)}, u32[]{:S(2)}) collective-permute-start(bf16[8,144,384]{2,1,0:T(8,128)(2,1)S(1)} %constant_dynamic-update-slice_fusion.5.rest_0_), channel_id=1, source_target_pairs={{0,4},{1,3},{2,6},{3,1},{4,0},{5,7},{6,2},{7,5},{8,12},{9,11},{10,... | collective-permute-start | bytes 2654216 | tf_op jit(solution)/shard_map/ppermute | solution.py:348
  31.3 6.4 %collective-permute-start.9 = (bf16[240,384]{1,0:T(8,128)(2,1)S(1)}, bf16[240,384]{1,0:T(8,128)(2,1)S(1)}, u32[]{:S(2)}, u32[]{:S(2)}) collective-permute-start(bf16[240,384]{1,0:T(8,128)(2,1)S(1)} %constant_dynamic-update-slice_fusion), channel_id=1, source_target_pairs={{0,8},{1,9},{2,10},{3,11},{4,12},{5,13},{6,14},{7,15},{8,0},{9,1},... | collective-permute-start | bytes 552968 | tf_op jit(solution)/shard_map/ppermute | solution.py:348
  32.3 10.7 %collective-permute-start.8 = (bf16[240,384]{1,0:T(8,128)(2,1)S(1)}, bf16[240,384]{1,0:T(8,128)(2,1)S(1)}, u32[]{:S(2)}, u32[]{:S(2)}) collective-permute-start(bf16[240,384]{1,0:T(8,128)(2,1)S(1)} %constant_dynamic-update-slice_fusion), channel_id=1, source_target_pairs={{0,24},{1,25},{2,26},{3,27},{4,28},{5,29},{6,30},{7,31},{8,16},{9,... | collective-permute-start | bytes 552968 | tf_op jit(solution)/shard_map/ppermute | solution.py:348
  43.0 5.8 %collective-permute-start.11 = (bf16[8,144,384]{2,1,0:T(8,128)(2,1)S(1)}, bf16[8,144,384]{2,1,0:T(8,128)(2,1)S(1)}, u32[]{:S(2)}, u32[]{:S(2)}) collective-permute-start(bf16[8,144,384]{2,1,0:T(8,128)(2,1)S(1)} %collective-permute-done.6.rest_1_), channel_id=1, source_target_pairs={{0,1},{1,0},{2,3},{3,2},{4,5},{5,4},{6,7},{7,6},{8,9},{9,8},{10,11... | collective-permute-start | bytes 2654216 | tf_op jit(solution)/shard_map/ppermute | solution.py:348
  43.1 33.4 %collective-permute-start.16 = (bf16[2,192,384]{2,1,0:T(8,128)(2,1)S(1)}, bf16[2,192,384]{2,1,0:T(8,128)(2,1)S(1)}, u32[]{:S(2)}, u32[]{:S(2)}) collective-permute-start(bf16[2,192,384]{2,1,0:T(8,128)(2,1)S(1)} %pad_maximum_fusion.2), channel_id=1, source_target_pairs={{0,24},{1,25},{2,26},{3,27},{4,28},{5,29},{6,30},{7,31},{8,16},{9,... | collective-permute-start | bytes 884744 | tf_op jit(solution)/shard_map/ppermute | solution.py:348
  45.9 30.6 %collective-permute-start.15 = (bf16[2,192,384]{2,1,0:T(8,128)(2,1)S(1)}, bf16[2,192,384]{2,1,0:T(8,128)(2,1)S(1)}, u32[]{:S(2)}, u32[]{:S(2)}) collective-permute-start(bf16[2,192,384]{2,1,0:T(8,128)(2,1)S(1)} %pad_maximum_fusion.2), channel_id=1, source_target_pairs={{0,16},{1,17},{2,18},{3,19},{4,20},{5,21},{6,22},{7,23},{8,24},{9,... | collective-permute-start | bytes 884744 | tf_op jit(solution)/shard_map/ppermute | solution.py:348
  45.9 30.6 %collective-permute-start.14 = (bf16[2,192,384]{2,1,0:T(8,128)(2,1)S(1)}, bf16[2,192,384]{2,1,0:T(8,128)(2,1)S(1)}, u32[]{:S(2)}, u32[]{:S(2)}) collective-permute-start(bf16[2,192,384]{2,1,0:T(8,128)(2,1)S(1)} %pad_maximum_fusion.2), channel_id=1, source_target_pairs={{0,8},{1,9},{2,10},{3,11},{4,12},{5,13},{6,14},{7,15},{8,0},{9,1},... | collective-permute-start | bytes 884744 | tf_op jit(solution)/shard_map/ppermute | solution.py:348
  47.7 11.5 %collective-permute-start.10 = (bf16[4,240,384]{2,1,0:T(8,128)(2,1)S(1)}, bf16[4,240,384]{2,1,0:T(8,128)(2,1)S(1)}, u32[]{:S(2)}, u32[]{:S(2)}) collective-permute-start(bf16[4,240,384]{2,1,0:T(8,128)(2,1)S(1)} %pad_maximum_fusion), channel_id=1, source_target_pairs={{0,2},{1,5},{2,0},{3,7},{4,6},{5,1},{6,4},{7,3},{8,10},{9,13},{10,... | collective-permute-start | bytes 2211848 | tf_op jit(solution)/shard_map/ppermute | solution.py:348
  59.3 17.2 %collective-permute-start.13 = (bf16[8,240,384]{2,1,0:T(8,128)(2,1)S(1)}, bf16[8,240,384]{2,1,0:T(8,128)(2,1)S(1)}, u32[]{:S(2)}, u32[]{:S(2)}) collective-permute-start(bf16[8,240,384]{2,1,0:T(8,128)(2,1)S(1)} %constant_dynamic-update-slice_fusion.10.rest_0_), channel_id=1, source_target_pairs={{0,1},{1,0},{2,3},{3,2},{4,5},{5,4},{6,7},{7,6},{8,9},{9,8},{10,11... | collective-permute-start | bytes 4423688 | tf_op jit(solution)/shard_map/ppermute | solution.py:348
  59.4 19.4 %collective-permute-start.12 = (bf16[8,240,384]{2,1,0:T(8,128)(2,1)S(1)}, bf16[8,240,384]{2,1,0:T(8,128)(2,1)S(1)}, u32[]{:S(2)}, u32[]{:S(2)}) collective-permute-start(bf16[8,240,384]{2,1,0:T(8,128)(2,1)S(1)} %constant_dynamic-update-slice_fusion.10.rest_0_), channel_id=1, source_target_pairs={{0,4},{1,3},{2,6},{3,1},{4,0},{5,7},{6,2},{7,5},{8,12},{9,11},{10,... | collective-permute-start | bytes 4423688 | tf_op jit(solution)/shard_map/ppermute | solution.py:348
  78.8 3.3 %collective-permute-start.18 = (bf16[8,240,384]{2,1,0:T(8,128)(2,1)S(1)}, bf16[8,240,384]{2,1,0:T(8,128)(2,1)S(1)}, u32[]{:S(2)}, u32[]{:S(2)}) collective-permute-start(bf16[8,240,384]{2,1,0:T(8,128)(2,1)S(1)} %collective-permute-done.12.rest_1_), channel_id=1, source_target_pairs={{0,1},{1,0},{2,3},{3,2},{4,5},{5,4},{6,7},{7,6},{8,9},{9,8},{10,11... | collective-permute-start | bytes 4423688 | tf_op jit(solution)/shard_map/ppermute | solution.py:348
  79.1 19.7 %collective-permute-start.19 = (bf16[8,192,384]{2,1,0:T(8,128)(2,1)S(1)}, bf16[8,192,384]{2,1,0:T(8,128)(2,1)S(1)}, u32[]{:S(2)}, u32[]{:S(2)}) collective-permute-start(bf16[8,192,384]{2,1,0:T(8,128)(2,1)S(1)} %constant_dynamic-update-slice_fusion.15.rest_0_), channel_id=1, source_target_pairs={{0,1},{1,0},{2,3},{3,2},{4,5},{5,4},{6,7},{7,6},{8,9},{9,8},{10,11... | collective-permute-start | bytes 3538952 | tf_op jit(solution)/shard_map/ppermute | solution.py:348
  79.6 19.1 %collective-permute-start.17 = (bf16[8,192,384]{2,1,0:T(8,128)(2,1)S(1)}, bf16[8,192,384]{2,1,0:T(8,128)(2,1)S(1)}, u32[]{:S(2)}, u32[]{:S(2)}) collective-permute-start(bf16[8,192,384]{2,1,0:T(8,128)(2,1)S(1)} %constant_dynamic-update-slice_fusion.15.rest_0_), channel_id=1, source_target_pairs={{0,4},{1,3},{2,6},{3,1},{4,0},{5,7},{6,2},{7,5},{8,12},{9,11},{10,... | collective-permute-start | bytes 3538952 | tf_op jit(solution)/shard_map/ppermute | solution.py:348
  98.7 2.9 %collective-permute-start.20 = (bf16[8,192,384]{2,1,0:T(8,128)(2,1)S(1)}, bf16[8,192,384]{2,1,0:T(8,128)(2,1)S(1)}, u32[]{:S(2)}, u32[]{:S(2)}) collective-permute-start(bf16[8,192,384]{2,1,0:T(8,128)(2,1)S(1)} %collective-permute-done.17.rest_1_), channel_id=1, source_target_pairs={{0,1},{1,0},{2,3},{3,2},{4,5},{5,4},{6,7},{7,6},{8,9},{9,8},{10,11... | collective-permute-start | bytes 3538952 | tf_op jit(solution)/shard_map/ppermute | solution.py:348
  101.7 25.0 %copy-start.9 = (f32[6,8,512]{2,1,0:T(8,128)S(1)}, f32[6,8,512]{2,1,0:T(8,128)}, u32[]{:S(2)}) copy-start(f32[6,8,512]{2,1,0:T(8,128)} %get-tuple-element.118.rt_ref) | copy-start | bytes 294916
  126.6 29.7 %copy-start.6 = (bf16[768,2304]{1,0:T(8,128)(2,1)S(1)}, bf16[768,2304]{1,0:T(8,128)(2,1)}, u32[]{:S(2)}) copy-start(bf16[768,2304]{1,0:T(8,128)(2,1)} %get-tuple-element.126.w_ref) | copy-start | bytes 10616836
  126.6 29.7 %copy-start.7 = (f32[1024,768]{1,0:T(8,128)S(1)}, f32[1024,768]{1,0:T(8,128)}, u32[]{:S(2)}) copy-start(f32[1024,768]{1,0:T(8,128)} %get-tuple-element.123.gfs_ref) | copy-start | bytes 9437188
  144.0 1.3 collective-permute-start.21
  145.3 5.2 %collective-permute-start.24 = (f32[16,768]{1,0:T(8,128)S(1)}, f32[16,768]{1,0:T(8,128)S(1)}, u32[]{:S(2)}, u32[]{:S(2)}) collective-permute-start(f32[16,768]{1,0:T(8,128)S(1)} %add.63), channel_id=1, source_target_pairs={{0,6},{1,7},{2,4},{3,5},{4,2},{5,3},{6,0},{7,1},{8,14},{9,15},{10,... | collective-permute-start | bytes 147464 | tf_op jit(solution)/shard_map/ppermute | solution.py:348
  147.2 4.1 %collective-permute-start.23 = (f32[16,768]{1,0:T(8,128)S(1)}, f32[16,768]{1,0:T(8,128)S(1)}, u32[]{:S(2)}, u32[]{:S(2)}) collective-permute-start(f32[16,768]{1,0:T(8,128)S(1)} %add.63), channel_id=1, source_target_pairs={{0,4},{1,5},{2,6},{3,7},{4,0},{5,1},{6,2},{7,3},{8,12},{9,13},{10,... | collective-permute-start | bytes 147464 | tf_op jit(solution)/shard_map/ppermute | solution.py:348
  147.7 4.1 %collective-permute-start.22 = (f32[16,768]{1,0:T(8,128)S(1)}, f32[16,768]{1,0:T(8,128)S(1)}, u32[]{:S(2)}, u32[]{:S(2)}) collective-permute-start(f32[16,768]{1,0:T(8,128)S(1)} %add.63), channel_id=1, source_target_pairs={{0,2},{1,3},{2,0},{3,1},{4,6},{5,7},{6,4},{7,5},{8,10},{9,11},{10,... | collective-permute-start | bytes 147464 | tf_op jit(solution)/shard_map/ppermute | solution.py:348
  151.8 10.1 %collective-permute-start.27 = (f32[16,768]{1,0:T(8,128)S(1)}, f32[16,768]{1,0:T(8,128)S(1)}, u32[]{:S(2)}, u32[]{:S(2)}) collective-permute-start(f32[16,768]{1,0:T(8,128)S(1)} %add_add_fusion.1), channel_id=1, source_target_pairs={{0,24},{1,25},{2,26},{3,27},{4,28},{5,29},{6,30},{7,31},{8,16},{9,... | collective-permute-start | bytes 147464 | tf_op jit(solution)/shard_map/ppermute | solution.py:348
  154.9 7.0 %collective-permute-start.26 = (f32[16,768]{1,0:T(8,128)S(1)}, f32[16,768]{1,0:T(8,128)S(1)}, u32[]{:S(2)}, u32[]{:S(2)}) collective-permute-start(f32[16,768]{1,0:T(8,128)S(1)} %add_add_fusion.1), channel_id=1, source_target_pairs={{0,16},{1,17},{2,18},{3,19},{4,20},{5,21},{6,22},{7,23},{8,24},{9,... | collective-permute-start | bytes 147464 | tf_op jit(solution)/shard_map/ppermute | solution.py:348
  154.9 7.0 %collective-permute-start.25 = (f32[16,768]{1,0:T(8,128)S(1)}, f32[16,768]{1,0:T(8,128)S(1)}, u32[]{:S(2)}, u32[]{:S(2)}) collective-permute-start(f32[16,768]{1,0:T(8,128)S(1)} %add_add_fusion.1), channel_id=1, source_target_pairs={{0,8},{1,9},{2,10},{3,11},{4,12},{5,13},{6,14},{7,15},{8,0},{9,1},... | collective-permute-start | bytes 147464 | tf_op jit(solution)/shard_map/ppermute | solution.py:348
  162.0 1.3 collective-permute-start.28
  (15 other events, 200.3 us)

commit v4 on v3

--- a/solution.py
+++ b/solution.py
@@ -30,32 +30,19 @@
     return pltpu.with_memory_space_constraint(v,pltpu.HBM)
 
 
-def block_copies(layout,me,bufs,outs,sems,near_inside=False):
-    if layout is None:
-        return [[pltpu.make_async_copy(b,o,sems.at[t])] for t,(b,o) in enumerate(zip(bufs,outs))]
-    first,second,other_first,other_second=bufs
+def block_copies(me,bufs,to,sems):
+    if len(bufs)==1:
+        return [pltpu.make_async_copy(bufs[0],to,sems.at[0])]
     chip=lax.div(me,2); core=lax.rem(me,2)
-    lists=[[] for _ in layout]
-    count=[0]
-    def add(lay,buf,at_block,origin,rel):
-        dst=lax.bitwise_xor(chip,rel)
-        half=buf.shape[-1]
-        at=0
-        for t,(bands,rows,start,size) in enumerate(lay):
-            for b in range(bands):
-                to=outs[t].at[pl.ds(pl.multiple_of(dst*rows+start,16),size),pl.ds(pl.multiple_of(2*half*b+origin*half,128),half)]
-                lists[t].append(pltpu.make_async_copy(buf.at[at_block,pl.ds(at,size),:],to,sems.at[count[0]]))
-                count[0]+=1
-                at+=size
-    for which,(near,far) in enumerate(((first,second),(other_first,other_second))):
-        origin=core if which==0 else 1-core
-        near_axis=1+origin
-        far_axis=2-origin
-        for hop,buf in enumerate((near,far)):
-            for i in range(8):
-                n,z=(i%2,i//2) if near_inside else (i//4,i%4)
-                add(layout,buf,i,origin,hop*far_axis+n*near_axis+4*z)
-    return lists
+    copies=[]
+    for which,buf in enumerate(bufs):
+        origin=core if which<2 else 1-core
+        _,_,rows,half=buf.shape
+        for i in range(8):
+            dst=lax.bitwise_xor(chip,(which%2)*(2-origin)+(i//4)*(1+origin)+4*(i%4))
+            at=to.at[:,pl.ds(pl.multiple_of(dst*rows,16),rows),pl.ds(pl.multiple_of(origin*half,128),half)]
+            copies.append(pltpu.make_async_copy(buf.at[i],at,sems.at[len(copies)]))
+    return copies
 
 def start_all(copies):
     for c in copies: c.start()
@@ -63,8 +50,7 @@
 def wait_all(copies):
     for c in copies: c.wait()
 
-def copy_count(layout):
-    return 2 if layout is None else 32*sum(l[0] for l in layout)
+BLOCK_COPIES=32
 
 def prep_kernel(qdt_ref,vdt_ref,qu_ref,vu_ref,ag_ref,ash_ref,fg_ref,fsh_ref,dn_ref,upq_ref,upv_ref,dnt_ref,nm_ref):
     D=qu_ref.shape[1]
@@ -84,32 +70,34 @@
         compiler_params=params(8),cost_estimate=takes(1),name="prep")(qd.T,vd.T,qu,vu,*(v.reshape(1,D) for v in (ag,ash,fg,fsh)))
 
 
-def project_kernel(layout,sc_ref,x_ref,dn_ref,upq_ref,upv_ref,*rest):
+def project_kernel(sc_ref,x_ref,dn_ref,upq_ref,upv_ref,*rest):
     *blocks,qkv_ref,low_ref,wo,w,sems,osem=rest
-    i=pl.program_id(0)
-    D=x_ref.shape[1]
+    rows,D=x_ref.shape
+    copies=block_copies(sc_ref[0],blocks,w,sems)
+    start_all(copies)
+    lows=[]
+    for s in range(rows//SLOT):
+        low=dg(x_ref[s*SLOT:(s+1)*SLOT,:],dn_ref[...],1,0).astype(BF)
+        low_ref[:,s*SLOT:(s+1)*SLOT]=low.T[:32]
+        lows.append(low)
+    wait_all(copies)
     whole=[pltpu.make_async_copy(w,wo,osem.at[0])]
-    @pl.when(i==0)
-    def _():
-        copies,=block_copies(layout,sc_ref[0],blocks,(w,),sems)
-        start_all(copies); wait_all(copies); start_all(whole)
-    x=x_ref[...]
-    rows=pl.ds(pl.multiple_of(i*SLOT,SLOT),SLOT)
-    low=dg(x,dn_ref[...],1,0).astype(BF)
-    low_ref[...]=low.T[:32]
-    qkv_ref[rows,0:D]=(dg(x,w[:,0:D],1,0)+2.0*dg(low,upq_ref[...],1,0)).astype(BF)
-    qkv_ref[rows,D:2*D]=dg(x,w[:,D:2*D],1,0).astype(BF)
-    qkv_ref[rows,2*D:]=(dg(x,w[:,2*D:],1,0)+2.0*dg(low,upv_ref[...],1,0)).astype(BF)
-    @pl.when(i==pl.num_programs(0)-1)
-    def _(): wait_all(whole)
-
-def project(scalars,x,dn,upq,upv,blocks,layout):
+    start_all(whole)
+    for t,up in enumerate((upq_ref,None,upv_ref)):
+        for s in range(rows//SLOT):
+            r=slice(s*SLOT,(s+1)*SLOT)
+            v=dg(x_ref[r,:],w[t],1,0)
+            if up is not None: v=v+2.0*dg(lows[s],up[...],1,0)
+            qkv_ref[r,t*D:(t+1)*D]=v.astype(BF)
+    wait_all(whole)
+
+def project(scalars,x,dn,upq,upv,blocks):
     rows,D=x.shape
-    return pl.pallas_call(functools.partial(project_kernel,layout),grid=(rows//SLOT,),
-        in_specs=[SCALARS,pl.BlockSpec((SLOT,D),lambda i:(i,0)),HELD,HELD,HELD]+[ANY]*len(blocks),
-        out_specs=[HELD,pl.BlockSpec((32,SLOT),lambda i:(0,i)),ANY],
-        out_shape=[sd((rows,3*D),BF),sd((32,rows),BF),pltpu.HBM((D,3*D),BF)],
-        scratch_shapes=[pltpu.VMEM((D,3*D),BF),pltpu.SemaphoreType.DMA((copy_count(layout),)),pltpu.SemaphoreType.DMA((1,))],
+    return pl.pallas_call(project_kernel,
+        in_specs=[SCALARS,HELD,HELD,HELD,HELD]+[ANY]*len(blocks),
+        out_specs=[HELD,HELD,ANY],
+        out_shape=[pltpu.VMEM((rows,3*D),BF),sd((32,rows),BF),pltpu.HBM((3,D,D),BF)],
+        scratch_shapes=[pltpu.VMEM((3,D,D),BF),pltpu.SemaphoreType.DMA((BLOCK_COPIES,)),pltpu.SemaphoreType.DMA((1,))],
         compiler_params=params(LIM["project"]),cost_estimate=takes(8),name="project")(scalars,x,dn,upq,upv,*blocks)
 
 def attend_kernel(sc_ref,qkv_ref,e_ref,ot_ref,o_ref,rt_ref):
@@ -120,27 +108,33 @@
     rows=pl.ds(pl.multiple_of(s*SLOT,SLOT),SLOT)
     def part(which,p):
         return qkv_ref[rows,pl.ds(pl.multiple_of(which*D+256*j+128*p,128),128)].astype(F32)
-    totals=[]; os=[]
+    heads=[]
     for p in range(2):
-        qp=part(0,p)*0.125
-        kp=part(1,p)
-        vp=part(2,p)
+        qp,kp,vp=part(0,p)*0.125,part(1,p),part(2,p)
         for h in range(2):
             own=(lane<64) if h==0 else (lane>=64)
             aux=64 if h==0 else 0
             one=jnp.where(lane==aux,1.0,0.0)
-            qm=jnp.where(own,qp,one).astype(BF)
-            km=jnp.where(own,kp,jnp.where(lane==aux,bias,0.0)).astype(BF)
-            vm=jnp.where(own,vp,one).astype(BF)
-            st=dg(km,qm,1,1)
-            top=jnp.max(st,axis=0,keepdims=True)
-            e=jnp.exp(st-top).astype(BF)
-            e_ref[2*p+h]=e
-            ot=dg(vm,e,0,0)
-            r=1.0/ot[aux:aux+1]
-            totals.append(r)
-            lo=64*h
-            os.append((ot[lo:lo+64]*r).astype(BF))
+            heads.append((64*h,aux,jnp.where(own,qp,one).astype(BF),
+                          jnp.where(own,kp,jnp.where(lane==aux,bias,0.0)).astype(BF),jnp.where(own,vp,one).astype(BF)))
+    totals=[]; os=[]
+    def weights(n,st):
+        e_ref[n]=jnp.exp(st-jnp.max(st,axis=0,keepdims=True)).astype(BF)
+    def mix(n):
+        lo,aux,_,_,vm=heads[n]
+        ot=dg(vm,e_ref[n],0,0)
+        r=1.0/ot[aux:aux+1]
+        totals.append(r)
+        os.append((ot[lo:lo+64]*r).astype(BF))
+    before=None
+    for n in range(4):
+        st=dg(heads[n][3],heads[n][2],1,1)
+        if before is not None:
+            weights(n-1,before)
+            if n>1: mix(n-2)
+        before=st
+    weights(3,before)
+    mix(2); mix(3)
     ot=jnp.concatenate(os,axis=0)
     ot_ref[...]=ot
     o_ref[rows,pl.ds(pl.multiple_of(256*j,256),256)]=ot.T
@@ -168,71 +162,71 @@
     cdf=0.5+0.5*lax.erf(v*0.7071067811865476)
     return v*cdf, cdf+(0.3989422804014327*v)*jnp.exp(-0.5*v*v)
 
-CH=512
-TILE=256
-LIM={"project":8,"attend":10,"feed_in":6,"feed_out":14,"attend_back":10,"inputs_grad":6}
-
-def feed_in_kernel(layout,sc_ref,x_ref,o_ref,nm_ref,*rest):
-    *blocks,n1_ref,r1_ref,act_ref,gp_ref,wo,wi,sems=rest
-    i=pl.program_id(0)
-    @pl.when(i==0)
-    def _():
-        lists=block_copies(layout,sc_ref[0],blocks,(wo,wi),sems)
-        for l in lists: start_all(l)
-        for l in lists: wait_all(l)
-    T=x_ref.shape[0]
-    rows=pl.ds(pl.multiple_of(i*T,T),T)
-    first=x_ref[...].astype(F32)+dg(o_ref[rows,:],wo[...],1,0)
-    n1,r1=norm_stats(first)
-    n1_ref[rows,:]=n1; r1_ref[rows,:]=jnp.broadcast_to(r1,(T,128))
-    hb=(n1*nm_ref[0:1,:]+nm_ref[1:2,:]).astype(BF)
-    for c in range(wi.shape[1]//CH):
-        z=dg(hb,wi[:,c*CH:(c+1)*CH],1,0)
-        act,gp=gelu_pair(z)
-        act_ref[rows,c*CH:(c+1)*CH]=act.astype(BF)
-        gp_ref[rows,c*CH:(c+1)*CH]=gp.astype(BF)
-
-def feed_in(scalars,x,o,nm,blocks,layout,FF):
+CH=256
+LIM={"project":10,"attend":12,"feed_in":8,"feed_out":20,"attend_back":12,"inputs_grad":10}
+
+def feed_in_kernel(sc_ref,x_ref,o_ref,nm_ref,*rest):
+    *blocks,n1_ref,r1_ref,act_ref,gp_ref,w,sems=rest
+    D=x_ref.shape[1]
+    copies=block_copies(sc_ref[0],blocks,w,sems)
+    start_all(copies); wait_all(copies)
+    parts=[]
+    for s in range(x_ref.shape[0]//SLOT):
+        rows=slice(s*SLOT,(s+1)*SLOT)
+        first=x_ref[rows,:].astype(F32)+dg(o_ref[rows,:],w[0],1,0)
+        n1,r1=norm_stats(first)
+        n1_ref[rows,:]=n1; r1_ref[rows,:]=jnp.broadcast_to(r1,(SLOT,128))
+        parts.append((rows,(n1*nm_ref[0:1,:]+nm_ref[1:2,:]).astype(BF)))
+    for c in range(0,act_ref.shape[1],CH):
+        for rows,hb in parts:
+            act,gp=gelu_pair(dg(hb,w[1+c//D,:,c%D:c%D+CH],1,0))
+            act_ref[rows,c:c+CH]=act.astype(BF)
+            gp_ref[rows,c:c+CH]=gp.astype(BF)
+
+def feed_in(scalars,x,o,nm,blocks,FF):
     rows,D=x.shape
-    return pl.pallas_call(functools.partial(feed_in_kernel,layout),grid=(rows//TILE,),
-        in_specs=[SCALARS,pl.BlockSpec((TILE,D),lambda i:(i,0)),HELD,HELD]+[ANY]*len(blocks),
-        out_specs=[HELD]*6,
-        out_shape=[pltpu.VMEM((rows,D),F32),pltpu.VMEM((rows,128),F32),pltpu.VMEM((rows,FF),BF),pltpu.VMEM((rows,FF),BF),pltpu.VMEM((D,D),BF),pltpu.VMEM((D,FF),BF)],
-        scratch_shapes=[pltpu.SemaphoreType.DMA((copy_count(layout),))],
-        compiler_params=params(LIM["feed_in"]),cost_estimate=takes(17),name="feed_in")(scalars,x,o,nm,*blocks)
-
-def feed_out_kernel(layout,sc_ref,n1_ref,r1_ref,act_ref,gp_ref,go_ref,nm_ref,wo,wi,*rest):
+    return pl.pallas_call(feed_in_kernel,
+        in_specs=[SCALARS,HELD,HELD,HELD]+[ANY]*len(blocks),
+        out_specs=[HELD]*5,
+        out_shape=[pltpu.VMEM((rows,D),F32),pltpu.VMEM((rows,128),F32),pltpu.VMEM((rows,FF),BF),pltpu.VMEM((rows,FF),BF),pltpu.VMEM((1+FF//D,D,D),BF)],
+        scratch_shapes=[pltpu.SemaphoreType.DMA((BLOCK_COPIES,))],
+        compiler_params=params(LIM["feed_in"]),cost_estimate=takes(14),name="feed_in")(scalars,x,o,nm,*blocks)
+
+def feed_out_kernel(sc_ref,n1_ref,r1_ref,act_ref,gp_ref,go_ref,nm_ref,w,*rest):
     *blocks,out_ref,gfs_ref,gmt_ref,wt,gi_ref,sems=rest
     i=pl.program_id(0)
     @pl.when(i==0)
     def _():
-        copies,=block_copies(layout,sc_ref[0],blocks,(wt,),sems,True)
+        copies=block_copies(sc_ref[0],blocks,wt,sems)
         start_all(copies); wait_all(copies)
-    T=go_ref.shape[0]
+    T,D=go_ref.shape
     rows=pl.ds(pl.multiple_of(i*T,T),T)
     ag,ash,fg,fsh=(nm_ref[i:i+1,:] for i in range(4))
     n1=n1_ref[rows,:]; r1=r1_ref[rows,0:1]
-    acc=n1*ag+ash+dg(act_ref[rows,:],wt[...],1,0)
+    acc=n1*ag+ash+dg(act_ref[rows,:],wt[0],1,0)
     n2,r2=norm_stats(acc)
     out_ref[...]=(n2*fg+fsh).astype(BF)
     g2=norm_back(go_ref[...].astype(F32)*fg,n2,r2)
     g2b=g2.astype(BF)
-    for c in range(wi.shape[1]//CH):
-        ga=dg(g2b,wt[c*CH:(c+1)*CH,:],1,1)
-        gi_ref[:,c*CH:(c+1)*CH]=(ga*gp_ref[rows,c*CH:(c+1)*CH].astype(F32)).astype(BF)
-    g1=norm_back((g2+dg(gi_ref[...],wi[...],1,1))*ag,n1,r1)
+    for c in range(0,gi_ref.shape[1],CH):
+        ga=dg(g2b,wt[0,c:c+CH,:],1,1)
+        gi_ref[:,c:c+CH]=(ga*gp_ref[rows,c:c+CH].astype(F32)).astype(BF)
+    acc=g2
+    for b in range(gi_ref.shape[1]//D):
+        acc=acc+dg(gi_ref[:,b*D:(b+1)*D],w[1+b],1,1)
+    g1=norm_back(acc*ag,n1,r1)
     gfs_ref[...]=g1
-    gmt_ref[:,rows]=dg(wo[...],g1.astype(BF),1,1).astype(BF)
-
-def feed_out(scalars,n1,r1,act,gp,go,wo,wi,nm,blocks,layout):
-    rows,D=n1.shape; FF=wi.shape[1]
-    row=pl.BlockSpec((TILE,D),lambda i:(i,0))
-    return pl.pallas_call(functools.partial(feed_out_kernel,layout),grid=(rows//TILE,),
-        in_specs=[SCALARS,HELD,HELD,HELD,HELD,row,HELD,HELD,HELD]+[ANY]*len(blocks),
+    gmt_ref[:,rows]=dg(w[0],g1.astype(BF),1,1).astype(BF)
+
+def feed_out(scalars,n1,r1,act,gp,go,w,nm,blocks):
+    rows,D=n1.shape; FF=act.shape[1]
+    row=pl.BlockSpec((SLOT,D),lambda i:(i,0))
+    return pl.pallas_call(feed_out_kernel,grid=(rows//SLOT,),
+        in_specs=[SCALARS,HELD,HELD,HELD,HELD,row,HELD,HELD]+[ANY]*len(blocks),
         out_specs=[row,row,HELD],
         out_shape=[sd((rows,D),BF),pltpu.HBM((rows,D),F32),pltpu.VMEM((D,rows),BF)],
-        scratch_shapes=[pltpu.VMEM((FF,D),BF),pltpu.VMEM((TILE,FF),BF),pltpu.SemaphoreType.DMA((copy_count(layout),))],
-        compiler_params=params(LIM["feed_out"]),cost_estimate=takes(28),name="feed_out")(scalars,n1,r1,act,gp,go,nm,wo,wi,*blocks)
+        scratch_shapes=[pltpu.VMEM((1,FF,D),BF),pltpu.VMEM((SLOT,FF),BF),pltpu.SemaphoreType.DMA((BLOCK_COPIES,))],
+        compiler_params=params(LIM["feed_out"]),cost_estimate=takes(24),name="feed_out")(scalars,n1,r1,act,gp,go,nm,w,*blocks)
 
 
 def attend_back_kernel(sc_ref,q_ref,k_ref,v_ref,e_ref,ot_ref,rt_ref,gmt_ref,x_ref,low_ref,upq_ref,upv_ref,
@@ -330,7 +324,10 @@
 def inputs_kernel(gfs_ref,d_ref,gl,w_ref,dnt_ref,out_ref):
     T=gfs_ref.shape[0]
     rows=pl.ds(pl.multiple_of(pl.program_id(0)*T,T),T)
-    out_ref[...]=gfs_ref[...]+dg(d_ref[rows,:],w_ref[...],1,1)+dg(gl[...],dnt_ref[...],0,0)
+    D=gfs_ref.shape[1]
+    v=gfs_ref[...]+dg(gl[...],dnt_ref[...],0,0)
+    for t in range(3): v=v+dg(d_ref[rows,t*D:(t+1)*D],w_ref[t],1,1)
+    out_ref[...]=v
 
 def inputs_grad(gfs,d,gl,w,dnt):
     rows,D=gfs.shape
@@ -359,6 +356,9 @@
 
 def far_hop(v):
     return permute(v,lambda i:i^(2 if i%2 else 4))
+
+def in_bands(bands,*blocks):
+    return tuple(b.reshape(8,bands,-1,b.shape[2]) for b in blocks)
 
 def core_pair(v):
     groups=[[2*i,2*i+1] for i in range(lax.axis_size("fsdp")//2)]
@@ -395,7 +395,7 @@
     return lax.optimization_barrier(v)
 
 def by_hops(scalars,x,wq,wk,wv,wo,wi,wt,ag,ash,fg,fsh,qd,qu,vd,vu,go):
-    D=wq.shape[1]; FF=wi.shape[1]; bands=FF//D; r=wq.shape[0]; rt_=wt.shape[0]
+    D=wq.shape[1]; FF=wi.shape[1]; bands=FF//D; r=wq.shape[0]
     top=device_count()//4
     both=core_pair(jnp.concatenate([wq,wk,wv],0))
     s1=jnp.concatenate([column_half(both[:,r*t:r*t+r]) for t in range(3)],0)
@@ -420,29 +420,30 @@
     n2=near_hop(a2)
     z3=along_z(jnp.stack([s3,n3],0))
     oh1,=tie(oh1)
-    qkv,low,wqkv=project(scalars,x,dn,upq,upv,(f1,h1,of1,oh1),((3,2*r,0,2*r),))
+    qkv,low,wqkv=project(scalars,x,dn,upq,upv,in_bands(3,f1,h1,of1,oh1))
     n2,qkv=tie(n2,qkv)
     f2=jnp.concatenate([a2,n2],0)
     h2=far_hop(f2); of2=exchange(f2,1)
     e,ot,o,rt=attend(scalars,qkv,x.shape[0]//SLOT)
     h2,o,of2,z3=tie(h2,o,of2,z3)
     oh2=exchange(h2,1)
-    f3=jnp.concatenate(z3,0)
+    f3=jnp.stack(z3,1).reshape(8,-1,D//2)
     h3=far_hop(f3); of3=exchange(f3,1)
     oh2,=tie(oh2)
-    nn,r1,act,gp,wo,wi=feed_in(scalars,x,o,nm,(f2,h2,of2,oh2),((1,2*r,0,2*r),(bands,2*r,0,2*r)),FF)
+    nn,r1,act,gp,w=feed_in(scalars,x,o,nm,in_bands(1+bands,f2,h2,of2,oh2),FF)
     h3,nn,of3=tie(h3,nn,of3)
     oh3=exchange(h3,1)
-    out,gfs,gmt=feed_out(scalars,nn,r1,act,gp,go,wo,wi,nm,(f3,h3,of3,oh3),((1,2*rt_,0,2*rt_),))
+    out,gfs,gmt=feed_out(scalars,nn,r1,act,gp,go,w,nm,in_bands(1,f3,h3,of3,oh3))
     return qkv,low,wqkv,e,ot,rt,out,gfs,gmt,upq,upv,dnt
 
 def by_all_gather(scalars,x,wq,wk,wv,wo,wi,wt,ag,ash,fg,fsh,qd,qu,vd,vu,go):
     wq,wk,wv,wo,wi,wt=(lax.all_gather(w,AXES,axis=0,tiled=True) for w in (wq,wk,wv,wo,wi,wt))
+    D=wq.shape[1]; FF=wi.shape[1]
     dn,upq,upv,dnt,nm=prep(qd,qu,vd,vu,ag,ash,fg,fsh)
-    qkv,low,wqkv=project(scalars,x,dn,upq,upv,(jnp.concatenate([wq,wk,wv],1),),None)
+    qkv,low,wqkv=project(scalars,x,dn,upq,upv,(jnp.stack([wq,wk,wv],0),))
     e,ot,o,rt=attend(scalars,qkv,x.shape[0]//SLOT)
-    nn,r1,act,gp,wo,wi=feed_in(scalars,x,o,nm,(wo,wi),None,wi.shape[1])
-    out,gfs,gmt=feed_out(scalars,nn,r1,act,gp,go,wo,wi,nm,(wt,),None)
+    nn,r1,act,gp,w=feed_in(scalars,x,o,nm,(jnp.stack([wo]+[wi[:,c:c+D] for c in range(0,FF,D)],0),),FF)
+    out,gfs,gmt=feed_out(scalars,nn,r1,act,gp,go,w,nm,(wt[None],))
     return qkv,low,wqkv,e,ot,rt,out,gfs,gmt,upq,upv,dnt
 
 def shards(x,lengths,wq,wk,wv,wo,wi,wt,ag,ash,fg,fsh,qd,qu,vd,vu,go):

time: 165 us -> 160 us (0.970)
  Pallas kernels: 90 us -> 79.7 us
  waiting for transfers between devices: 31 us -> 37.4 us
    pallas_call x3, Pallas kernels: 49.9 us -> 42.3 us  [the longest x1 23.4 us: feed_out(): pl.pallas_call(feed_out_kernel, grid=(rows // SLOT,), in_specs=[SCALARS,...]
    ppermute x29, waiting for transfers between devices: 31 us -> 37.4 us  [permute(): lax.ppermute(v, AXES, [(i, target(i)) for i in range(device_count())])]
    pallas_call x1, Pallas kernels: 15.8 us -> 13.1 us  [attend(): pl.pallas_call(attend_kernel, grid=(slots, J), in_specs=[SCALARS, HELD],...]
  transfers between devices with their start and end apart: 29 -> 29, of which waited for: 13 -> 14; matrix products, arithmetic and copies ran while one was open for 1% -> 1% of each run, Pallas kernels for 28% -> 24%
where the time goes in v4:
time: 160 us
  Pallas kernels  79.7 us (50%)
  waiting for transfers between devices  37.4 us (23%)
  starting transfers between devices  31.3 us (20%)
  blocking collectives  7.94 us (5%)
  other arithmetic  1.68 us (1%)
    ppermute x29, waiting for transfers between devices, permute(): lax.ppermute(v, AXES, [(i, target(i)) for i in range(device_count())])  37.4 us
    ppermute x29, starting transfers between devices, permute(): lax.ppermute(v, AXES, [(i, target(i)) for i in range(device_count())])  31.3 us
    pallas_call x1, Pallas kernels, feed_out(): pl.pallas_call(feed_out_kernel, grid=(rows // SLOT,), in_specs=[SCALARS,...  23.4 us
    pallas_call x1, Pallas kernels, attend_back(): pl.pallas_call(attend_back_kernel, grid=(S, J), in_specs=[SCALARS, *[pl.B...  17.3 us
    pallas_call x1, Pallas kernels, attend(): pl.pallas_call(attend_kernel, grid=(slots, J), in_specs=[SCALARS, HELD],...  13.1 us
    pallas_call x1, Pallas kernels, feed_in(): pl.pallas_call(feed_in_kernel, in_specs=[SCALARS, HELD, HELD, HELD] + [AN...  11.9 us
    all_gather x4, blocking collectives, core_pair(): lax.all_gather(v, 'fsdp', axis=0, tiled=False, axis_index_groups=groups)  7.94 us
    pallas_call x1, Pallas kernels, project(): pl.pallas_call(project_kernel, in_specs=[SCALARS, HELD, HELD, HELD, HELD]...  7 us
  transfers between devices with their start and end apart: 29, of which 14 were waited for; matrix products, arithmetic and copies ran while one was open for 1% of the time, Pallas kernels for 24%

profile of v4, /device:TPU:0, one launch (start us, length us, event | category | flops | bytes accessed | tf_op | source)
XLA Modules:
  0.0 160.3 jit_solution(3405984162278240449)
XLA Ops:
  1.7 2.1 %all-gather = bf16[144,768]{1,0:T(8,128)(2,1)S(1)} all-gather(bf16[72,768]{1,0:T(8,128)(2,1)S(1)} %pad_maximum_fusion.4), channel_id=2, replica_groups={{0,1},{2,3},{4,5},{6,7},{8,9},{10,11},{12,13},{14,15},{16,17},{18,19},{..., dimensions={0}, use_global_device_ids=true | all-gather | bytes 331776 | tf_op jit(solution)/shard_map/all_gather | solution.py:365
  3.9 5.0 %collective-permute-start.2 = (bf16[144,384]{1,0:T(8,128)(2,1)S(1)}, bf16[144,384]{1,0:T(8,128)(2,1)S(1)}, u32[]{:S(2)}, u32[]{:S(2)}) collective-permute-start(bf16[144,384]{1,0:T(8,128)(2,1)S(1)} %pad_maximum_fusion.5), channel_id=1, source_target_pairs={{0,24},{1,25},{2,26},{3,27},{4,28},{5,29},{6,30},{7,31},{8,16},{9,... | collective-permute-start | bytes 331784 | tf_op jit(solution)/shard_map/ppermute | solution.py:345
  9.5 2.0 %all-gather.3 = bf16[192,768]{1,0:T(8,128)(2,1)S(1)} all-gather(bf16[96,768]{1,0:T(8,128)(2,1)S(1)} %copy-done.10), channel_id=5, replica_groups={{0,1},{2,3},{4,5},{6,7},{8,9},{10,11},{12,13},{14,15},{16,17},{18,19},{..., dimensions={0}, use_global_device_ids=true | all-gather | bytes 442368 | tf_op jit(solution)/shard_map/all_gather | solution.py:365
  11.6 1.7 %collective-permute-start.5 = (bf16[192,384]{1,0:T(8,128)(2,1)S(1)}, bf16[192,384]{1,0:T(8,128)(2,1)S(1)}, u32[]{:S(2)}, u32[]{:S(2)}) collective-permute-start(bf16[192,384]{1,0:T(8,128)(2,1)S(1)} %bitcast.107), channel_id=1, source_target_pairs={{0,2},{1,5},{2,0},{3,7},{4,6},{5,1},{6,4},{7,3},{8,10},{9,13},{10,... | collective-permute-start | bytes 442376 | tf_op jit(solution)/shard_map/ppermute | solution.py:345
  13.6 1.9 %all-gather.1 = bf16[48,768]{1,0:T(8,128)(2,1)S(1)} all-gather(bf16[24,768]{1,0:T(8,128)(2,1)S(1)} %copy-done.12), channel_id=3, replica_groups={{0,1},{2,3},{4,5},{6,7},{8,9},{10,11},{12,13},{14,15},{16,17},{18,19},{..., dimensions={0}, use_global_device_ids=true | all-gather | bytes 110592 | tf_op jit(solution)/shard_map/all_gather | solution.py:365
  15.4 2.0 %all-gather.2 = bf16[48,3072]{1,0:T(8,128)(2,1)S(1)} all-gather(bf16[24,3072]{1,0:T(8,128)(2,1)S(1)} %copy-done.11), channel_id=4, replica_groups={{0,1},{2,3},{4,5},{6,7},{8,9},{10,11},{12,13},{14,15},{16,17},{18,19},{..., dimensions={0}, use_global_device_ids=true | all-gather | bytes 442368 | tf_op jit(solution)/shard_map/all_gather | solution.py:365
  18.5 1.6 collective-permute-start.4
  21.4 8.1 %collective-permute-done.4 = bf16[240,384]{1,0:T(8,128)(2,1)S(1)} collective-permute-done((bf16[240,384]{1,0:T(8,128)(2,1)S(1)}, bf16[240,384]{1,0:T(8,128)(2,1)S(1)}, u32[]{:S(2)}, u32[]{:S(2)}) %collective-permute-start.4) | collective-permute-done | bytes 184352 | tf_op jit(solution)/shard_map/ppermute | solution.py:345
  29.7 1.6 collective-permute-start.6
  32.5 2.0 %collective-permute-start.8 = (bf16[240,384]{1,0:T(8,128)(2,1)S(1)}, bf16[240,384]{1,0:T(8,128)(2,1)S(1)}, u32[]{:S(2)}, u32[]{:S(2)}) collective-permute-start(bf16[240,384]{1,0:T(8,128)(2,1)S(1)} %constant_dynamic-update-slice_fusion), channel_id=1, source_target_pairs={{0,24},{1,25},{2,26},{3,27},{4,28},{5,29},{6,30},{7,31},{8,16},{9,... | collective-permute-start | bytes 552968 | tf_op jit(solution)/shard_map/ppermute | solution.py:345
  34.7 3.2 %collective-permute-done.9 = bf16[240,384]{1,0:T(8,128)(2,1)S(1)} collective-permute-done((bf16[240,384]{1,0:T(8,128)(2,1)S(1)}, bf16[240,384]{1,0:T(8,128)(2,1)S(1)}, u32[]{:S(2)}, u32[]{:S(2)}) %collective-permute-start.9) | collective-permute-done | bytes 184352 | tf_op jit(solution)/shard_map/ppermute | solution.py:345
  37.8 5.4 %collective-permute-done.8 = bf16[240,384]{1,0:T(8,128)(2,1)S(1)} collective-permute-done((bf16[240,384]{1,0:T(8,128)(2,1)S(1)}, bf16[240,384]{1,0:T(8,128)(2,1)S(1)}, u32[]{:S(2)}, u32[]{:S(2)}) %collective-permute-start.8) | collective-permute-done | bytes 184352 | tf_op jit(solution)/shard_map/ppermute | solution.py:345
  43.3 2.7 %collective-permute-start.16 = (bf16[2,192,384]{2,1,0:T(8,128)(2,1)S(1)}, bf16[2,192,384]{2,1,0:T(8,128)(2,1)S(1)}, u32[]{:S(2)}, u32[]{:S(2)}) collective-permute-start(bf16[2,192,384]{2,1,0:T(8,128)(2,1)S(1)} %pad_maximum_fusion.3), channel_id=1, source_target_pairs={{0,24},{1,25},{2,26},{3,27},{4,28},{5,29},{6,30},{7,31},{8,16},{9,... | collective-permute-start | bytes 884744 | tf_op jit(solution)/shard_map/ppermute | solution.py:345
  45.9 1.8 %collective-permute-start.14 = (bf16[2,192,384]{2,1,0:T(8,128)(2,1)S(1)}, bf16[2,192,384]{2,1,0:T(8,128)(2,1)S(1)}, u32[]{:S(2)}, u32[]{:S(2)}) collective-permute-start(bf16[2,192,384]{2,1,0:T(8,128)(2,1)S(1)} %pad_maximum_fusion.3), channel_id=1, source_target_pairs={{0,8},{1,9},{2,10},{3,11},{4,12},{5,13},{6,14},{7,15},{8,0},{9,1},... | collective-permute-start | bytes 884744 | tf_op jit(solution)/shard_map/ppermute | solution.py:345
  48.8 7.0 %project.1 = (bf16[1024,2304]{1,0:T(8,128)(2,1)S(1)}, bf16[32,1024]{1,0:T(8,128)(2,1)S(1)}, bf16[3,768,768]{2,1,0:T(8,128)(2,1)}) custom-call(s32[3]{0:T(128)S(1)} %pad_add_fusion.sc_ref, bf16[1024,768]{1,0:T(8,128)(2,1)S(1)} %copy-done.1, bf16[768,128]{1,0:T(8,128)(2,1)S(1)} %get-tuple-element.87.dn_ref, bf16[128,768]{1,0:T(8,128)(2,1)S(1)} %get-tuple-element.88.upq_ref, ...), custom_call_target="tpu_custom_call" | custom-call | flops 8800000000 | tf_op jit(solution)/shard_map/project/pallas_call | solution.py:96
  55.9 3.5 %collective-permute-done.10 = bf16[4,240,384]{2,1,0:T(8,128)(2,1)S(1)} collective-permute-done((bf16[4,240,384]{2,1,0:T(8,128)(2,1)S(1)}, bf16[4,240,384]{2,1,0:T(8,128)(2,1)S(1)}, u32[]{:S(2)}, u32[]{:S(2)}) %collective-permute-start.10) | collective-permute-done | bytes 737312 | tf_op jit(solution)/shard_map/ppermute | solution.py:345
  60.7 13.1 %attend.1 = (bf16[24,512,512]{2,1,0:T(8,128)(2,1)}, bf16[1536,512]{1,0:T(8,128)(2,1)}, bf16[1024,768]{1,0:T(8,128)(2,1)S(1)}, f32[6,8,512]{2,1,0:T(8,128)}) custom-call(s32[3]{0:T(128)S(1)} %pad_add_fusion.sc_ref, bf16[1024,2304]{1,0:T(8,128)(2,1)S(1)} %get-tuple-element.94.qkv_ref.q_ref.k_ref.v_ref), custom_call_target="tpu_custom_call" | custom-call | flops 17600000000 | tf_op jit(solution)/shard_map/attend/pallas_call | solution.py:145
  73.8 5.2 %collective-permute-done.12 = bf16[8,240,384]{2,1,0:T(8,128)(2,1)S(1)} collective-permute-done((bf16[8,240,384]{2,1,0:T(8,128)(2,1)S(1)}, bf16[8,240,384]{2,1,0:T(8,128)(2,1)S(1)}, u32[]{:S(2)}, u32[]{:S(2)}) %collective-permute-start.12) | collective-permute-done | bytes 1474592 | tf_op jit(solution)/shard_map/ppermute | solution.py:345
  82.3 11.9 %feed_in.1 = (f32[1024,768]{1,0:T(8,128)S(1)}, f32[1024,128]{1,0:T(8,128)S(1)}, bf16[1024,3072]{1,0:T(8,128)(2,1)S(1)}, bf16[1024,3072]{1,0:T(8,128)(2,1)S(1)}, bf16[5,768,768]{2,1,0:T(8,128)(2,1)S(1)}) custom-call(s32[3]{0:T(128)S(1)} %pad_add_fusion.sc_ref, bf16[1024,768]{1,0:T(8,128)(2,1)S(1)} %copy-done.1, ...), custom_call_target="tpu_custom_call" | custom-call | flops 15399999488 | tf_op jit(solution)/shard_map/feed_in/pallas_call | solution.py:188
  94.2 2.1 %collective-permute-done.17 = bf16[8,192,384]{2,1,0:T(8,128)(2,1)S(1)} collective-permute-done((bf16[8,192,384]{2,1,0:T(8,128)(2,1)S(1)}, bf16[8,192,384]{2,1,0:T(8,128)(2,1)S(1)}, u32[]{:S(2)}, u32[]{:S(2)}) %collective-permute-start.17) | collective-permute-done | bytes 1179680 | tf_op jit(solution)/shard_map/ppermute | solution.py:345
  96.3 2.8 %collective-permute-done.20 = bf16[8,192,384]{2,1,0:T(8,128)(2,1)S(1)} collective-permute-done((bf16[8,192,384]{2,1,0:T(8,128)(2,1)S(1)}, bf16[8,192,384]{2,1,0:T(8,128)(2,1)S(1)}, u32[]{:S(2)}, u32[]{:S(2)}) %collective-permute-start.20) | collective-permute-done | bytes 1179680 | tf_op jit(solution)/shard_map/ppermute | solution.py:345
  99.1 23.4 %feed_out.1 = (bf16[1024,768]{1,0:T(8,128)(2,1)}, f32[1024,768]{1,0:T(8,128)}, bf16[768,1024]{1,0:T(8,128)(2,1)S(1)}) custom-call(s32[3]{0:T(128)S(1)} %pad_add_fusion.sc_ref, f32[1024,768]{1,0:T(8,128)S(1)} %get-tuple-element.106.n1_ref, f32[1024,128]{1,0:T(8,128)S(1)} %get-tuple-element.107.r1_ref, bf16[1024,3072]{1,0:T(8,128)(2,1)S(1)} %get-tuple-element.108.act_ref, ...), custom_call_target="tpu_custom_call" | custom-call | flops 26400000000 | tf_op jit(solution)/shard_map/feed_out/pallas_call | solution.py:224
  122.5 17.3 %attend_back.1 = (bf16[1024,2304]{1,0:T(8,128)(2,1)S(1)}, bf16[16,1024]{1,0:T(8,128)(2,1)S(1)}, f32[16,768]{1,0:T(8,128)S(1)}, f32[16,768]{1,0:T(8,128)S(1)}) custom-call(s32[3]{0:T(128)S(1)} %pad_add_fusion.sc_ref, bf16[1024,2304]{1,0:T(8,128)(2,1)} %copy-done.8, bf16[1024,2304]{1,0:T(8,128)(2,1)} %copy-done.8, bf16[1024,2304]{1,0:T(8,128)(2,1)} %copy-done.8, ...), custom_call_target="tpu_custom_call" | custom-call | flops 19800000512 | tf_op jit(solution)/shard_map/attend_back/pallas_call | solution.py:314
  140.0 1.2 collective-permute-done.21
  141.2 1.8 %collective-permute-start.24 = (f32[16,768]{1,0:T(8,128)S(1)}, f32[16,768]{1,0:T(8,128)S(1)}, u32[]{:S(2)}, u32[]{:S(2)}) collective-permute-start(f32[16,768]{1,0:T(8,128)S(1)} %add.63), channel_id=1, source_target_pairs={{0,6},{1,7},{2,4},{3,5},{4,2},{5,3},{6,0},{7,1},{8,14},{9,15},{10,... | collective-permute-start | bytes 147464 | tf_op jit(solution)/shard_map/ppermute | solution.py:345
  143.5 1.2 collective-permute-start.22
  144.7 1.6 %collective-permute-done.24 = f32[16,768]{1,0:T(8,128)S(1)} collective-permute-done((f32[16,768]{1,0:T(8,128)S(1)}, f32[16,768]{1,0:T(8,128)S(1)}, u32[]{:S(2)}, u32[]{:S(2)}) %collective-permute-start.24) | collective-permute-done | bytes 49184 | tf_op jit(solution)/shard_map/ppermute | solution.py:345
  147.6 3.1 %collective-permute-start.27 = (f32[16,768]{1,0:T(8,128)S(1)}, f32[16,768]{1,0:T(8,128)S(1)}, u32[]{:S(2)}, u32[]{:S(2)}) collective-permute-start(f32[16,768]{1,0:T(8,128)S(1)} %add_add_fusion.1), channel_id=1, source_target_pairs={{0,24},{1,25},{2,26},{3,27},{4,28},{5,29},{6,30},{7,31},{8,16},{9,... | collective-permute-start | bytes 147464 | tf_op jit(solution)/shard_map/ppermute | solution.py:345
  150.7 1.4 collective-permute-start.25
  152.0 5.7 %inputs_grad.1 = f32[1024,768]{1,0:T(8,128)} custom-call(f32[1024,768]{1,0:T(8,128)S(1)} %copy-done.7, bf16[1024,2304]{1,0:T(8,128)(2,1)S(1)} %get-tuple-element.122.d_ref, bf16[16,1024]{1,0:T(8,128)(2,1)S(1)} %get-tuple-element.123.gl, bf16[3,768,768]{2,1,0:T(8,128)(2,1)S(1)} %copy-done.6, bf16[16,768]{1,0:T(8,128)(2,1)S(1)} %get-tuple-element.125.dnt_ref), custom_call_target="tpu_custom_call" | custom-call | flops 7699999744 | tf_op jit(solution)/shard_map/inputs_grad/pallas_call | solution.py:335
  157.9 1.2 collective-permute-done.28.other_ref
  159.1 1.2 finish.1
  (124 shorter events, 13.4 us)
Async XLA Ops:
  3.9 14.0 %collective-permute-start.2 = (bf16[144,384]{1,0:T(8,128)(2,1)S(1)}, bf16[144,384]{1,0:T(8,128)(2,1)S(1)}, u32[]{:S(2)}, u32[]{:S(2)}) collective-permute-start(bf16[144,384]{1,0:T(8,128)(2,1)S(1)} %pad_maximum_fusion.5), channel_id=1, source_target_pairs={{0,24},{1,25},{2,26},{3,27},{4,28},{5,29},{6,30},{7,31},{8,16},{9,... | collective-permute-start | bytes 331784 | tf_op jit(solution)/shard_map/ppermute | solution.py:345
  8.9 9.6 %collective-permute-start.1 = (bf16[144,384]{1,0:T(8,128)(2,1)S(1)}, bf16[144,384]{1,0:T(8,128)(2,1)S(1)}, u32[]{:S(2)}, u32[]{:S(2)}) collective-permute-start(bf16[144,384]{1,0:T(8,128)(2,1)S(1)} %pad_maximum_fusion.5), channel_id=1, source_target_pairs={{0,16},{1,17},{2,18},{3,19},{4,20},{5,21},{6,22},{7,23},{8,24},{9,... | collective-permute-start | bytes 331784 | tf_op jit(solution)/shard_map/ppermute | solution.py:345
  8.9 9.6 %collective-permute-start = (bf16[144,384]{1,0:T(8,128)(2,1)S(1)}, bf16[144,384]{1,0:T(8,128)(2,1)S(1)}, u32[]{:S(2)}, u32[]{:S(2)}) collective-permute-start(bf16[144,384]{1,0:T(8,128)(2,1)S(1)} %pad_maximum_fusion.5), channel_id=1, source_target_pairs={{0,8},{1,9},{2,10},{3,11},{4,12},{5,13},{6,14},{7,15},{8,0},{9,1},... | collective-permute-start | bytes 331784 | tf_op jit(solution)/shard_map/ppermute | solution.py:345
  11.6 9.8 %collective-permute-start.5 = (bf16[192,384]{1,0:T(8,128)(2,1)S(1)}, bf16[192,384]{1,0:T(8,128)(2,1)S(1)}, u32[]{:S(2)}, u32[]{:S(2)}) collective-permute-start(bf16[192,384]{1,0:T(8,128)(2,1)S(1)} %bitcast.107), channel_id=1, source_target_pairs={{0,2},{1,5},{2,0},{3,7},{4,6},{5,1},{6,4},{7,3},{8,10},{9,13},{10,... | collective-permute-start | bytes 442376 | tf_op jit(solution)/shard_map/ppermute | solution.py:345
  18.5 11.0 %collective-permute-start.4 = (bf16[240,384]{1,0:T(8,128)(2,1)S(1)}, bf16[240,384]{1,0:T(8,128)(2,1)S(1)}, u32[]{:S(2)}, u32[]{:S(2)}) collective-permute-start(bf16[240,384]{1,0:T(8,128)(2,1)S(1)} %constant_dynamic-update-slice_fusion), channel_id=1, source_target_pairs={{0,16},{1,17},{2,18},{3,19},{4,20},{5,21},{6,22},{7,23},{8,24},{9,... | collective-permute-start | bytes 552968 | tf_op jit(solution)/shard_map/ppermute | solution.py:345
  20.2 9.3 %collective-permute-start.3 = (bf16[4,144,384]{2,1,0:T(8,128)(2,1)S(1)}, bf16[4,144,384]{2,1,0:T(8,128)(2,1)S(1)}, u32[]{:S(2)}, u32[]{:S(2)}) collective-permute-start(bf16[4,144,384]{2,1,0:T(8,128)(2,1)S(1)} %pad_maximum_fusion.2), channel_id=1, source_target_pairs={{0,2},{1,5},{2,0},{3,7},{4,6},{5,1},{6,4},{7,3},{8,10},{9,13},{10,... | collective-permute-start | bytes 1327112 | tf_op jit(solution)/shard_map/ppermute | solution.py:345
  29.6 13.6 %collective-permute-start.7 = (bf16[8,144,384]{2,1,0:T(8,128)(2,1)S(1)}, bf16[8,144,384]{2,1,0:T(8,128)(2,1)S(1)}, u32[]{:S(2)}, u32[]{:S(2)}) collective-permute-start(bf16[8,144,384]{2,1,0:T(8,128)(2,1)S(1)} %constant_dynamic-update-slice_fusion.5), channel_id=1, source_target_pairs={{0,1},{1,0},{2,3},{3,2},{4,5},{5,4},{6,7},{7,6},{8,9},{9,8},{10,11... | collective-permute-start | bytes 2654216 | tf_op jit(solution)/shard_map/ppermute | solution.py:345
  29.7 13.5 %collective-permute-start.6 = (bf16[8,144,384]{2,1,0:T(8,128)(2,1)S(1)}, bf16[8,144,384]{2,1,0:T(8,128)(2,1)S(1)}, u32[]{:S(2)}, u32[]{:S(2)}) collective-permute-start(bf16[8,144,384]{2,1,0:T(8,128)(2,1)S(1)} %constant_dynamic-update-slice_fusion.5), channel_id=1, source_target_pairs={{0,4},{1,3},{2,6},{3,1},{4,0},{5,7},{6,2},{7,5},{8,12},{9,11},{10,... | collective-permute-start | bytes 2654216 | tf_op jit(solution)/shard_map/ppermute | solution.py:345
  31.4 6.5 %collective-permute-start.9 = (bf16[240,384]{1,0:T(8,128)(2,1)S(1)}, bf16[240,384]{1,0:T(8,128)(2,1)S(1)}, u32[]{:S(2)}, u32[]{:S(2)}) collective-permute-start(bf16[240,384]{1,0:T(8,128)(2,1)S(1)} %constant_dynamic-update-slice_fusion), channel_id=1, source_target_pairs={{0,8},{1,9},{2,10},{3,11},{4,12},{5,13},{6,14},{7,15},{8,0},{9,1},... | collective-permute-start | bytes 552968 | tf_op jit(solution)/shard_map/ppermute | solution.py:345
  32.5 10.7 %collective-permute-start.8 = (bf16[240,384]{1,0:T(8,128)(2,1)S(1)}, bf16[240,384]{1,0:T(8,128)(2,1)S(1)}, u32[]{:S(2)}, u32[]{:S(2)}) collective-permute-start(bf16[240,384]{1,0:T(8,128)(2,1)S(1)} %constant_dynamic-update-slice_fusion), channel_id=1, source_target_pairs={{0,24},{1,25},{2,26},{3,27},{4,28},{5,29},{6,30},{7,31},{8,16},{9,... | collective-permute-start | bytes 552968 | tf_op jit(solution)/shard_map/ppermute | solution.py:345
  43.2 5.6 %collective-permute-start.11 = (bf16[8,144,384]{2,1,0:T(8,128)(2,1)S(1)}, bf16[8,144,384]{2,1,0:T(8,128)(2,1)S(1)}, u32[]{:S(2)}, u32[]{:S(2)}) collective-permute-start(bf16[8,144,384]{2,1,0:T(8,128)(2,1)S(1)} %collective-permute-done.6), channel_id=1, source_target_pairs={{0,1},{1,0},{2,3},{3,2},{4,5},{5,4},{6,7},{7,6},{8,9},{9,8},{10,11... | collective-permute-start | bytes 2654216 | tf_op jit(solution)/shard_map/ppermute | solution.py:345
  43.3 30.5 %collective-permute-start.16 = (bf16[2,192,384]{2,1,0:T(8,128)(2,1)S(1)}, bf16[2,192,384]{2,1,0:T(8,128)(2,1)S(1)}, u32[]{:S(2)}, u32[]{:S(2)}) collective-permute-start(bf16[2,192,384]{2,1,0:T(8,128)(2,1)S(1)} %pad_maximum_fusion.3), channel_id=1, source_target_pairs={{0,24},{1,25},{2,26},{3,27},{4,28},{5,29},{6,30},{7,31},{8,16},{9,... | collective-permute-start | bytes 884744 | tf_op jit(solution)/shard_map/ppermute | solution.py:345
  45.9 27.9 %collective-permute-start.15 = (bf16[2,192,384]{2,1,0:T(8,128)(2,1)S(1)}, bf16[2,192,384]{2,1,0:T(8,128)(2,1)S(1)}, u32[]{:S(2)}, u32[]{:S(2)}) collective-permute-start(bf16[2,192,384]{2,1,0:T(8,128)(2,1)S(1)} %pad_maximum_fusion.3), channel_id=1, source_target_pairs={{0,16},{1,17},{2,18},{3,19},{4,20},{5,21},{6,22},{7,23},{8,24},{9,... | collective-permute-start | bytes 884744 | tf_op jit(solution)/shard_map/ppermute | solution.py:345
  45.9 27.9 %collective-permute-start.14 = (bf16[2,192,384]{2,1,0:T(8,128)(2,1)S(1)}, bf16[2,192,384]{2,1,0:T(8,128)(2,1)S(1)}, u32[]{:S(2)}, u32[]{:S(2)}) collective-permute-start(bf16[2,192,384]{2,1,0:T(8,128)(2,1)S(1)} %pad_maximum_fusion.3), channel_id=1, source_target_pairs={{0,8},{1,9},{2,10},{3,11},{4,12},{5,13},{6,14},{7,15},{8,0},{9,1},... | collective-permute-start | bytes 884744 | tf_op jit(solution)/shard_map/ppermute | solution.py:345
  47.8 11.5 %collective-permute-start.10 = (bf16[4,240,384]{2,1,0:T(8,128)(2,1)S(1)}, bf16[4,240,384]{2,1,0:T(8,128)(2,1)S(1)}, u32[]{:S(2)}, u32[]{:S(2)}) collective-permute-start(bf16[4,240,384]{2,1,0:T(8,128)(2,1)S(1)} %pad_maximum_fusion.1), channel_id=1, source_target_pairs={{0,2},{1,5},{2,0},{3,7},{4,6},{5,1},{6,4},{7,3},{8,10},{9,13},{10,... | collective-permute-start | bytes 2211848 | tf_op jit(solution)/shard_map/ppermute | solution.py:345
  59.5 14.3 %collective-permute-start.13 = (bf16[8,240,384]{2,1,0:T(8,128)(2,1)S(1)}, bf16[8,240,384]{2,1,0:T(8,128)(2,1)S(1)}, u32[]{:S(2)}, u32[]{:S(2)}) collective-permute-start(bf16[8,240,384]{2,1,0:T(8,128)(2,1)S(1)} %constant_dynamic-update-slice_fusion.15), channel_id=1, source_target_pairs={{0,1},{1,0},{2,3},{3,2},{4,5},{5,4},{6,7},{7,6},{8,9},{9,8},{10,11... | collective-permute-start | bytes 4423688 | tf_op jit(solution)/shard_map/ppermute | solution.py:345
  59.6 19.4 %collective-permute-start.12 = (bf16[8,240,384]{2,1,0:T(8,128)(2,1)S(1)}, bf16[8,240,384]{2,1,0:T(8,128)(2,1)S(1)}, u32[]{:S(2)}, u32[]{:S(2)}) collective-permute-start(bf16[8,240,384]{2,1,0:T(8,128)(2,1)S(1)} %constant_dynamic-update-slice_fusion.15), channel_id=1, source_target_pairs={{0,4},{1,3},{2,6},{3,1},{4,0},{5,7},{6,2},{7,5},{8,12},{9,11},{10,... | collective-permute-start | bytes 4423688 | tf_op jit(solution)/shard_map/ppermute | solution.py:345
  79.0 3.3 %collective-permute-start.18 = (bf16[8,240,384]{2,1,0:T(8,128)(2,1)S(1)}, bf16[8,240,384]{2,1,0:T(8,128)(2,1)S(1)}, u32[]{:S(2)}, u32[]{:S(2)}) collective-permute-start(bf16[8,240,384]{2,1,0:T(8,128)(2,1)S(1)} %collective-permute-done.12), channel_id=1, source_target_pairs={{0,1},{1,0},{2,3},{3,2},{4,5},{5,4},{6,7},{7,6},{8,9},{9,8},{10,11... | collective-permute-start | bytes 4423688 | tf_op jit(solution)/shard_map/ppermute | solution.py:345
  79.5 14.7 %collective-permute-start.19 = (bf16[8,192,384]{2,1,0:T(8,128)(2,1)S(1)}, bf16[8,192,384]{2,1,0:T(8,128)(2,1)S(1)}, u32[]{:S(2)}, u32[]{:S(2)}) collective-permute-start(bf16[8,192,384]{2,1,0:T(8,128)(2,1)S(1)} %bitcast.71), channel_id=1, source_target_pairs={{0,1},{1,0},{2,3},{3,2},{4,5},{5,4},{6,7},{7,6},{8,9},{9,8},{10,11... | collective-permute-start | bytes 3538952 | tf_op jit(solution)/shard_map/ppermute | solution.py:345
  80.1 16.2 %collective-permute-start.17 = (bf16[8,192,384]{2,1,0:T(8,128)(2,1)S(1)}, bf16[8,192,384]{2,1,0:T(8,128)(2,1)S(1)}, u32[]{:S(2)}, u32[]{:S(2)}) collective-permute-start(bf16[8,192,384]{2,1,0:T(8,128)(2,1)S(1)} %bitcast.72), channel_id=1, source_target_pairs={{0,4},{1,3},{2,6},{3,1},{4,0},{5,7},{6,2},{7,5},{8,12},{9,11},{10,... | collective-permute-start | bytes 3538952 | tf_op jit(solution)/shard_map/ppermute | solution.py:345
  96.3 2.8 %collective-permute-start.20 = (bf16[8,192,384]{2,1,0:T(8,128)(2,1)S(1)}, bf16[8,192,384]{2,1,0:T(8,128)(2,1)S(1)}, u32[]{:S(2)}, u32[]{:S(2)}) collective-permute-start(bf16[8,192,384]{2,1,0:T(8,128)(2,1)S(1)} %collective-permute-done.17), channel_id=1, source_target_pairs={{0,1},{1,0},{2,3},{3,2},{4,5},{5,4},{6,7},{7,6},{8,9},{9,8},{10,11... | collective-permute-start | bytes 3538952 | tf_op jit(solution)/shard_map/ppermute | solution.py:345
  99.1 23.4 %copy-start.9 = (f32[6,8,512]{2,1,0:T(8,128)S(1)}, f32[6,8,512]{2,1,0:T(8,128)}, u32[]{:S(2)}) copy-start(f32[6,8,512]{2,1,0:T(8,128)} %get-tuple-element.116.rt_ref) | copy-start | bytes 294916
  122.5 29.5 %copy-start.6 = (bf16[3,768,768]{2,1,0:T(8,128)(2,1)S(1)}, bf16[3,768,768]{2,1,0:T(8,128)(2,1)}, u32[]{:S(2)}) copy-start(bf16[3,768,768]{2,1,0:T(8,128)(2,1)} %get-tuple-element.124.w_ref) | copy-start | bytes 10616836
  122.5 29.5 %copy-start.7 = (f32[1024,768]{1,0:T(8,128)S(1)}, f32[1024,768]{1,0:T(8,128)}, u32[]{:S(2)}) copy-start(f32[1024,768]{1,0:T(8,128)} %get-tuple-element.121.gfs_ref) | copy-start | bytes 9437188
  139.8 1.3 collective-permute-start.21
  141.2 5.2 %collective-permute-start.24 = (f32[16,768]{1,0:T(8,128)S(1)}, f32[16,768]{1,0:T(8,128)S(1)}, u32[]{:S(2)}, u32[]{:S(2)}) collective-permute-start(f32[16,768]{1,0:T(8,128)S(1)} %add.63), channel_id=1, source_target_pairs={{0,6},{1,7},{2,4},{3,5},{4,2},{5,3},{6,0},{7,1},{8,14},{9,15},{10,... | collective-permute-start | bytes 147464 | tf_op jit(solution)/shard_map/ppermute | solution.py:345
  143.0 4.1 %collective-permute-start.23 = (f32[16,768]{1,0:T(8,128)S(1)}, f32[16,768]{1,0:T(8,128)S(1)}, u32[]{:S(2)}, u32[]{:S(2)}) collective-permute-start(f32[16,768]{1,0:T(8,128)S(1)} %add.63), channel_id=1, source_target_pairs={{0,4},{1,5},{2,6},{3,7},{4,0},{5,1},{6,2},{7,3},{8,12},{9,13},{10,... | collective-permute-start | bytes 147464 | tf_op jit(solution)/shard_map/ppermute | solution.py:345
  143.5 4.1 %collective-permute-start.22 = (f32[16,768]{1,0:T(8,128)S(1)}, f32[16,768]{1,0:T(8,128)S(1)}, u32[]{:S(2)}, u32[]{:S(2)}) collective-permute-start(f32[16,768]{1,0:T(8,128)S(1)} %add.63), channel_id=1, source_target_pairs={{0,2},{1,3},{2,0},{3,1},{4,6},{5,7},{6,4},{7,5},{8,10},{9,11},{10,... | collective-permute-start | bytes 147464 | tf_op jit(solution)/shard_map/ppermute | solution.py:345
  147.6 10.2 %collective-permute-start.27 = (f32[16,768]{1,0:T(8,128)S(1)}, f32[16,768]{1,0:T(8,128)S(1)}, u32[]{:S(2)}, u32[]{:S(2)}) collective-permute-start(f32[16,768]{1,0:T(8,128)S(1)} %add_add_fusion.1), channel_id=1, source_target_pairs={{0,24},{1,25},{2,26},{3,27},{4,28},{5,29},{6,30},{7,31},{8,16},{9,... | collective-permute-start | bytes 147464 | tf_op jit(solution)/shard_map/ppermute | solution.py:345
  150.7 7.1 %collective-permute-start.26 = (f32[16,768]{1,0:T(8,128)S(1)}, f32[16,768]{1,0:T(8,128)S(1)}, u32[]{:S(2)}, u32[]{:S(2)}) collective-permute-start(f32[16,768]{1,0:T(8,128)S(1)} %add_add_fusion.1), channel_id=1, source_target_pairs={{0,16},{1,17},{2,18},{3,19},{4,20},{5,21},{6,22},{7,23},{8,24},{9,... | collective-permute-start | bytes 147464 | tf_op jit(solution)/shard_map/ppermute | solution.py:345
  150.7 7.1 %collective-permute-start.25 = (f32[16,768]{1,0:T(8,128)S(1)}, f32[16,768]{1,0:T(8,128)S(1)}, u32[]{:S(2)}, u32[]{:S(2)}) collective-permute-start(f32[16,768]{1,0:T(8,128)S(1)} %add_add_fusion.1), channel_id=1, source_target_pairs={{0,8},{1,9},{2,10},{3,11},{4,12},{5,13},{6,14},{7,15},{8,0},{9,1},... | collective-permute-start | bytes 147464 | tf_op jit(solution)/shard_map/ppermute | solution.py:345
  157.8 1.3 collective-permute-start.28
  (15 other events, 196.1 us)

commit v5 on v4

--- a/solution.py
+++ b/solution.py
@@ -409,25 +409,28 @@
     z1,s2,dn,scalars=tie(z1,s2,dn,scalars)
     a1=jnp.stack(z1,0)
     n1=near_hop(a1)
-    z22=exchange(s2,2*top)
-    n1,z22,s2,n3=tie(n1,z22,s2,n3)
+    z2=exchange(s2,2*top)
+    n1,z2,s2,n3=tie(n1,z2,s2,n3)
     f1=jnp.concatenate([a1,n1],0)
     h1=far_hop(f1); of1=exchange(f1,1)
-    z23=exchange(s2,3*top); z21=exchange(s2,top)
-    h1,of1,z23,z21,n3=tie(h1,of1,z23,z21,n3)
+    y2=exchange(jnp.stack([s2,z2],0),top)
+    h1,of1,y2,n3=tie(h1,of1,y2,n3)
     oh1=exchange(h1,1)
-    a2=jnp.stack([s2,z21,z22,z23],0)
+    a2=jnp.stack([s2,y2[0],z2,y2[1]],0)
     n2=near_hop(a2)
-    z3=along_z(jnp.stack([s3,n3],0))
+    b3=jnp.stack([s3,n3],0)
+    z3=exchange(b3,2*top)
     oh1,=tie(oh1)
     qkv,low,wqkv=project(scalars,x,dn,upq,upv,in_bands(3,f1,h1,of1,oh1))
     n2,qkv=tie(n2,qkv)
+    z3,_=tie(z3,n2)
     f2=jnp.concatenate([a2,n2],0)
     h2=far_hop(f2); of2=exchange(f2,1)
+    y3=exchange(jnp.stack([b3,z3],0),top)
     e,ot,o,rt=attend(scalars,qkv,x.shape[0]//SLOT)
-    h2,o,of2,z3=tie(h2,o,of2,z3)
+    h2,o,of2,y3=tie(h2,o,of2,y3)
     oh2=exchange(h2,1)
-    f3=jnp.stack(z3,1).reshape(8,-1,D//2)
+    f3=jnp.stack([b3,y3[0],z3,y3[1]],1).reshape(8,-1,D//2)
     h3=far_hop(f3); of3=exchange(f3,1)
     oh2,=tie(oh2)
     nn,r1,act,gp,w=feed_in(scalars,x,o,nm,in_bands(1+bands,f2,h2,of2,oh2),FF)

time: 160 us -> 157 us (0.981)
  starting transfers between devices: 31.3 us -> 26.4 us
    ppermute x29 -> x27, starting transfers between devices: 31.3 us -> 26.4 us  [permute(): lax.ppermute(v, AXES, [(i, target(i)) for i in range(device_count())])]
    ppermute x29 -> x27, waiting for transfers between devices: 37.4 us -> 38.5 us  [permute(): lax.ppermute(v, AXES, [(i, target(i)) for i in range(device_count())])]
  transfers between devices with their start and end apart: 29 -> 27, of which waited for: 14 -> 16; matrix products, arithmetic and copies ran while one was open for 1% -> 1% of each run, Pallas kernels for 24% -> 24%
where the time goes in v5:
time: 157 us
  Pallas kernels  79.7 us (51%)
  waiting for transfers between devices  38.5 us (25%)
  starting transfers between devices  26.4 us (17%)
  blocking collectives  7.94 us (5%)
  other arithmetic  1.84 us (1%)
    ppermute x27, waiting for transfers between devices, permute(): lax.ppermute(v, AXES, [(i, target(i)) for i in range(device_count())])  38.5 us
    ppermute x27, starting transfers between devices, permute(): lax.ppermute(v, AXES, [(i, target(i)) for i in range(device_count())])  26.4 us
    pallas_call x1, Pallas kernels, feed_out(): pl.pallas_call(feed_out_kernel, grid=(rows // SLOT,), in_specs=[SCALARS,...  23.4 us
    pallas_call x1, Pallas kernels, attend_back(): pl.pallas_call(attend_back_kernel, grid=(S, J), in_specs=[SCALARS, *[pl.B...  17.3 us
    pallas_call x1, Pallas kernels, attend(): pl.pallas_call(attend_kernel, grid=(slots, J), in_specs=[SCALARS, HELD],...  13.1 us
    pallas_call x1, Pallas kernels, feed_in(): pl.pallas_call(feed_in_kernel, in_specs=[SCALARS, HELD, HELD, HELD] + [AN...  11.9 us
    all_gather x4, blocking collectives, core_pair(): lax.all_gather(v, 'fsdp', axis=0, tiled=False, axis_index_groups=groups)  7.94 us
    pallas_call x1, Pallas kernels, project(): pl.pallas_call(project_kernel, in_specs=[SCALARS, HELD, HELD, HELD, HELD]...  6.99 us
  transfers between devices with their start and end apart: 27, of which 16 were waited for; matrix products, arithmetic and copies ran while one was open for 1% of the time, Pallas kernels for 24%

profile of v5, /device:TPU:0, one launch (start us, length us, event | category | flops | bytes accessed | tf_op | source)
XLA Modules:
  0.0 156.8 jit_solution(6897008465867000273)
XLA Ops:
  1.7 2.1 %all-gather = bf16[144,768]{1,0:T(8,128)(2,1)S(1)} all-gather(bf16[72,768]{1,0:T(8,128)(2,1)S(1)} %pad_maximum_fusion.6), channel_id=2, replica_groups={{0,1},{2,3},{4,5},{6,7},{8,9},{10,11},{12,13},{14,15},{16,17},{18,19},{..., dimensions={0}, use_global_device_ids=true | all-gather | bytes 331776 | tf_op jit(solution)/shard_map/all_gather | solution.py:365
  3.9 5.0 %collective-permute-start.2 = (bf16[144,384]{1,0:T(8,128)(2,1)S(1)}, bf16[144,384]{1,0:T(8,128)(2,1)S(1)}, u32[]{:S(2)}, u32[]{:S(2)}) collective-permute-start(bf16[144,384]{1,0:T(8,128)(2,1)S(1)} %pad_maximum_fusion.7), channel_id=1, source_target_pairs={{0,24},{1,25},{2,26},{3,27},{4,28},{5,29},{6,30},{7,31},{8,16},{9,... | collective-permute-start | bytes 331784 | tf_op jit(solution)/shard_map/ppermute | solution.py:345
  9.5 2.0 %all-gather.3 = bf16[192,768]{1,0:T(8,128)(2,1)S(1)} all-gather(bf16[96,768]{1,0:T(8,128)(2,1)S(1)} %copy-done.10), channel_id=5, replica_groups={{0,1},{2,3},{4,5},{6,7},{8,9},{10,11},{12,13},{14,15},{16,17},{18,19},{..., dimensions={0}, use_global_device_ids=true | all-gather | bytes 442368 | tf_op jit(solution)/shard_map/all_gather | solution.py:365
  11.6 1.7 %collective-permute-start.5 = (bf16[192,384]{1,0:T(8,128)(2,1)S(1)}, bf16[192,384]{1,0:T(8,128)(2,1)S(1)}, u32[]{:S(2)}, u32[]{:S(2)}) collective-permute-start(bf16[192,384]{1,0:T(8,128)(2,1)S(1)} %bitcast.110), channel_id=1, source_target_pairs={{0,2},{1,5},{2,0},{3,7},{4,6},{5,1},{6,4},{7,3},{8,10},{9,13},{10,... | collective-permute-start | bytes 442376 | tf_op jit(solution)/shard_map/ppermute | solution.py:345
  13.6 1.9 %all-gather.1 = bf16[48,768]{1,0:T(8,128)(2,1)S(1)} all-gather(bf16[24,768]{1,0:T(8,128)(2,1)S(1)} %copy-done.12), channel_id=3, replica_groups={{0,1},{2,3},{4,5},{6,7},{8,9},{10,11},{12,13},{14,15},{16,17},{18,19},{..., dimensions={0}, use_global_device_ids=true | all-gather | bytes 110592 | tf_op jit(solution)/shard_map/all_gather | solution.py:365
  15.4 2.0 %all-gather.2 = bf16[48,3072]{1,0:T(8,128)(2,1)S(1)} all-gather(bf16[24,3072]{1,0:T(8,128)(2,1)S(1)} %copy-done.11), channel_id=4, replica_groups={{0,1},{2,3},{4,5},{6,7},{8,9},{10,11},{12,13},{14,15},{16,17},{18,19},{..., dimensions={0}, use_global_device_ids=true | all-gather | bytes 442368 | tf_op jit(solution)/shard_map/all_gather | solution.py:365
  18.5 1.6 %collective-permute-start.4 = (bf16[240,384]{1,0:T(8,128)(2,1)S(1)}, bf16[240,384]{1,0:T(8,128)(2,1)S(1)}, u32[]{:S(2)}, u32[]{:S(2)}) collective-permute-start(bf16[240,384]{1,0:T(8,128)(2,1)S(1)} %constant_dynamic-update-slice_fusion), channel_id=1, source_target_pairs={{0,16},{1,17},{2,18},{3,19},{4,20},{5,21},{6,22},{7,23},{8,24},{9,... | collective-permute-start | bytes 552968 | tf_op jit(solution)/shard_map/ppermute | solution.py:345
  20.2 1.1 collective-permute-start.3
  21.4 8.1 %collective-permute-done.4 = bf16[240,384]{1,0:T(8,128)(2,1)S(1)} collective-permute-done((bf16[240,384]{1,0:T(8,128)(2,1)S(1)}, bf16[240,384]{1,0:T(8,128)(2,1)S(1)}, u32[]{:S(2)}, u32[]{:S(2)}) %collective-permute-start.4) | collective-permute-done | bytes 184352 | tf_op jit(solution)/shard_map/ppermute | solution.py:345
  29.7 1.6 %collective-permute-start.6 = (bf16[8,144,384]{2,1,0:T(8,128)(2,1)S(1)}, bf16[8,144,384]{2,1,0:T(8,128)(2,1)S(1)}, u32[]{:S(2)}, u32[]{:S(2)}) collective-permute-start(bf16[8,144,384]{2,1,0:T(8,128)(2,1)S(1)} %constant_dynamic-update-slice_fusion.5), channel_id=1, source_target_pairs={{0,4},{1,3},{2,6},{3,1},{4,0},{5,7},{6,2},{7,5},{8,12},{9,11},{10,... | collective-permute-start | bytes 2654216 | tf_op jit(solution)/shard_map/ppermute | solution.py:345
  31.4 1.1 collective-permute-start.8
  32.7 9.1 %collective-permute-done.8 = bf16[2,240,384]{2,1,0:T(8,128)(2,1)S(1)} collective-permute-done((bf16[2,240,384]{2,1,0:T(8,128)(2,1)S(1)}, bf16[2,240,384]{2,1,0:T(8,128)(2,1)S(1)}, u32[]{:S(2)}, u32[]{:S(2)}) %collective-permute-start.8) | collective-permute-done | bytes 368672 | tf_op jit(solution)/shard_map/ppermute | solution.py:345
  45.2 7.0 %project.1 = (bf16[1024,2304]{1,0:T(8,128)(2,1)S(1)}, bf16[32,1024]{1,0:T(8,128)(2,1)S(1)}, bf16[3,768,768]{2,1,0:T(8,128)(2,1)}) custom-call(s32[3]{0:T(128)S(1)} %pad_add_fusion.sc_ref, bf16[1024,768]{1,0:T(8,128)(2,1)S(1)} %copy-done.1, bf16[768,128]{1,0:T(8,128)(2,1)S(1)} %get-tuple-element.84.dn_ref, bf16[128,768]{1,0:T(8,128)(2,1)S(1)} %get-tuple-element.85.upq_ref, ...), custom_call_target="tpu_custom_call" | custom-call | flops 8800000000 | tf_op jit(solution)/shard_map/project/pallas_call | solution.py:96
  52.2 3.3 %collective-permute-done.9 = bf16[4,240,384]{2,1,0:T(8,128)(2,1)S(1)} collective-permute-done((bf16[4,240,384]{2,1,0:T(8,128)(2,1)S(1)}, bf16[4,240,384]{2,1,0:T(8,128)(2,1)S(1)}, u32[]{:S(2)}, u32[]{:S(2)}) %collective-permute-start.9) | collective-permute-done | bytes 737312 | tf_op jit(solution)/shard_map/ppermute | solution.py:345
  55.8 1.1 collective-permute-start.11
  56.9 2.7 %collective-permute-done.13 = bf16[2,192,384]{2,1,0:T(8,128)(2,1)S(1)} collective-permute-done((bf16[2,192,384]{2,1,0:T(8,128)(2,1)S(1)}, bf16[2,192,384]{2,1,0:T(8,128)(2,1)S(1)}, u32[]{:S(2)}, u32[]{:S(2)}) %collective-permute-start.13) | collective-permute-done | bytes 294944 | tf_op jit(solution)/shard_map/ppermute | solution.py:345
  60.2 13.1 %attend.1 = (bf16[24,512,512]{2,1,0:T(8,128)(2,1)}, bf16[1536,512]{1,0:T(8,128)(2,1)}, bf16[1024,768]{1,0:T(8,128)(2,1)S(1)}, f32[6,8,512]{2,1,0:T(8,128)}) custom-call(s32[3]{0:T(128)S(1)} %pad_add_fusion.sc_ref, bf16[1024,2304]{1,0:T(8,128)(2,1)S(1)} %get-tuple-element.91.qkv_ref.q_ref.k_ref.v_ref), custom_call_target="tpu_custom_call" | custom-call | flops 17600000000 | tf_op jit(solution)/shard_map/attend/pallas_call | solution.py:145
  73.3 1.4 collective-permute-done.14
  77.4 1.1 collective-permute-done.16
  78.5 11.9 %feed_in.1 = (f32[1024,768]{1,0:T(8,128)S(1)}, f32[1024,128]{1,0:T(8,128)S(1)}, bf16[1024,3072]{1,0:T(8,128)(2,1)S(1)}, bf16[1024,3072]{1,0:T(8,128)(2,1)S(1)}, bf16[5,768,768]{2,1,0:T(8,128)(2,1)S(1)}) custom-call(s32[3]{0:T(128)S(1)} %pad_add_fusion.sc_ref, bf16[1024,768]{1,0:T(8,128)(2,1)S(1)} %copy-done.1, ...), custom_call_target="tpu_custom_call" | custom-call | flops 15399999488 | tf_op jit(solution)/shard_map/feed_in/pallas_call | solution.py:188
  90.4 2.2 %collective-permute-done.15 = bf16[8,192,384]{2,1,0:T(8,128)(2,1)S(1)} collective-permute-done((bf16[8,192,384]{2,1,0:T(8,128)(2,1)S(1)}, bf16[8,192,384]{2,1,0:T(8,128)(2,1)S(1)}, u32[]{:S(2)}, u32[]{:S(2)}) %collective-permute-start.15) | collective-permute-done | bytes 1179680 | tf_op jit(solution)/shard_map/ppermute | solution.py:345
  92.5 2.8 %collective-permute-done.18 = bf16[8,192,384]{2,1,0:T(8,128)(2,1)S(1)} collective-permute-done((bf16[8,192,384]{2,1,0:T(8,128)(2,1)S(1)}, bf16[8,192,384]{2,1,0:T(8,128)(2,1)S(1)}, u32[]{:S(2)}, u32[]{:S(2)}) %collective-permute-start.18) | collective-permute-done | bytes 1179680 | tf_op jit(solution)/shard_map/ppermute | solution.py:345
  95.4 23.4 %feed_out.1 = (bf16[1024,768]{1,0:T(8,128)(2,1)}, f32[1024,768]{1,0:T(8,128)}, bf16[768,1024]{1,0:T(8,128)(2,1)S(1)}) custom-call(s32[3]{0:T(128)S(1)} %pad_add_fusion.sc_ref, f32[1024,768]{1,0:T(8,128)S(1)} %get-tuple-element.100.n1_ref, f32[1024,128]{1,0:T(8,128)S(1)} %get-tuple-element.101.r1_ref, bf16[1024,3072]{1,0:T(8,128)(2,1)S(1)} %get-tuple-element.102.act_ref, ...), custom_call_target="tpu_custom_call" | custom-call | flops 26400000000 | tf_op jit(solution)/shard_map/feed_out/pallas_call | solution.py:224
  118.8 17.3 %attend_back.1 = (bf16[1024,2304]{1,0:T(8,128)(2,1)S(1)}, bf16[16,1024]{1,0:T(8,128)(2,1)S(1)}, f32[16,768]{1,0:T(8,128)S(1)}, f32[16,768]{1,0:T(8,128)S(1)}) custom-call(s32[3]{0:T(128)S(1)} %pad_add_fusion.sc_ref, bf16[1024,2304]{1,0:T(8,128)(2,1)} %copy-done.8, bf16[1024,2304]{1,0:T(8,128)(2,1)} %copy-done.8, bf16[1024,2304]{1,0:T(8,128)(2,1)} %copy-done.8, ...), custom_call_target="tpu_custom_call" | custom-call | flops 19800000512 | tf_op jit(solution)/shard_map/attend_back/pallas_call | solution.py:314
  136.2 1.2 collective-permute-done.19
  137.4 2.0 %collective-permute-start.22 = (f32[16,768]{1,0:T(8,128)S(1)}, f32[16,768]{1,0:T(8,128)S(1)}, u32[]{:S(2)}, u32[]{:S(2)}) collective-permute-start(f32[16,768]{1,0:T(8,128)S(1)} %add.63), channel_id=1, source_target_pairs={{0,6},{1,7},{2,4},{3,5},{4,2},{5,3},{6,0},{7,1},{8,14},{9,15},{10,... | collective-permute-start | bytes 147464 | tf_op jit(solution)/shard_map/ppermute | solution.py:345
  141.0 1.6 %collective-permute-done.22 = f32[16,768]{1,0:T(8,128)S(1)} collective-permute-done((f32[16,768]{1,0:T(8,128)S(1)}, f32[16,768]{1,0:T(8,128)S(1)}, u32[]{:S(2)}, u32[]{:S(2)}) %collective-permute-start.22) | collective-permute-done | bytes 49184 | tf_op jit(solution)/shard_map/ppermute | solution.py:345
  144.1 2.6 %collective-permute-start.25 = (f32[16,768]{1,0:T(8,128)S(1)}, f32[16,768]{1,0:T(8,128)S(1)}, u32[]{:S(2)}, u32[]{:S(2)}) collective-permute-start(f32[16,768]{1,0:T(8,128)S(1)} %add_add_fusion.1), channel_id=1, source_target_pairs={{0,24},{1,25},{2,26},{3,27},{4,28},{5,29},{6,30},{7,31},{8,16},{9,... | collective-permute-start | bytes 147464 | tf_op jit(solution)/shard_map/ppermute | solution.py:345
  146.7 1.8 %collective-permute-start.24 = (f32[16,768]{1,0:T(8,128)S(1)}, f32[16,768]{1,0:T(8,128)S(1)}, u32[]{:S(2)}, u32[]{:S(2)}) collective-permute-start(f32[16,768]{1,0:T(8,128)S(1)} %add_add_fusion.1), channel_id=1, source_target_pairs={{0,16},{1,17},{2,18},{3,19},{4,20},{5,21},{6,22},{7,23},{8,24},{9,... | collective-permute-start | bytes 147464 | tf_op jit(solution)/shard_map/ppermute | solution.py:345
  148.5 5.7 %inputs_grad.1 = f32[1024,768]{1,0:T(8,128)} custom-call(f32[1024,768]{1,0:T(8,128)S(1)} %copy-done.7, bf16[1024,2304]{1,0:T(8,128)(2,1)S(1)} %get-tuple-element.116.d_ref, bf16[16,1024]{1,0:T(8,128)(2,1)S(1)} %get-tuple-element.117.gl, bf16[3,768,768]{2,1,0:T(8,128)(2,1)S(1)} %copy-done.6, bf16[16,768]{1,0:T(8,128)(2,1)S(1)} %get-tuple-element.119.dnt_ref), custom_call_target="tpu_custom_call" | custom-call | flops 7699999744 | tf_op jit(solution)/shard_map/inputs_grad/pallas_call | solution.py:335
  154.4 1.2 collective-permute-done.26.other_ref
  155.6 1.2 finish.1
  (123 shorter events, 13.5 us)
Async XLA Ops:
  3.9 14.0 %collective-permute-start.2 = (bf16[144,384]{1,0:T(8,128)(2,1)S(1)}, bf16[144,384]{1,0:T(8,128)(2,1)S(1)}, u32[]{:S(2)}, u32[]{:S(2)}) collective-permute-start(bf16[144,384]{1,0:T(8,128)(2,1)S(1)} %pad_maximum_fusion.7), channel_id=1, source_target_pairs={{0,24},{1,25},{2,26},{3,27},{4,28},{5,29},{6,30},{7,31},{8,16},{9,... | collective-permute-start | bytes 331784 | tf_op jit(solution)/shard_map/ppermute | solution.py:345
  8.9 9.6 %collective-permute-start.1 = (bf16[144,384]{1,0:T(8,128)(2,1)S(1)}, bf16[144,384]{1,0:T(8,128)(2,1)S(1)}, u32[]{:S(2)}, u32[]{:S(2)}) collective-permute-start(bf16[144,384]{1,0:T(8,128)(2,1)S(1)} %pad_maximum_fusion.7), channel_id=1, source_target_pairs={{0,16},{1,17},{2,18},{3,19},{4,20},{5,21},{6,22},{7,23},{8,24},{9,... | collective-permute-start | bytes 331784 | tf_op jit(solution)/shard_map/ppermute | solution.py:345
  8.9 9.6 %collective-permute-start = (bf16[144,384]{1,0:T(8,128)(2,1)S(1)}, bf16[144,384]{1,0:T(8,128)(2,1)S(1)}, u32[]{:S(2)}, u32[]{:S(2)}) collective-permute-start(bf16[144,384]{1,0:T(8,128)(2,1)S(1)} %pad_maximum_fusion.7), channel_id=1, source_target_pairs={{0,8},{1,9},{2,10},{3,11},{4,12},{5,13},{6,14},{7,15},{8,0},{9,1},... | collective-permute-start | bytes 331784 | tf_op jit(solution)/shard_map/ppermute | solution.py:345
  11.6 9.8 %collective-permute-start.5 = (bf16[192,384]{1,0:T(8,128)(2,1)S(1)}, bf16[192,384]{1,0:T(8,128)(2,1)S(1)}, u32[]{:S(2)}, u32[]{:S(2)}) collective-permute-start(bf16[192,384]{1,0:T(8,128)(2,1)S(1)} %bitcast.110), channel_id=1, source_target_pairs={{0,2},{1,5},{2,0},{3,7},{4,6},{5,1},{6,4},{7,3},{8,10},{9,13},{10,... | collective-permute-start | bytes 442376 | tf_op jit(solution)/shard_map/ppermute | solution.py:345
  18.5 11.0 %collective-permute-start.4 = (bf16[240,384]{1,0:T(8,128)(2,1)S(1)}, bf16[240,384]{1,0:T(8,128)(2,1)S(1)}, u32[]{:S(2)}, u32[]{:S(2)}) collective-permute-start(bf16[240,384]{1,0:T(8,128)(2,1)S(1)} %constant_dynamic-update-slice_fusion), channel_id=1, source_target_pairs={{0,16},{1,17},{2,18},{3,19},{4,20},{5,21},{6,22},{7,23},{8,24},{9,... | collective-permute-start | bytes 552968 | tf_op jit(solution)/shard_map/ppermute | solution.py:345
  20.2 9.3 %collective-permute-start.3 = (bf16[4,144,384]{2,1,0:T(8,128)(2,1)S(1)}, bf16[4,144,384]{2,1,0:T(8,128)(2,1)S(1)}, u32[]{:S(2)}, u32[]{:S(2)}) collective-permute-start(bf16[4,144,384]{2,1,0:T(8,128)(2,1)S(1)} %pad_maximum_fusion.3), channel_id=1, source_target_pairs={{0,2},{1,5},{2,0},{3,7},{4,6},{5,1},{6,4},{7,3},{8,10},{9,13},{10,... | collective-permute-start | bytes 1327112 | tf_op jit(solution)/shard_map/ppermute | solution.py:345
  29.6 12.2 %collective-permute-start.7 = (bf16[8,144,384]{2,1,0:T(8,128)(2,1)S(1)}, bf16[8,144,384]{2,1,0:T(8,128)(2,1)S(1)}, u32[]{:S(2)}, u32[]{:S(2)}) collective-permute-start(bf16[8,144,384]{2,1,0:T(8,128)(2,1)S(1)} %constant_dynamic-update-slice_fusion.5), channel_id=1, source_target_pairs={{0,1},{1,0},{2,3},{3,2},{4,5},{5,4},{6,7},{7,6},{8,9},{9,8},{10,11... | collective-permute-start | bytes 2654216 | tf_op jit(solution)/shard_map/ppermute | solution.py:345
  29.7 13.1 %collective-permute-start.6 = (bf16[8,144,384]{2,1,0:T(8,128)(2,1)S(1)}, bf16[8,144,384]{2,1,0:T(8,128)(2,1)S(1)}, u32[]{:S(2)}, u32[]{:S(2)}) collective-permute-start(bf16[8,144,384]{2,1,0:T(8,128)(2,1)S(1)} %constant_dynamic-update-slice_fusion.5), channel_id=1, source_target_pairs={{0,4},{1,3},{2,6},{3,1},{4,0},{5,7},{6,2},{7,5},{8,12},{9,11},{10,... | collective-permute-start | bytes 2654216 | tf_op jit(solution)/shard_map/ppermute | solution.py:345
  31.4 10.4 %collective-permute-start.8 = (bf16[2,240,384]{2,1,0:T(8,128)(2,1)S(1)}, bf16[2,240,384]{2,1,0:T(8,128)(2,1)S(1)}, u32[]{:S(2)}, u32[]{:S(2)}) collective-permute-start(bf16[2,240,384]{2,1,0:T(8,128)(2,1)S(1)} %pad_maximum_fusion.4), channel_id=1, source_target_pairs={{0,8},{1,9},{2,10},{3,11},{4,12},{5,13},{6,14},{7,15},{8,0},{9,1},... | collective-permute-start | bytes 1105928 | tf_op jit(solution)/shard_map/ppermute | solution.py:345
  42.8 2.4 %collective-permute-start.10 = (bf16[8,144,384]{2,1,0:T(8,128)(2,1)S(1)}, bf16[8,144,384]{2,1,0:T(8,128)(2,1)S(1)}, u32[]{:S(2)}, u32[]{:S(2)}) collective-permute-start(bf16[8,144,384]{2,1,0:T(8,128)(2,1)S(1)} %collective-permute-done.6), channel_id=1, source_target_pairs={{0,1},{1,0},{2,3},{3,2},{4,5},{5,4},{6,7},{7,6},{8,9},{9,8},{10,11... | collective-permute-start | bytes 2654216 | tf_op jit(solution)/shard_map/ppermute | solution.py:345
  42.9 16.7 %collective-permute-start.13 = (bf16[2,192,384]{2,1,0:T(8,128)(2,1)S(1)}, bf16[2,192,384]{2,1,0:T(8,128)(2,1)S(1)}, u32[]{:S(2)}, u32[]{:S(2)}) collective-permute-start(bf16[2,192,384]{2,1,0:T(8,128)(2,1)S(1)} %get-tuple-element.135), channel_id=1, source_target_pairs={{0,16},{1,17},{2,18},{3,19},{4,20},{5,21},{6,22},{7,23},{8,24},{9,... | collective-permute-start | bytes 884744 | tf_op jit(solution)/shard_map/ppermute | solution.py:345
  44.0 11.5 %collective-permute-start.9 = (bf16[4,240,384]{2,1,0:T(8,128)(2,1)S(1)}, bf16[4,240,384]{2,1,0:T(8,128)(2,1)S(1)}, u32[]{:S(2)}, u32[]{:S(2)}) collective-permute-start(bf16[4,240,384]{2,1,0:T(8,128)(2,1)S(1)} %pad_maximum_fusion.1), channel_id=1, source_target_pairs={{0,2},{1,5},{2,0},{3,7},{4,6},{5,1},{6,4},{7,3},{8,10},{9,13},{10,... | collective-permute-start | bytes 2211848 | tf_op jit(solution)/shard_map/ppermute | solution.py:345
  52.2 21.1 %copy-start.8 = (bf16[1024,2304]{1,0:T(8,128)(2,1)}, bf16[1024,2304]{1,0:T(8,128)(2,1)S(1)}, u32[]{:S(2)}) copy-start(bf16[1024,2304]{1,0:T(8,128)(2,1)S(1)} %get-tuple-element.91.qkv_ref.q_ref.k_ref.v_ref) | copy-start | bytes 14155780
  55.7 19.0 %collective-permute-start.12 = (bf16[8,240,384]{2,1,0:T(8,128)(2,1)S(1)}, bf16[8,240,384]{2,1,0:T(8,128)(2,1)S(1)}, u32[]{:S(2)}, u32[]{:S(2)}) collective-permute-start(bf16[8,240,384]{2,1,0:T(8,128)(2,1)S(1)} %constant_dynamic-update-slice_fusion.15), channel_id=1, source_target_pairs={{0,1},{1,0},{2,3},{3,2},{4,5},{5,4},{6,7},{7,6},{8,9},{9,8},{10,11... | collective-permute-start | bytes 4423688 | tf_op jit(solution)/shard_map/ppermute | solution.py:345
  55.8 19.4 %collective-permute-start.11 = (bf16[8,240,384]{2,1,0:T(8,128)(2,1)S(1)}, bf16[8,240,384]{2,1,0:T(8,128)(2,1)S(1)}, u32[]{:S(2)}, u32[]{:S(2)}) collective-permute-start(bf16[8,240,384]{2,1,0:T(8,128)(2,1)S(1)} %constant_dynamic-update-slice_fusion.15), channel_id=1, source_target_pairs={{0,4},{1,3},{2,6},{3,1},{4,0},{5,7},{6,2},{7,5},{8,12},{9,11},{10,... | collective-permute-start | bytes 4423688 | tf_op jit(solution)/shard_map/ppermute | solution.py:345
  59.7 15.0 %collective-permute-start.14 = (bf16[2,2,192,384]{3,2,1,0:T(8,128)(2,1)S(1)}, bf16[2,2,192,384]{3,2,1,0:T(8,128)(2,1)S(1)}, u32[]{:S(2)}, u32[]{:S(2)}) collective-permute-start(bf16[2,2,192,384]{3,2,1,0:T(8,128)(2,1)S(1)} %pad_maximum_fusion.2), channel_id=1, source_target_pairs={{0,8},{1,9},{2,10},{3,11},{4,12},{5,13},{6,14},{7,15},{8,0},{9,1},... | collective-permute-start | bytes 1769480 | tf_op jit(solution)/shard_map/ppermute | solution.py:345
  75.2 3.3 %collective-permute-start.16 = (bf16[8,240,384]{2,1,0:T(8,128)(2,1)S(1)}, bf16[8,240,384]{2,1,0:T(8,128)(2,1)S(1)}, u32[]{:S(2)}, u32[]{:S(2)}) collective-permute-start(bf16[8,240,384]{2,1,0:T(8,128)(2,1)S(1)} %collective-permute-done.11), channel_id=1, source_target_pairs={{0,1},{1,0},{2,3},{3,2},{4,5},{5,4},{6,7},{7,6},{8,9},{9,8},{10,11... | collective-permute-start | bytes 4423688 | tf_op jit(solution)/shard_map/ppermute | solution.py:345
  75.8 14.6 %collective-permute-start.17 = (bf16[8,192,384]{2,1,0:T(8,128)(2,1)S(1)}, bf16[8,192,384]{2,1,0:T(8,128)(2,1)S(1)}, u32[]{:S(2)}, u32[]{:S(2)}) collective-permute-start(bf16[8,192,384]{2,1,0:T(8,128)(2,1)S(1)} %bitcast.73), channel_id=1, source_target_pairs={{0,1},{1,0},{2,3},{3,2},{4,5},{5,4},{6,7},{7,6},{8,9},{9,8},{10,11... | collective-permute-start | bytes 3538952 | tf_op jit(solution)/shard_map/ppermute | solution.py:345
  76.3 16.2 %collective-permute-start.15 = (bf16[8,192,384]{2,1,0:T(8,128)(2,1)S(1)}, bf16[8,192,384]{2,1,0:T(8,128)(2,1)S(1)}, u32[]{:S(2)}, u32[]{:S(2)}) collective-permute-start(bf16[8,192,384]{2,1,0:T(8,128)(2,1)S(1)} %bitcast.74), channel_id=1, source_target_pairs={{0,4},{1,3},{2,6},{3,1},{4,0},{5,7},{6,2},{7,5},{8,12},{9,11},{10,... | collective-permute-start | bytes 3538952 | tf_op jit(solution)/shard_map/ppermute | solution.py:345
  78.5 16.9 %copy-start = (bf16[1024,768]{1,0:T(8,128)(2,1)S(1)}, bf16[1024,768]{1,0:T(8,128)(2,1)}, u32[]{:S(2)}) copy-start(bf16[1024,768]{1,0:T(8,128)(2,1)} %go_ref.1) | copy-start | bytes 4718596
  92.5 2.8 %collective-permute-start.18 = (bf16[8,192,384]{2,1,0:T(8,128)(2,1)S(1)}, bf16[8,192,384]{2,1,0:T(8,128)(2,1)S(1)}, u32[]{:S(2)}, u32[]{:S(2)}) collective-permute-start(bf16[8,192,384]{2,1,0:T(8,128)(2,1)S(1)} %collective-permute-done.15), channel_id=1, source_target_pairs={{0,1},{1,0},{2,3},{3,2},{4,5},{5,4},{6,7},{7,6},{8,9},{9,8},{10,11... | collective-permute-start | bytes 3538952 | tf_op jit(solution)/shard_map/ppermute | solution.py:345
  95.4 23.4 %copy-start.9 = (f32[6,8,512]{2,1,0:T(8,128)S(1)}, f32[6,8,512]{2,1,0:T(8,128)}, u32[]{:S(2)}) copy-start(f32[6,8,512]{2,1,0:T(8,128)} %get-tuple-element.110.rt_ref) | copy-start | bytes 294916
  118.8 29.7 %copy-start.6 = (bf16[3,768,768]{2,1,0:T(8,128)(2,1)S(1)}, bf16[3,768,768]{2,1,0:T(8,128)(2,1)}, u32[]{:S(2)}) copy-start(bf16[3,768,768]{2,1,0:T(8,128)(2,1)} %get-tuple-element.118.w_ref) | copy-start | bytes 10616836
  118.8 29.7 %copy-start.7 = (f32[1024,768]{1,0:T(8,128)S(1)}, f32[1024,768]{1,0:T(8,128)}, u32[]{:S(2)}) copy-start(f32[1024,768]{1,0:T(8,128)} %get-tuple-element.115.gfs_ref) | copy-start | bytes 9437188
  136.1 1.3 collective-permute-start.19
  137.4 5.2 %collective-permute-start.22 = (f32[16,768]{1,0:T(8,128)S(1)}, f32[16,768]{1,0:T(8,128)S(1)}, u32[]{:S(2)}, u32[]{:S(2)}) collective-permute-start(f32[16,768]{1,0:T(8,128)S(1)} %add.63), channel_id=1, source_target_pairs={{0,6},{1,7},{2,4},{3,5},{4,2},{5,3},{6,0},{7,1},{8,14},{9,15},{10,... | collective-permute-start | bytes 147464 | tf_op jit(solution)/shard_map/ppermute | solution.py:345
  139.4 4.1 %collective-permute-start.21 = (f32[16,768]{1,0:T(8,128)S(1)}, f32[16,768]{1,0:T(8,128)S(1)}, u32[]{:S(2)}, u32[]{:S(2)}) collective-permute-start(f32[16,768]{1,0:T(8,128)S(1)} %add.63), channel_id=1, source_target_pairs={{0,4},{1,5},{2,6},{3,7},{4,0},{5,1},{6,2},{7,3},{8,12},{9,13},{10,... | collective-permute-start | bytes 147464 | tf_op jit(solution)/shard_map/ppermute | solution.py:345
  139.9 4.1 %collective-permute-start.20 = (f32[16,768]{1,0:T(8,128)S(1)}, f32[16,768]{1,0:T(8,128)S(1)}, u32[]{:S(2)}, u32[]{:S(2)}) collective-permute-start(f32[16,768]{1,0:T(8,128)S(1)} %add.63), channel_id=1, source_target_pairs={{0,2},{1,3},{2,0},{3,1},{4,6},{5,7},{6,4},{7,5},{8,10},{9,11},{10,... | collective-permute-start | bytes 147464 | tf_op jit(solution)/shard_map/ppermute | solution.py:345
  144.1 10.2 %collective-permute-start.25 = (f32[16,768]{1,0:T(8,128)S(1)}, f32[16,768]{1,0:T(8,128)S(1)}, u32[]{:S(2)}, u32[]{:S(2)}) collective-permute-start(f32[16,768]{1,0:T(8,128)S(1)} %add_add_fusion.1), channel_id=1, source_target_pairs={{0,24},{1,25},{2,26},{3,27},{4,28},{5,29},{6,30},{7,31},{8,16},{9,... | collective-permute-start | bytes 147464 | tf_op jit(solution)/shard_map/ppermute | solution.py:345
  146.7 7.6 %collective-permute-start.24 = (f32[16,768]{1,0:T(8,128)S(1)}, f32[16,768]{1,0:T(8,128)S(1)}, u32[]{:S(2)}, u32[]{:S(2)}) collective-permute-start(f32[16,768]{1,0:T(8,128)S(1)} %add_add_fusion.1), channel_id=1, source_target_pairs={{0,16},{1,17},{2,18},{3,19},{4,20},{5,21},{6,22},{7,23},{8,24},{9,... | collective-permute-start | bytes 147464 | tf_op jit(solution)/shard_map/ppermute | solution.py:345
  148.5 5.8 %collective-permute-start.23 = (f32[16,768]{1,0:T(8,128)S(1)}, f32[16,768]{1,0:T(8,128)S(1)}, u32[]{:S(2)}, u32[]{:S(2)}) collective-permute-start(f32[16,768]{1,0:T(8,128)S(1)} %add_add_fusion.1), channel_id=1, source_target_pairs={{0,8},{1,9},{2,10},{3,11},{4,12},{5,13},{6,14},{7,15},{8,0},{9,1},... | collective-permute-start | bytes 147464 | tf_op jit(solution)/shard_map/ppermute | solution.py:345
  154.3 1.3 collective-permute-start.26
  (13 other events, 158.0 us)

commit v6 on v4

--- a/solution.py
+++ b/solution.py
@@ -409,25 +409,29 @@
     z1,s2,dn,scalars=tie(z1,s2,dn,scalars)
     a1=jnp.stack(z1,0)
     n1=near_hop(a1)
-    z22=exchange(s2,2*top)
-    n1,z22,s2,n3=tie(n1,z22,s2,n3)
+    z2=exchange(s2,2*top)
+    b3=jnp.stack([s3,n3],0)
+    y3=exchange(b3,top)
+    n1,z2,s2,n3=tie(n1,z2,s2,n3)
     f1=jnp.concatenate([a1,n1],0)
     h1=far_hop(f1); of1=exchange(f1,1)
-    z23=exchange(s2,3*top); z21=exchange(s2,top)
-    h1,of1,z23,z21,n3=tie(h1,of1,z23,z21,n3)
+    e2=jnp.stack([s2,z2],0)
+    y2=exchange(e2,top)
+    m2=near_hop(e2)
+    y2,y3=tie(y2,y3)
+    n2=near_hop(y2)
+    g3=jnp.stack([b3,y3],0)
+    z3=exchange(g3,2*top)
+    h1,of1=tie(h1,of1)
     oh1=exchange(h1,1)
-    a2=jnp.stack([s2,z21,z22,z23],0)
-    n2=near_hop(a2)
-    z3=along_z(jnp.stack([s3,n3],0))
     oh1,=tie(oh1)
+    f2=jnp.stack([e2[0],y2[0],e2[1],y2[1],m2[0],n2[0],m2[1],n2[1]],0)
+    h2=far_hop(f2); of2=exchange(f2,1)
     qkv,low,wqkv=project(scalars,x,dn,upq,upv,in_bands(3,f1,h1,of1,oh1))
-    n2,qkv=tie(n2,qkv)
-    f2=jnp.concatenate([a2,n2],0)
-    h2=far_hop(f2); of2=exchange(f2,1)
     e,ot,o,rt=attend(scalars,qkv,x.shape[0]//SLOT)
     h2,o,of2,z3=tie(h2,o,of2,z3)
     oh2=exchange(h2,1)
-    f3=jnp.stack(z3,1).reshape(8,-1,D//2)
+    f3=jnp.concatenate([g3,z3],0).swapaxes(0,1).reshape(8,-1,D//2)
     h3=far_hop(f3); of3=exchange(f3,1)
     oh2,=tie(oh2)
     nn,r1,act,gp,w=feed_in(scalars,x,o,nm,in_bands(1+bands,f2,h2,of2,oh2),FF)

time: 160 us -> 155 us (0.969)
  waiting for transfers between devices: 37.4 us -> 31.5 us
    ppermute x29 -> x28, waiting for transfers between devices: 37.4 us -> 31.5 us  [permute(): lax.ppermute(v, AXES, [(i, target(i)) for i in range(device_count())])]
    ppermute x29 -> x28, starting transfers between devices: 31.3 us -> 31.2 us  [permute(): lax.ppermute(v, AXES, [(i, target(i)) for i in range(device_count())])]
  transfers between devices with their start and end apart: 29 -> 28, of which waited for: 14 -> 14; matrix products, arithmetic and copies ran while one was open for 1% -> 1% of each run, Pallas kernels for 24% -> 24%
where the time goes in v6:
time: 155 us; the launch traced here: 154 us
  Pallas kernels  79.7 us (51%)
  waiting for transfers between devices  31.5 us (20%)
  starting transfers between devices  31.2 us (20%)
  blocking collectives  7.94 us (5%)
  other arithmetic  1.66 us (1%)
    ppermute x28, waiting for transfers between devices, permute(): lax.ppermute(v, AXES, [(i, target(i)) for i in range(device_count())])  31.5 us
    ppermute x28, starting transfers between devices, permute(): lax.ppermute(v, AXES, [(i, target(i)) for i in range(device_count())])  31.2 us
    pallas_call x1, Pallas kernels, feed_out(): pl.pallas_call(feed_out_kernel, grid=(rows // SLOT,), in_specs=[SCALARS,...  23.4 us
    pallas_call x1, Pallas kernels, attend_back(): pl.pallas_call(attend_back_kernel, grid=(S, J), in_specs=[SCALARS, *[pl.B...  17.3 us
    pallas_call x1, Pallas kernels, attend(): pl.pallas_call(attend_kernel, grid=(slots, J), in_specs=[SCALARS, HELD],...  13.1 us
    pallas_call x1, Pallas kernels, feed_in(): pl.pallas_call(feed_in_kernel, in_specs=[SCALARS, HELD, HELD, HELD] + [AN...  11.9 us
    all_gather x4, blocking collectives, core_pair(): lax.all_gather(v, 'fsdp', axis=0, tiled=False, axis_index_groups=groups)  7.94 us
    pallas_call x1, Pallas kernels, project(): pl.pallas_call(project_kernel, in_specs=[SCALARS, HELD, HELD, HELD, HELD]...  6.99 us
  transfers between devices with their start and end apart: 28, of which 14 were waited for; matrix products, arithmetic and copies ran while one was open for 1% of the time, Pallas kernels for 24%

profile of v6, /device:TPU:0, one launch (start us, length us, event | category | flops | bytes accessed | tf_op | source)
XLA Modules:
  0.0 154.4 jit_solution(12308782048116441120)
XLA Ops:
  1.7 2.1 %all-gather = bf16[144,768]{1,0:T(8,128)(2,1)S(1)} all-gather(bf16[72,768]{1,0:T(8,128)(2,1)S(1)} %pad_maximum_fusion.5), channel_id=2, replica_groups={{0,1},{2,3},{4,5},{6,7},{8,9},{10,11},{12,13},{14,15},{16,17},{18,19},{..., dimensions={0}, use_global_device_ids=true | all-gather | bytes 331776 | tf_op jit(solution)/shard_map/all_gather | solution.py:365
  3.9 5.0 %collective-permute-start.2 = (bf16[144,384]{1,0:T(8,128)(2,1)S(1)}, bf16[144,384]{1,0:T(8,128)(2,1)S(1)}, u32[]{:S(2)}, u32[]{:S(2)}) collective-permute-start(bf16[144,384]{1,0:T(8,128)(2,1)S(1)} %pad_maximum_fusion.6), channel_id=1, source_target_pairs={{0,24},{1,25},{2,26},{3,27},{4,28},{5,29},{6,30},{7,31},{8,16},{9,... | collective-permute-start | bytes 331784 | tf_op jit(solution)/shard_map/ppermute | solution.py:345
  9.5 2.0 %all-gather.3 = bf16[192,768]{1,0:T(8,128)(2,1)S(1)} all-gather(bf16[96,768]{1,0:T(8,128)(2,1)S(1)} %copy-done.10), channel_id=5, replica_groups={{0,1},{2,3},{4,5},{6,7},{8,9},{10,11},{12,13},{14,15},{16,17},{18,19},{..., dimensions={0}, use_global_device_ids=true | all-gather | bytes 442368 | tf_op jit(solution)/shard_map/all_gather | solution.py:365
  11.6 1.7 %collective-permute-start.3 = (bf16[192,384]{1,0:T(8,128)(2,1)S(1)}, bf16[192,384]{1,0:T(8,128)(2,1)S(1)}, u32[]{:S(2)}, u32[]{:S(2)}) collective-permute-start(bf16[192,384]{1,0:T(8,128)(2,1)S(1)} %bitcast.106), channel_id=1, source_target_pairs={{0,2},{1,5},{2,0},{3,7},{4,6},{5,1},{6,4},{7,3},{8,10},{9,13},{10,... | collective-permute-start | bytes 442376 | tf_op jit(solution)/shard_map/ppermute | solution.py:345
  13.6 1.9 %all-gather.1 = bf16[48,768]{1,0:T(8,128)(2,1)S(1)} all-gather(bf16[24,768]{1,0:T(8,128)(2,1)S(1)} %copy-done.12), channel_id=3, replica_groups={{0,1},{2,3},{4,5},{6,7},{8,9},{10,11},{12,13},{14,15},{16,17},{18,19},{..., dimensions={0}, use_global_device_ids=true | all-gather | bytes 110592 | tf_op jit(solution)/shard_map/all_gather | solution.py:365
  15.4 2.0 %all-gather.2 = bf16[48,3072]{1,0:T(8,128)(2,1)S(1)} all-gather(bf16[24,3072]{1,0:T(8,128)(2,1)S(1)} %copy-done.11), channel_id=4, replica_groups={{0,1},{2,3},{4,5},{6,7},{8,9},{10,11},{12,13},{14,15},{16,17},{18,19},{..., dimensions={0}, use_global_device_ids=true | all-gather | bytes 442368 | tf_op jit(solution)/shard_map/all_gather | solution.py:365
  18.5 1.6 %collective-permute-start.5 = (bf16[240,384]{1,0:T(8,128)(2,1)S(1)}, bf16[240,384]{1,0:T(8,128)(2,1)S(1)}, u32[]{:S(2)}, u32[]{:S(2)}) collective-permute-start(bf16[240,384]{1,0:T(8,128)(2,1)S(1)} %constant_dynamic-update-slice_fusion), channel_id=1, source_target_pairs={{0,16},{1,17},{2,18},{3,19},{4,20},{5,21},{6,22},{7,23},{8,24},{9,... | collective-permute-start | bytes 552968 | tf_op jit(solution)/shard_map/ppermute | solution.py:345
  21.6 2.1 %collective-permute-start.7 = (bf16[2,192,384]{2,1,0:T(8,128)(2,1)S(1)}, bf16[2,192,384]{2,1,0:T(8,128)(2,1)S(1)}, u32[]{:S(2)}, u32[]{:S(2)}) collective-permute-start(bf16[2,192,384]{2,1,0:T(8,128)(2,1)S(1)} %get-tuple-element.130), channel_id=1, source_target_pairs={{0,8},{1,9},{2,10},{3,11},{4,12},{5,13},{6,14},{7,15},{8,0},{9,1},... | collective-permute-start | bytes 884744 | tf_op jit(solution)/shard_map/ppermute | solution.py:345
  23.7 6.0 %collective-permute-done.5 = bf16[240,384]{1,0:T(8,128)(2,1)S(1)} collective-permute-done((bf16[240,384]{1,0:T(8,128)(2,1)S(1)}, bf16[240,384]{1,0:T(8,128)(2,1)S(1)}, u32[]{:S(2)}, u32[]{:S(2)}) %collective-permute-start.5) | collective-permute-done | bytes 184352 | tf_op jit(solution)/shard_map/ppermute | solution.py:345
  29.7 1.3 collective-permute-start.8
  31.9 1.5 collective-permute-start.11
  34.3 7.4 %collective-permute-done.6 = bf16[2,240,384]{2,1,0:T(8,128)(2,1)S(1)} collective-permute-done((bf16[2,240,384]{2,1,0:T(8,128)(2,1)S(1)}, bf16[2,240,384]{2,1,0:T(8,128)(2,1)S(1)}, u32[]{:S(2)}, u32[]{:S(2)}) %collective-permute-start.6) | collective-permute-done | bytes 368672 | tf_op jit(solution)/shard_map/ppermute | solution.py:345
  42.4 1.6 %collective-permute-start.15 = (bf16[2,2,192,384]{3,2,0,1:T(8,128)(2,1)S(1)}, bf16[2,2,192,384]{3,2,0,1:T(8,128)(2,1)S(1)}, u32[]{:S(2)}, u32[]{:S(2)}) collective-permute-start(bf16[2,2,192,384]{3,2,0,1:T(8,128)(2,1)S(1)} %pad_maximum_fusion.1), channel_id=1, source_target_pairs={{0,16},{1,17},{2,18},{3,19},{4,20},{5,21},{6,22},{7,23},{8,24},{9,... | collective-permute-start | bytes 1769480 | tf_op jit(solution)/shard_map/ppermute | solution.py:345
  44.1 2.3 %collective-permute-done.11 = bf16[8,144,384]{2,1,0:T(8,128)(2,1)S(1)} collective-permute-done((bf16[8,144,384]{2,1,0:T(8,128)(2,1)S(1)}, bf16[8,144,384]{2,1,0:T(8,128)(2,1)S(1)}, u32[]{:S(2)}, u32[]{:S(2)}) %collective-permute-start.11) | collective-permute-done | bytes 884768 | tf_op jit(solution)/shard_map/ppermute | solution.py:345
  46.4 1.8 %collective-permute-start.13 = (bf16[8,144,384]{2,1,0:T(8,128)(2,1)S(1)}, bf16[8,144,384]{2,1,0:T(8,128)(2,1)S(1)}, u32[]{:S(2)}, u32[]{:S(2)}) collective-permute-start(bf16[8,144,384]{2,1,0:T(8,128)(2,1)S(1)} %collective-permute-done.11), channel_id=1, source_target_pairs={{0,1},{1,0},{2,3},{3,2},{4,5},{5,4},{6,7},{7,6},{8,9},{9,8},{10,11... | collective-permute-start | bytes 2654216 | tf_op jit(solution)/shard_map/ppermute | solution.py:345
  48.3 2.4 %collective-permute-done.9 = bf16[2,240,384]{2,1,0:T(8,128)(2,1)S(1)} collective-permute-done((bf16[2,240,384]{2,1,0:T(8,128)(2,1)S(1)}, bf16[2,240,384]{2,1,0:T(8,128)(2,1)S(1)}, u32[]{:S(2)}, u32[]{:S(2)}) %collective-permute-start.9) | collective-permute-done | bytes 368672 | tf_op jit(solution)/shard_map/ppermute | solution.py:345
  50.9 1.6 %collective-permute-start.10 = (bf16[8,240,384]{2,1,0:T(8,128)(2,1)S(1)}, bf16[8,240,384]{2,1,0:T(8,128)(2,1)S(1)}, u32[]{:S(2)}, u32[]{:S(2)}) collective-permute-start(bf16[8,240,384]{2,1,0:T(8,128)(2,1)S(1)} %constant_dynamic-update-slice_fusion.5), channel_id=1, source_target_pairs={{0,4},{1,3},{2,6},{3,1},{4,0},{5,7},{6,2},{7,5},{8,12},{9,11},{10,... | collective-permute-start | bytes 4423688 | tf_op jit(solution)/shard_map/ppermute | solution.py:345
  52.5 7.0 %project.1 = (bf16[1024,2304]{1,0:T(8,128)(2,1)S(1)}, bf16[32,1024]{1,0:T(8,128)(2,1)S(1)}, bf16[3,768,768]{2,1,0:T(8,128)(2,1)}) custom-call(s32[3]{0:T(128)S(1)} %pad_add_fusion.sc_ref, bf16[1024,768]{1,0:T(8,128)(2,1)S(1)} %copy-done.1, bf16[768,128]{1,0:T(8,128)(2,1)S(1)} %get-tuple-element.78.dn_ref, bf16[128,768]{1,0:T(8,128)(2,1)S(1)} %get-tuple-element.79.upq_ref, ...), custom_call_target="tpu_custom_call" | custom-call | flops 8800000000 | tf_op jit(solution)/shard_map/project/pallas_call | solution.py:96
  59.5 13.1 %attend.1 = (bf16[24,512,512]{2,1,0:T(8,128)(2,1)}, bf16[1536,512]{1,0:T(8,128)(2,1)}, bf16[1024,768]{1,0:T(8,128)(2,1)S(1)}, f32[6,8,512]{2,1,0:T(8,128)}) custom-call(s32[3]{0:T(128)S(1)} %pad_add_fusion.sc_ref, bf16[1024,2304]{1,0:T(8,128)(2,1)S(1)} %get-tuple-element.84.qkv_ref.q_ref.k_ref.v_ref), custom_call_target="tpu_custom_call" | custom-call | flops 17600000000 | tf_op jit(solution)/shard_map/attend/pallas_call | solution.py:145
  74.6 1.3 collective-permute-done.17
  75.9 11.9 %feed_in.1 = (f32[1024,768]{1,0:T(8,128)S(1)}, f32[1024,128]{1,0:T(8,128)S(1)}, bf16[1024,3072]{1,0:T(8,128)(2,1)S(1)}, bf16[1024,3072]{1,0:T(8,128)(2,1)S(1)}, bf16[5,768,768]{2,1,0:T(8,128)(2,1)S(1)}) custom-call(s32[3]{0:T(128)S(1)} %pad_add_fusion.sc_ref, bf16[1024,768]{1,0:T(8,128)(2,1)S(1)} %copy-done.1, ...), custom_call_target="tpu_custom_call" | custom-call | flops 15399999488 | tf_op jit(solution)/shard_map/feed_in/pallas_call | solution.py:188
  87.8 2.1 %collective-permute-done.16 = bf16[8,192,384]{2,1,0:T(8,128)(2,1)S(1)} collective-permute-done((bf16[8,192,384]{2,1,0:T(8,128)(2,1)S(1)}, bf16[8,192,384]{2,1,0:T(8,128)(2,1)S(1)}, u32[]{:S(2)}, u32[]{:S(2)}) %collective-permute-start.16) | collective-permute-done | bytes 1179680 | tf_op jit(solution)/shard_map/ppermute | solution.py:345
  89.9 2.8 %collective-permute-done.19 = bf16[8,192,384]{2,1,0:T(8,128)(2,1)S(1)} collective-permute-done((bf16[8,192,384]{2,1,0:T(8,128)(2,1)S(1)}, bf16[8,192,384]{2,1,0:T(8,128)(2,1)S(1)}, u32[]{:S(2)}, u32[]{:S(2)}) %collective-permute-start.19) | collective-permute-done | bytes 1179680 | tf_op jit(solution)/shard_map/ppermute | solution.py:345
  92.7 23.4 %feed_out.1 = (bf16[1024,768]{1,0:T(8,128)(2,1)}, f32[1024,768]{1,0:T(8,128)}, bf16[768,1024]{1,0:T(8,128)(2,1)S(1)}) custom-call(s32[3]{0:T(128)S(1)} %pad_add_fusion.sc_ref, f32[1024,768]{1,0:T(8,128)S(1)} %get-tuple-element.92.n1_ref, f32[1024,128]{1,0:T(8,128)S(1)} %get-tuple-element.93.r1_ref, bf16[1024,3072]{1,0:T(8,128)(2,1)S(1)} %get-tuple-element.94.act_ref, ...), custom_call_target="tpu_custom_call" | custom-call | flops 26400000000 | tf_op jit(solution)/shard_map/feed_out/pallas_call | solution.py:224
  116.2 17.3 %attend_back.1 = (bf16[1024,2304]{1,0:T(8,128)(2,1)S(1)}, bf16[16,1024]{1,0:T(8,128)(2,1)S(1)}, f32[16,768]{1,0:T(8,128)S(1)}, f32[16,768]{1,0:T(8,128)S(1)}) custom-call(s32[3]{0:T(128)S(1)} %pad_add_fusion.sc_ref, bf16[1024,2304]{1,0:T(8,128)(2,1)} %copy-done.8, bf16[1024,2304]{1,0:T(8,128)(2,1)} %copy-done.8, bf16[1024,2304]{1,0:T(8,128)(2,1)} %copy-done.8, ...), custom_call_target="tpu_custom_call" | custom-call | flops 19800000512 | tf_op jit(solution)/shard_map/attend_back/pallas_call | solution.py:314
  134.8 1.2 collective-permute-start.23
  136.0 1.5 collective-permute-start.22
  138.4 1.7 %collective-permute-done.23 = f32[16,768]{1,0:T(8,128)S(1)} collective-permute-done((f32[16,768]{1,0:T(8,128)S(1)}, f32[16,768]{1,0:T(8,128)S(1)}, u32[]{:S(2)}, u32[]{:S(2)}) %collective-permute-start.23) | collective-permute-done | bytes 49184 | tf_op jit(solution)/shard_map/ppermute | solution.py:345
  141.7 2.4 %collective-permute-start.26 = (f32[16,768]{1,0:T(8,128)S(1)}, f32[16,768]{1,0:T(8,128)S(1)}, u32[]{:S(2)}, u32[]{:S(2)}) collective-permute-start(f32[16,768]{1,0:T(8,128)S(1)} %add_add_fusion.1), channel_id=1, source_target_pairs={{0,24},{1,25},{2,26},{3,27},{4,28},{5,29},{6,30},{7,31},{8,16},{9,... | collective-permute-start | bytes 147464 | tf_op jit(solution)/shard_map/ppermute | solution.py:345
  144.1 2.0 %collective-permute-start.24 = (f32[16,768]{1,0:T(8,128)S(1)}, f32[16,768]{1,0:T(8,128)S(1)}, u32[]{:S(2)}, u32[]{:S(2)}) collective-permute-start(f32[16,768]{1,0:T(8,128)S(1)} %add_add_fusion.1), channel_id=1, source_target_pairs={{0,8},{1,9},{2,10},{3,11},{4,12},{5,13},{6,14},{7,15},{8,0},{9,1},... | collective-permute-start | bytes 147464 | tf_op jit(solution)/shard_map/ppermute | solution.py:345
  146.1 5.7 %inputs_grad.1 = f32[1024,768]{1,0:T(8,128)} custom-call(f32[1024,768]{1,0:T(8,128)S(1)} %copy-done.7, bf16[1024,2304]{1,0:T(8,128)(2,1)S(1)} %get-tuple-element.108.d_ref, bf16[16,1024]{1,0:T(8,128)(2,1)S(1)} %get-tuple-element.109.gl, bf16[3,768,768]{2,1,0:T(8,128)(2,1)S(1)} %copy-done.6, bf16[16,768]{1,0:T(8,128)(2,1)S(1)} %get-tuple-element.111.dnt_ref), custom_call_target="tpu_custom_call" | custom-call | flops 7699999744 | tf_op jit(solution)/shard_map/inputs_grad/pallas_call | solution.py:335
  152.0 1.2 collective-permute-done.27.other_ref
  (129 shorter events, 14.2 us)
Async XLA Ops:
  3.9 14.0 %collective-permute-start.2 = (bf16[144,384]{1,0:T(8,128)(2,1)S(1)}, bf16[144,384]{1,0:T(8,128)(2,1)S(1)}, u32[]{:S(2)}, u32[]{:S(2)}) collective-permute-start(bf16[144,384]{1,0:T(8,128)(2,1)S(1)} %pad_maximum_fusion.6), channel_id=1, source_target_pairs={{0,24},{1,25},{2,26},{3,27},{4,28},{5,29},{6,30},{7,31},{8,16},{9,... | collective-permute-start | bytes 331784 | tf_op jit(solution)/shard_map/ppermute | solution.py:345
  8.9 9.6 %collective-permute-start.1 = (bf16[144,384]{1,0:T(8,128)(2,1)S(1)}, bf16[144,384]{1,0:T(8,128)(2,1)S(1)}, u32[]{:S(2)}, u32[]{:S(2)}) collective-permute-start(bf16[144,384]{1,0:T(8,128)(2,1)S(1)} %pad_maximum_fusion.6), channel_id=1, source_target_pairs={{0,16},{1,17},{2,18},{3,19},{4,20},{5,21},{6,22},{7,23},{8,24},{9,... | collective-permute-start | bytes 331784 | tf_op jit(solution)/shard_map/ppermute | solution.py:345
  8.9 9.6 %collective-permute-start = (bf16[144,384]{1,0:T(8,128)(2,1)S(1)}, bf16[144,384]{1,0:T(8,128)(2,1)S(1)}, u32[]{:S(2)}, u32[]{:S(2)}) collective-permute-start(bf16[144,384]{1,0:T(8,128)(2,1)S(1)} %pad_maximum_fusion.6), channel_id=1, source_target_pairs={{0,8},{1,9},{2,10},{3,11},{4,12},{5,13},{6,14},{7,15},{8,0},{9,1},... | collective-permute-start | bytes 331784 | tf_op jit(solution)/shard_map/ppermute | solution.py:345
  11.6 9.9 %collective-permute-start.3 = (bf16[192,384]{1,0:T(8,128)(2,1)S(1)}, bf16[192,384]{1,0:T(8,128)(2,1)S(1)}, u32[]{:S(2)}, u32[]{:S(2)}) collective-permute-start(bf16[192,384]{1,0:T(8,128)(2,1)S(1)} %bitcast.106), channel_id=1, source_target_pairs={{0,2},{1,5},{2,0},{3,7},{4,6},{5,1},{6,4},{7,3},{8,10},{9,13},{10,... | collective-permute-start | bytes 442376 | tf_op jit(solution)/shard_map/ppermute | solution.py:345
  18.5 11.1 %collective-permute-start.5 = (bf16[240,384]{1,0:T(8,128)(2,1)S(1)}, bf16[240,384]{1,0:T(8,128)(2,1)S(1)}, u32[]{:S(2)}, u32[]{:S(2)}) collective-permute-start(bf16[240,384]{1,0:T(8,128)(2,1)S(1)} %constant_dynamic-update-slice_fusion), channel_id=1, source_target_pairs={{0,16},{1,17},{2,18},{3,19},{4,20},{5,21},{6,22},{7,23},{8,24},{9,... | collective-permute-start | bytes 552968 | tf_op jit(solution)/shard_map/ppermute | solution.py:345
  20.2 9.4 %collective-permute-start.4 = (bf16[4,144,384]{2,1,0:T(8,128)(2,1)S(1)}, bf16[4,144,384]{2,1,0:T(8,128)(2,1)S(1)}, u32[]{:S(2)}, u32[]{:S(2)}) collective-permute-start(bf16[4,144,384]{2,1,0:T(8,128)(2,1)S(1)} %pad_maximum_fusion.2), channel_id=1, source_target_pairs={{0,2},{1,5},{2,0},{3,7},{4,6},{5,1},{6,4},{7,3},{8,10},{9,13},{10,... | collective-permute-start | bytes 1327112 | tf_op jit(solution)/shard_map/ppermute | solution.py:345
  21.6 12.8 %collective-permute-start.7 = (bf16[2,192,384]{2,1,0:T(8,128)(2,1)S(1)}, bf16[2,192,384]{2,1,0:T(8,128)(2,1)S(1)}, u32[]{:S(2)}, u32[]{:S(2)}) collective-permute-start(bf16[2,192,384]{2,1,0:T(8,128)(2,1)S(1)} %get-tuple-element.130), channel_id=1, source_target_pairs={{0,8},{1,9},{2,10},{3,11},{4,12},{5,13},{6,14},{7,15},{8,0},{9,1},... | collective-permute-start | bytes 884744 | tf_op jit(solution)/shard_map/ppermute | solution.py:345
  29.7 18.6 %collective-permute-start.8 = (bf16[2,240,384]{2,1,0:T(8,128)(2,1)S(1)}, bf16[2,240,384]{2,1,0:T(8,128)(2,1)S(1)}, u32[]{:S(2)}, u32[]{:S(2)}) collective-permute-start(bf16[2,240,384]{2,1,0:T(8,128)(2,1)S(1)} %pad_maximum_fusion.3), channel_id=1, source_target_pairs={{0,2},{1,5},{2,0},{3,7},{4,6},{5,1},{6,4},{7,3},{8,10},{9,13},{10,... | collective-permute-start | bytes 1105928 | tf_op jit(solution)/shard_map/ppermute | solution.py:345
  31.0 10.7 %collective-permute-start.6 = (bf16[2,240,384]{2,1,0:T(8,128)(2,1)S(1)}, bf16[2,240,384]{2,1,0:T(8,128)(2,1)S(1)}, u32[]{:S(2)}, u32[]{:S(2)}) collective-permute-start(bf16[2,240,384]{2,1,0:T(8,128)(2,1)S(1)} %pad_maximum_fusion.3), channel_id=1, source_target_pairs={{0,8},{1,9},{2,10},{3,11},{4,12},{5,13},{6,14},{7,15},{8,0},{9,1},... | collective-permute-start | bytes 1105928 | tf_op jit(solution)/shard_map/ppermute | solution.py:345
  31.8 12.3 %collective-permute-start.12 = (bf16[8,144,384]{2,1,0:T(8,128)(2,1)S(1)}, bf16[8,144,384]{2,1,0:T(8,128)(2,1)S(1)}, u32[]{:S(2)}, u32[]{:S(2)}) collective-permute-start(bf16[8,144,384]{2,1,0:T(8,128)(2,1)S(1)} %constant_dynamic-update-slice_fusion.18), channel_id=1, source_target_pairs={{0,1},{1,0},{2,3},{3,2},{4,5},{5,4},{6,7},{7,6},{8,9},{9,8},{10,11... | collective-permute-start | bytes 2654216 | tf_op jit(solution)/shard_map/ppermute | solution.py:345
  31.9 14.5 %collective-permute-start.11 = (bf16[8,144,384]{2,1,0:T(8,128)(2,1)S(1)}, bf16[8,144,384]{2,1,0:T(8,128)(2,1)S(1)}, u32[]{:S(2)}, u32[]{:S(2)}) collective-permute-start(bf16[8,144,384]{2,1,0:T(8,128)(2,1)S(1)} %constant_dynamic-update-slice_fusion.18), channel_id=1, source_target_pairs={{0,4},{1,3},{2,6},{3,1},{4,0},{5,7},{6,2},{7,5},{8,12},{9,11},{10,... | collective-permute-start | bytes 2654216 | tf_op jit(solution)/shard_map/ppermute | solution.py:345
  41.7 9.0 %collective-permute-start.9 = (bf16[2,240,384]{2,1,0:T(8,128)(2,1)S(1)}, bf16[2,240,384]{2,1,0:T(8,128)(2,1)S(1)}, u32[]{:S(2)}, u32[]{:S(2)}) collective-permute-start(bf16[2,240,384]{2,1,0:T(8,128)(2,1)S(1)} %collective-permute-done.6), channel_id=1, source_target_pairs={{0,2},{1,5},{2,0},{3,7},{4,6},{5,1},{6,4},{7,3},{8,10},{9,13},{10,... | collective-permute-start | bytes 1105928 | tf_op jit(solution)/shard_map/ppermute | solution.py:345
  42.4 30.2 %collective-permute-start.15 = (bf16[2,2,192,384]{3,2,0,1:T(8,128)(2,1)S(1)}, bf16[2,2,192,384]{3,2,0,1:T(8,128)(2,1)S(1)}, u32[]{:S(2)}, u32[]{:S(2)}) collective-permute-start(bf16[2,2,192,384]{3,2,0,1:T(8,128)(2,1)S(1)} %pad_maximum_fusion.1), channel_id=1, source_target_pairs={{0,16},{1,17},{2,18},{3,19},{4,20},{5,21},{6,22},{7,23},{8,24},{9,... | collective-permute-start | bytes 1769480 | tf_op jit(solution)/shard_map/ppermute | solution.py:345
  46.4 6.1 %collective-permute-start.13 = (bf16[8,144,384]{2,1,0:T(8,128)(2,1)S(1)}, bf16[8,144,384]{2,1,0:T(8,128)(2,1)S(1)}, u32[]{:S(2)}, u32[]{:S(2)}) collective-permute-start(bf16[8,144,384]{2,1,0:T(8,128)(2,1)S(1)} %collective-permute-done.11), channel_id=1, source_target_pairs={{0,1},{1,0},{2,3},{3,2},{4,5},{5,4},{6,7},{7,6},{8,9},{9,8},{10,11... | collective-permute-start | bytes 2654216 | tf_op jit(solution)/shard_map/ppermute | solution.py:345
  50.8 21.8 %collective-permute-start.14 = (bf16[8,240,384]{2,1,0:T(8,128)(2,1)S(1)}, bf16[8,240,384]{2,1,0:T(8,128)(2,1)S(1)}, u32[]{:S(2)}, u32[]{:S(2)}) collective-permute-start(bf16[8,240,384]{2,1,0:T(8,128)(2,1)S(1)} %constant_dynamic-update-slice_fusion.5), channel_id=1, source_target_pairs={{0,1},{1,0},{2,3},{3,2},{4,5},{5,4},{6,7},{7,6},{8,9},{9,8},{10,11... | collective-permute-start | bytes 4423688 | tf_op jit(solution)/shard_map/ppermute | solution.py:345
  50.9 21.7 %collective-permute-start.10 = (bf16[8,240,384]{2,1,0:T(8,128)(2,1)S(1)}, bf16[8,240,384]{2,1,0:T(8,128)(2,1)S(1)}, u32[]{:S(2)}, u32[]{:S(2)}) collective-permute-start(bf16[8,240,384]{2,1,0:T(8,128)(2,1)S(1)} %constant_dynamic-update-slice_fusion.5), channel_id=1, source_target_pairs={{0,4},{1,3},{2,6},{3,1},{4,0},{5,7},{6,2},{7,5},{8,12},{9,11},{10,... | collective-permute-start | bytes 4423688 | tf_op jit(solution)/shard_map/ppermute | solution.py:345
  72.6 3.3 %collective-permute-start.17 = (bf16[8,240,384]{2,1,0:T(8,128)(2,1)S(1)}, bf16[8,240,384]{2,1,0:T(8,128)(2,1)S(1)}, u32[]{:S(2)}, u32[]{:S(2)}) collective-permute-start(bf16[8,240,384]{2,1,0:T(8,128)(2,1)S(1)} %collective-permute-done.10), channel_id=1, source_target_pairs={{0,1},{1,0},{2,3},{3,2},{4,5},{5,4},{6,7},{7,6},{8,9},{9,8},{10,11... | collective-permute-start | bytes 4423688 | tf_op jit(solution)/shard_map/ppermute | solution.py:345
  73.1 14.7 %collective-permute-start.18 = (bf16[8,192,384]{2,1,0:T(8,128)(2,1)S(1)}, bf16[8,192,384]{2,1,0:T(8,128)(2,1)S(1)}, u32[]{:S(2)}, u32[]{:S(2)}) collective-permute-start(bf16[8,192,384]{2,1,0:T(8,128)(2,1)S(1)} %bitcast.68), channel_id=1, source_target_pairs={{0,1},{1,0},{2,3},{3,2},{4,5},{5,4},{6,7},{7,6},{8,9},{9,8},{10,11... | collective-permute-start | bytes 3538952 | tf_op jit(solution)/shard_map/ppermute | solution.py:345
  73.7 16.2 %collective-permute-start.16 = (bf16[8,192,384]{2,1,0:T(8,128)(2,1)S(1)}, bf16[8,192,384]{2,1,0:T(8,128)(2,1)S(1)}, u32[]{:S(2)}, u32[]{:S(2)}) collective-permute-start(bf16[8,192,384]{2,1,0:T(8,128)(2,1)S(1)} %bitcast.69), channel_id=1, source_target_pairs={{0,4},{1,3},{2,6},{3,1},{4,0},{5,7},{6,2},{7,5},{8,12},{9,11},{10,... | collective-permute-start | bytes 3538952 | tf_op jit(solution)/shard_map/ppermute | solution.py:345
  75.9 16.8 %copy-start = (bf16[1024,768]{1,0:T(8,128)(2,1)S(1)}, bf16[1024,768]{1,0:T(8,128)(2,1)}, u32[]{:S(2)}) copy-start(bf16[1024,768]{1,0:T(8,128)(2,1)} %go_ref.1) | copy-start | bytes 4718596
  89.9 2.8 %collective-permute-start.19 = (bf16[8,192,384]{2,1,0:T(8,128)(2,1)S(1)}, bf16[8,192,384]{2,1,0:T(8,128)(2,1)S(1)}, u32[]{:S(2)}, u32[]{:S(2)}) collective-permute-start(bf16[8,192,384]{2,1,0:T(8,128)(2,1)S(1)} %collective-permute-done.16), channel_id=1, source_target_pairs={{0,1},{1,0},{2,3},{3,2},{4,5},{5,4},{6,7},{7,6},{8,9},{9,8},{10,11... | collective-permute-start | bytes 3538952 | tf_op jit(solution)/shard_map/ppermute | solution.py:345
  92.7 23.4 %copy-start.9 = (f32[6,8,512]{2,1,0:T(8,128)S(1)}, f32[6,8,512]{2,1,0:T(8,128)}, u32[]{:S(2)}) copy-start(f32[6,8,512]{2,1,0:T(8,128)} %get-tuple-element.102.rt_ref) | copy-start | bytes 294916
  116.1 30.0 %copy-start.6 = (bf16[3,768,768]{2,1,0:T(8,128)(2,1)S(1)}, bf16[3,768,768]{2,1,0:T(8,128)(2,1)}, u32[]{:S(2)}) copy-start(bf16[3,768,768]{2,1,0:T(8,128)(2,1)} %get-tuple-element.110.w_ref) | copy-start | bytes 10616836
  116.2 30.0 %copy-start.7 = (f32[1024,768]{1,0:T(8,128)S(1)}, f32[1024,768]{1,0:T(8,128)}, u32[]{:S(2)}) copy-start(f32[1024,768]{1,0:T(8,128)} %get-tuple-element.107.gfs_ref) | copy-start | bytes 9437188
  133.5 1.3 collective-permute-start.20
  134.8 5.3 %collective-permute-start.23 = (f32[16,768]{1,0:T(8,128)S(1)}, f32[16,768]{1,0:T(8,128)S(1)}, u32[]{:S(2)}, u32[]{:S(2)}) collective-permute-start(f32[16,768]{1,0:T(8,128)S(1)} %add.63), channel_id=1, source_target_pairs={{0,6},{1,7},{2,4},{3,5},{4,2},{5,3},{6,0},{7,1},{8,14},{9,15},{10,... | collective-permute-start | bytes 147464 | tf_op jit(solution)/shard_map/ppermute | solution.py:345
  136.0 4.5 %collective-permute-start.22 = (f32[16,768]{1,0:T(8,128)S(1)}, f32[16,768]{1,0:T(8,128)S(1)}, u32[]{:S(2)}, u32[]{:S(2)}) collective-permute-start(f32[16,768]{1,0:T(8,128)S(1)} %add.63), channel_id=1, source_target_pairs={{0,4},{1,5},{2,6},{3,7},{4,0},{5,1},{6,2},{7,3},{8,12},{9,13},{10,... | collective-permute-start | bytes 147464 | tf_op jit(solution)/shard_map/ppermute | solution.py:345
  137.6 4.1 %collective-permute-start.21 = (f32[16,768]{1,0:T(8,128)S(1)}, f32[16,768]{1,0:T(8,128)S(1)}, u32[]{:S(2)}, u32[]{:S(2)}) collective-permute-start(f32[16,768]{1,0:T(8,128)S(1)} %add.63), channel_id=1, source_target_pairs={{0,2},{1,3},{2,0},{3,1},{4,6},{5,7},{6,4},{7,5},{8,10},{9,11},{10,... | collective-permute-start | bytes 147464 | tf_op jit(solution)/shard_map/ppermute | solution.py:345
  141.7 10.2 %collective-permute-start.26 = (f32[16,768]{1,0:T(8,128)S(1)}, f32[16,768]{1,0:T(8,128)S(1)}, u32[]{:S(2)}, u32[]{:S(2)}) collective-permute-start(f32[16,768]{1,0:T(8,128)S(1)} %add_add_fusion.1), channel_id=1, source_target_pairs={{0,24},{1,25},{2,26},{3,27},{4,28},{5,29},{6,30},{7,31},{8,16},{9,... | collective-permute-start | bytes 147464 | tf_op jit(solution)/shard_map/ppermute | solution.py:345
  144.1 7.8 %collective-permute-start.25 = (f32[16,768]{1,0:T(8,128)S(1)}, f32[16,768]{1,0:T(8,128)S(1)}, u32[]{:S(2)}, u32[]{:S(2)}) collective-permute-start(f32[16,768]{1,0:T(8,128)S(1)} %add_add_fusion.1), channel_id=1, source_target_pairs={{0,16},{1,17},{2,18},{3,19},{4,20},{5,21},{6,22},{7,23},{8,24},{9,... | collective-permute-start | bytes 147464 | tf_op jit(solution)/shard_map/ppermute | solution.py:345
  144.1 7.8 %collective-permute-start.24 = (f32[16,768]{1,0:T(8,128)S(1)}, f32[16,768]{1,0:T(8,128)S(1)}, u32[]{:S(2)}, u32[]{:S(2)}) collective-permute-start(f32[16,768]{1,0:T(8,128)S(1)} %add_add_fusion.1), channel_id=1, source_target_pairs={{0,8},{1,9},{2,10},{3,11},{4,12},{5,13},{6,14},{7,15},{8,0},{9,1},... | collective-permute-start | bytes 147464 | tf_op jit(solution)/shard_map/ppermute | solution.py:345
  151.9 1.3 collective-permute-start.27
  (14 other events, 177.2 us)
